TPU v7x, 32 devices: a whole 2x2x4 slice. The times are simulated.
32 devices in a mesh: seq: 16 (over z, y, core), tp: 2 (over x).
Axes of the slice: x: 2, y: 2, z: 4, core: 2. Of those that a mesh axis runs over, the one named last changes fastest.
Arguments:
- queries: bfloat16 [16384, 4096], P('seq', 'tp'), may hold values from -600 to 600
- neighbours: bfloat16 [128, 896, 128], P('seq', 'tp'), may hold values from -6 to 6
- key_weight: bfloat16 [896, 4096], P(None, 'tp'), may hold values from -0.1875 to 0.1875
- value_weight: bfloat16 [896, 4096], P(None, 'tp'), may hold values from -0.1875 to 0.1875
- neighbour_ids: int32 [256, 2], P('seq'), may hold values from 0 to 127, as said below
Outputs:
- attended: bfloat16 [16384, 4096], P('seq', 'tp')
Inputs may be any that keep to these rules, and one draw needn't show every extreme that they name: `neighbour_ids`: block b is stored on index b // 8 of seq. Among the 32 neighbours of the spans of one index of seq, at most 2 are stored on any one index of seq, and exactly 2 on some.
All inputs are finite; a program needn't handle non-finite values.
Results may differ from a plain program's by a relative error of at most 0.014.
Values may be sent and summed in bfloat16 or wider, within the bound.
No kernel may reach another device: no remote copies, remote signals or barrier semaphores. Data moves between devices by JAX's collectives and lax.ppermute only.
A program may use at most 128 MiB of HBM per device.

v0:
```python
import functools

import jax
import jax.numpy as jnp
from jax import lax
from jax.experimental import pallas as pl
from jax.experimental.pallas import tpu as pltpu
from jax.sharding import PartitionSpec as P

HDIM = 128
SPAN = 64
GROUP = 4
PAIR = 2 * HDIM
VMEM_LIMIT = 56 * 1024 * 1024


def passed_along(x, axis, by):
    peers = lax.axis_size(axis)
    pairs = [(i, i + by) for i in range(peers) if 0 <= i + by < peers]
    return lax.ppermute(x, axis, pairs)


def slot_ranks(sources):
    positions = sources.shape[-1]
    alike = sources[..., :, None] == sources[..., None, :]
    earlier = jnp.arange(positions)[None, :] < jnp.arange(positions)[:, None]
    return jnp.sum(jnp.where(alike & earlier, 1, 0), axis=-1).astype(jnp.int32)


def pick_kernel(stored, blocks, picked, sems):
    count = picked.shape[0]
    copies = [
        pltpu.make_async_copy(blocks.at[stored[i]], picked.at[i], sems.at[i]) for i in range(count)
    ]
    for copy in copies:
        copy.start()
    for copy in copies:
        copy.wait()


def pick_blocks(stored, blocks):
    count = stored.shape[0]
    return pl.pallas_call(
        pick_kernel,
        grid_spec=pltpu.PrefetchScalarGridSpec(
            num_scalar_prefetch=1,
            grid=(1,),
            in_specs=[pl.BlockSpec(memory_space=pl.ANY)],
            out_specs=pl.BlockSpec(memory_space=pl.ANY),
            scratch_shapes=[pltpu.SemaphoreType.DMA((count,))],
        ),
        out_shape=jax.ShapeDtypeStruct((count,) + blocks.shape[1:], blocks.dtype),
        name="pick_blocks",
    )(stored, blocks)


def attend_kernel(sources, spans, *refs):
    x_refs = refs[:GROUP]
    q_refs = refs[GROUP : 2 * GROUP]
    wk_ref, wv_ref = refs[2 * GROUP : 2 * GROUP + 2]
    out_ref, lse_ref, xt, k_even, v_even, k_odd, v_odd = refs[-7:]
    nlen = x_refs[0].shape[-1]
    columns = wk_ref.shape[-1]
    pairs = columns // PAIR
    scale = HDIM ** (-0.5)
    for i in range(GROUP):
        xt[pl.ds(i * nlen, nlen), :] = x_refs[i][0].T
    lanes = lax.broadcasted_iota(jnp.int32, (SPAN, HDIM), 1)
    lse_ref[...] = jnp.zeros_like(lse_ref)

    def project(pair, k_ref, v_ref):
        cols = pl.ds(pl.multiple_of(pair * PAIR, PAIR), PAIR)
        rows = xt[...]
        k_ref[...] = jnp.dot(rows, wk_ref[:, cols], preferred_element_type=jnp.float32).astype(
            jnp.bfloat16
        )
        v_ref[...] = jnp.dot(rows, wv_ref[:, cols], preferred_element_type=jnp.float32).astype(
            jnp.bfloat16
        )

    def attend(pair, k_ref, v_ref):
        cols = pl.ds(pl.multiple_of(pair * PAIR, PAIR), PAIR)
        none = jnp.zeros((SPAN, HDIM), jnp.bfloat16)
        for i in range(GROUP):
            rows = pl.ds(i * nlen, nlen)
            q = q_refs[i][0, :, cols]
            upper = jnp.concatenate([q[:, :HDIM], none], axis=1)
            lower = jnp.concatenate([none, q[:, HDIM:]], axis=1)
            both = jnp.concatenate([upper, lower], axis=0)
            scores = lax.dot_general(
                both, k_ref[rows, :], (((1,), (1,)), ((), ())), preferred_element_type=jnp.float32
            )
            highest = jnp.max(scores, axis=-1, keepdims=True)
            exponent = jnp.exp((scores - highest) * scale)
            totals = jnp.sum(exponent, axis=-1, keepdims=True)
            blended = jnp.dot(
                exponent.astype(jnp.bfloat16), v_ref[rows, :], preferred_element_type=jnp.float32
            )
            inverse = 1.0 / totals
            first = blended[:SPAN, :HDIM] * inverse[:SPAN]
            second = blended[SPAN:, HDIM:] * inverse[SPAN:]
            out_ref[i, :, cols] = jnp.concatenate([first, second], axis=1).astype(jnp.bfloat16)
            lse = highest * scale + jnp.log(totals)
            held = lse_ref[i]
            held = jnp.where(lanes == 2 * pair, lse[:SPAN], held)
            lse_ref[i] = jnp.where(lanes == 2 * pair + 1, lse[SPAN:], held)

    project(0, k_even, v_even)

    def step(t, carry):
        project(2 * t + 1, k_odd, v_odd)
        attend(2 * t, k_even, v_even)
        project(2 * t + 2, k_even, v_even)
        attend(2 * t + 1, k_odd, v_odd)
        return carry

    lax.fori_loop(0, pairs // 2 - 1, step, 0)
    project(pairs - 1, k_odd, v_odd)
    attend(pairs - 2, k_even, v_even)
    attend(pairs - 1, k_odd, v_odd)


def attend_part(sources, spans, segment, windows, key_weight, value_weight, first, slots, held):
    count = sources.shape[0]
    features, nlen = segment.shape[1:]
    columns = windows.shape[-1]
    start = first // GROUP

    def block_at(i):
        return lambda g, sources, spans: (sources[g * GROUP + i], 0, 0)

    def window_at(i):
        return lambda g, sources, spans: (spans[g * GROUP + i], 0, 0)

    whole = pl.BlockSpec((features, columns), lambda g, *_: (0, 0))
    in_specs = [pl.BlockSpec((1, features, nlen), block_at(i)) for i in range(GROUP)]
    in_specs += [pl.BlockSpec((1, SPAN, columns), window_at(i)) for i in range(GROUP)]
    in_specs += [whole, whole]
    operands = [segment] * GROUP + [windows] * GROUP + [key_weight, value_weight]
    aliases = {}
    if held is not None:
        in_specs += [pl.BlockSpec(memory_space=pl.ANY)] * 2
        aliases = {2 + len(operands): 0, 3 + len(operands): 1}
        operands += list(held)
    kv = pltpu.VMEM((GROUP * nlen, PAIR), jnp.bfloat16)
    return pl.pallas_call(
        attend_kernel,
        grid_spec=pltpu.PrefetchScalarGridSpec(
            num_scalar_prefetch=2,
            grid=(count // GROUP,),
            in_specs=in_specs,
            out_specs=[
                pl.BlockSpec((GROUP, SPAN, columns), lambda g, *_: (g + start, 0, 0)),
                pl.BlockSpec((GROUP, SPAN, HDIM), lambda g, *_: (g + start, 0, 0)),
            ],
            scratch_shapes=[pltpu.VMEM((GROUP * nlen, features), jnp.bfloat16), kv, kv, kv, kv],
        ),
        out_shape=[
            jax.ShapeDtypeStruct((slots, SPAN, columns), jnp.bfloat16),
            jax.ShapeDtypeStruct((slots, SPAN, HDIM), jnp.float32),
        ],
        input_output_aliases=aliases,
        compiler_params=pltpu.CompilerParams(vmem_limit_bytes=VMEM_LIMIT),
        name="attend_part",
    )(sources, spans, *operands)


def mixed(p0, p1, l0, l1, head):
    cols = slice(head * HDIM, (head + 1) * HDIM)
    a, b = l0[:, head : head + 1], l1[:, head : head + 1]
    largest = jnp.maximum(a, b)
    ea, eb = jnp.exp(a - largest), jnp.exp(b - largest)
    inverse = 1.0 / (ea + eb)
    return p0[:, cols].astype(jnp.float32) * (ea * inverse) + p1[:, cols].astype(jnp.float32) * (
        eb * inverse
    )


def mix_last_kernel(places, p0, p1, l0, l1, out_ref):
    a, b = l0[0], l1[0]
    for head in range(out_ref.shape[-1] // HDIM):
        cols = slice(head * HDIM, (head + 1) * HDIM)
        out_ref[:, cols] = mixed(p0[0], p1[0], a, b, head).astype(jnp.bfloat16)


def mix_kernel(places, p0, p1, l0, l1, carried, out_ref, before):
    @pl.when(pl.program_id(0) == 0)
    def _():
        before[...] = carried[...]

    a, b = l0[0], l1[0]
    early = lax.broadcasted_iota(jnp.int32, (SPAN, HDIM), 0) < SPAN - 1
    for head in range(out_ref.shape[-1] // HDIM):
        cols = slice(head * HDIM, (head + 1) * HDIM)
        result = mixed(p0[0], p1[0], a, b, head)
        out_ref[:, cols] = jnp.where(early, before[:, cols].astype(jnp.float32), result).astype(
            jnp.bfloat16
        )
        before[:, cols] = result.astype(jnp.bfloat16)


def mix_specs(columns, span_of):
    def place(j, *shape):
        return pl.BlockSpec((1, SPAN) + shape, lambda k, places: (places[2 * span_of(k) + j], 0, 0))

    return [place(0, columns), place(1, columns), place(0, HDIM), place(1, HDIM)]


def mix_last(places, partials, log_totals, span_count):
    columns = partials.shape[-1]
    return pl.pallas_call(
        mix_last_kernel,
        grid_spec=pltpu.PrefetchScalarGridSpec(
            num_scalar_prefetch=1,
            grid=(1,),
            in_specs=mix_specs(columns, lambda k: span_count - 1),
            out_specs=pl.BlockSpec((SPAN, columns), lambda k, places: (0, 0)),
        ),
        out_shape=jax.ShapeDtypeStruct((SPAN, columns), jnp.bfloat16),
        name="mix_last",
    )(places, partials, partials, log_totals, log_totals)


def mix(places, partials, log_totals, carried, span_count):
    columns = partials.shape[-1]
    return pl.pallas_call(
        mix_kernel,
        grid_spec=pltpu.PrefetchScalarGridSpec(
            num_scalar_prefetch=1,
            grid=(span_count,),
            in_specs=mix_specs(columns, lambda k: k)
            + [pl.BlockSpec((SPAN, columns), lambda k, places: (0, 0))],
            out_specs=pl.BlockSpec((SPAN, columns), lambda k, places: (k, 0)),
            scratch_shapes=[pltpu.VMEM((SPAN, columns), jnp.bfloat16)],
        ),
        out_shape=jax.ShapeDtypeStruct((span_count * SPAN, columns), jnp.bfloat16),
        compiler_params=pltpu.CompilerParams(vmem_limit_bytes=VMEM_LIMIT),
        name="mix",
    )(places, partials, partials, log_totals, log_totals, carried)


def shards(queries, neighbours, key_weight, value_weight, neighbour_ids):
    tok_rows, columns = queries.shape
    span_count = neighbour_ids.shape[0]
    seq_count = lax.axis_size("seq")
    block_count = neighbours.shape[0]
    slots = 2 * span_count
    slots_per = (slots + seq_count - 1) // seq_count
    own_index = lax.axis_index("seq")

    all_ids = lax.all_gather(neighbour_ids, "seq", axis=0, tiled=True).reshape(seq_count, slots)
    wanted = all_ids // block_count == own_index
    order = jnp.arange(slots)
    earlier = order[None, :] < order[:, None]
    wanted_rank = jnp.sum(jnp.where(wanted[:, None, :] & earlier[None], 1, 0), axis=-1)
    local = all_ids % block_count

    own_ids = neighbour_ids.reshape(slots)
    own_sources = own_ids // block_count
    own_ranks = slot_ranks(own_sources)

    incoming = passed_along(queries[:SPAN], "seq", -1)
    later = jnp.concatenate([queries[SPAN:], incoming], axis=0).reshape(span_count, SPAN, columns)
    same = queries.reshape(span_count, SPAN, columns)
    early = (jnp.arange(SPAN) < SPAN - 1)[None, :, None]
    windows = jnp.where(early, later, same)

    held = None
    part = slots // slots_per
    every = slots == slots_per * seq_count
    for rank in range(slots_per):
        stored = jnp.sum(jnp.where(wanted & (wanted_rank == rank), local, 0), axis=1)
        outgoing = pick_blocks(stored.astype(jnp.int32), neighbours)
        arrived = lax.all_to_all(outgoing, "seq", split_axis=0, concat_axis=0, tiled=True)
        segment = lax.all_gather(arrived, "tp", axis=1, tiled=True)
        if every:
            sources = jnp.arange(seq_count, dtype=jnp.int32)
            hit = (own_sources[None, :] == sources[:, None]) & (own_ranks == rank)[None, :]
            spans = jnp.sum(jnp.where(hit, order[None, :] // 2, 0), axis=1).astype(jnp.int32)
        else:
            sources = own_sources.astype(jnp.int32)
            spans = (order // 2).astype(jnp.int32)
        held = attend_part(
            sources, spans, segment, windows, key_weight, value_weight, rank * part, slots, held
        )
    partials, log_totals = held
    places = own_ranks * seq_count + own_sources if every else order
    places = places.astype(jnp.int32)
    last = mix_last(places, partials, log_totals, span_count)
    carried = passed_along(last, "seq", 1)
    return mix(places, partials, log_totals, carried, span_count)


def solution(mesh):
    in_specs = (P("seq", "tp"), P("seq", "tp", None), P(None, "tp"), P(None, "tp"), P("seq", None))
    out_specs = P("seq", "tp")
    return jax.shard_map(shards, mesh=mesh, in_specs=in_specs, out_specs=out_specs, check_vma=False)
```

profile of v0, /device:TPU:1, one launch (start us, length us, event | category | flops | bytes accessed | tf_op | source)
XLA Modules:
  0.0 359.5 jit_solution(9477454550371735561)
XLA Ops:
  6.5 23.2 %all-gather = s32[16,16,2]{1,2,0:T(2,128)S(1)} all-gather(s32[1,16,2]{1,2,0:T(2,128)} %bitcast.9), channel_id=1, replica_groups=mesh['seq'=16,'tp'=2] {'seq'}, dimensions={0}, use_global_device_ids=true | all-gather | bytes 2176 | tf_op jit(solution)/shard_map/all_gather | solution.py:251
  31.0 0.7 reduce_sum.77.stored
  31.7 57.5 %pick_blocks.3 = bf16[16,448,128]{2,1,0:T(8,128)(2,1)} custom-call(s32[16]{0:T(128)} %reduce_sum.77.stored, bf16[8,448,128]{2,1,0:T(8,128)(2,1)} %blocks.3), custom_call_target="tpu_custom_call" | custom-call | tf_op jit(solution)/shard_map/pick_blocks/pallas_call | solution.py:43
  89.2 47.6 %all_to_all.10 = bf16[16,448,128]{2,1,0:T(8,128)(2,1)} all-to-all(bf16[16,448,128]{2,1,0:T(8,128)(2,1)} %pick_blocks.3), channel_id=1, replica_groups=mesh['seq'=16,'tp'=2] {'seq'}, dimensions={0} | all-to-all | bytes 3670016 | tf_op jit(solution)/shard_map/all_to_all | solution.py:274
  136.9 0.6 reduce_sum.73.stored
  137.6 57.6 %pick_blocks.2 = bf16[16,448,128]{2,1,0:T(8,128)(2,1)} custom-call(s32[16]{0:T(128)} %reduce_sum.73.stored, bf16[8,448,128]{2,1,0:T(8,128)(2,1)} %blocks.3), custom_call_target="tpu_custom_call" | custom-call | tf_op jit(solution)/shard_map/pick_blocks/pallas_call | solution.py:43
  195.2 47.1 %all_to_all.11 = bf16[16,448,128]{2,1,0:T(8,128)(2,1)} all-to-all(bf16[16,448,128]{2,1,0:T(8,128)(2,1)} %pick_blocks.2), channel_id=1, replica_groups=mesh['seq'=16,'tp'=2] {'seq'}, dimensions={0} | all-to-all | bytes 3670016 | tf_op jit(solution)/shard_map/all_to_all | solution.py:274
  242.4 1.0 slice.7
  243.3 1.9 collective-permute-start
  245.7 0.7 select_reduce_fusion.2
  246.4 0.6 multiply_add_fusion.places
  247.0 4.1 %collective-permute-done = bf16[64,2048]{1,0:T(8,128)(2,1)S(1)} collective-permute-done((bf16[64,2048]{1,0:T(8,128)(2,1)S(1)}, bf16[64,2048]{1,0:T(8,128)(2,1)S(1)}, u32[]{:S(2)}, u32[]{:S(2)}) %collective-permute-start) | collective-permute-done | bytes 262176 | tf_op jit(solution)/shard_map/ppermute | solution.py:20
  251.0 0.6 pad_maximum_fusion
  251.7 2.5 broadcast_select_fusion.refs_4_.refs_5_.refs_6_.refs_7_
  254.2 0.6 iota.40.sources
  254.8 35.2 %attend_part.2 = (bf16[32,64,2048]{2,1,0:T(8,128)(2,1)}, f32[32,64,128]{2,1,0:T(8,128)}) custom-call(s32[16]{0:T(128)} %iota.40.sources, s32[16]{0:T(128)} %get-tuple-element.15.spans, bf16[16,896,128]{2,1,0:T(8,128)(2,1)} %all-gather.6.cloned.1.call-done.refs_0_.refs_1_.refs_2_.refs_3_, ...), custom_call_target="tpu_custom_call" | custom-call | tf_op jit(solution)/shard_map/attend_part/pallas_call | solution.py:146
  289.9 1.8 all-gather.4.cloned.1.call-done.refs_0_.refs_1_.refs_2_.refs_3_
  291.7 0.6 iota.37.sources
  292.3 35.2 %attend_part.3 = (bf16[32,64,2048]{2,1,0:T(8,128)(2,1)}, f32[32,64,128]{2,1,0:T(8,128)}) custom-call(s32[16]{0:T(128)} %iota.37.sources, s32[16]{0:T(128)} %get-tuple-element.16.spans, bf16[16,896,128]{2,1,0:T(8,128)(2,1)} %all-gather.4.cloned.1.call-done.refs_0_.refs_1_.refs_2_.refs_3_, ...), custom_call_target="tpu_custom_call", output_to_operand_aliasing={{0}: (12, {}), {1}: (13, {})} | custom-call | tf_op jit(solution)/shard_map/attend_part/pallas_call | solution.py:146
  327.5 2.8 mix_last.1
  330.3 3.7 %collective-permute-start.1 = (bf16[64,2048]{1,0:T(8,128)(2,1)}, bf16[64,2048]{1,0:T(8,128)(2,1)S(1)}, u32[]{:S(2)}, u32[]{:S(2)}) collective-permute-start(bf16[64,2048]{1,0:T(8,128)(2,1)} %mix_last.1), channel_id=1, source_target_pairs={{0,2},{2,4},{4,6},{6,8},{8,10},{10,12},{12,14},{14,16},{16,18},{18... | collective-permute-start | bytes 786440 | tf_op jit(solution)/shard_map/ppermute | solution.py:20
  333.9 3.6 %collective-permute-done.1.carried = bf16[64,2048]{1,0:T(8,128)(2,1)S(1)} collective-permute-done((bf16[64,2048]{1,0:T(8,128)(2,1)}, bf16[64,2048]{1,0:T(8,128)(2,1)S(1)}, u32[]{:S(2)}, u32[]{:S(2)}) %collective-permute-start.1) | collective-permute-done | bytes 262176 | tf_op jit(solution)/shard_map/ppermute | solution.py:20
  337.6 0.7 copy-done.1
  338.3 14.4 %mix.1 = bf16[1024,2048]{1,0:T(8,128)(2,1)} custom-call(s32[32]{0:T(128)} %multiply_add_fusion.places, bf16[32,64,2048]{2,1,0:T(8,128)(2,1)} %get-tuple-element.11.p0.p1, bf16[32,64,2048]{2,1,0:T(8,128)(2,1)} %get-tuple-element.11.p0.p1, f32[32,64,128]{2,1,0:T(8,128)} %get-tuple-element.12.l0.l1, f32[32,64,128]{2,1,0:T(8,128)} %get-tuple-element.12.l0.l1, ...), custom_call_target="tpu_custom_call" | custom-call | tf_op jit(solution)/shard_map/mix/pallas_call | solution.py:226
  (34 shorter events, 1.7 us)
Async XLA Ops:
  6.5 247.6 %all-gather.6.cloned.1.call-start = ((), (), s32[]{:S(2)}) async-start(), calls=%async_computation.3 | async-start | bytes 5505024 | tf_op jit(solution)/shard_map/all_gather | solution.py:275
  136.8 154.9 %all-gather.4.cloned.1.call-start = ((), (), s32[]{:S(2)}) async-start(), calls=%async_computation.2 | async-start | bytes 5505024 | tf_op jit(solution)/shard_map/all_gather | solution.py:275
  137.6 107.7 %copy-start.2 = (s32[16,2]{0,1:T(2,128)S(1)}, s32[16,2]{0,1:T(2,128)}, u32[]{:S(2)}) copy-start(s32[16,2]{0,1:T(2,128)} %param.9) | copy-start | bytes 388
  243.3 7.7 %collective-permute-start = (bf16[64,2048]{1,0:T(8,128)(2,1)S(1)}, bf16[64,2048]{1,0:T(8,128)(2,1)S(1)}, u32[]{:S(2)}, u32[]{:S(2)}) collective-permute-start(bf16[64,2048]{1,0:T(8,128)(2,1)S(1)} %slice.7), channel_id=1, source_target_pairs={{2,0},{4,2},{6,4},{8,6},{10,8},{12,10},{14,12},{16,14},{18,16},{20... | collective-permute-start | bytes 786440 | tf_op jit(solution)/shard_map/ppermute | solution.py:20
  245.5 5.6 %slice-start = ((bf16[1024,2048]{1,0:T(8,128)(2,1)}), bf16[960,2048]{1,0:T(8,128)(2,1)S(1)}, s32[]{:S(2)}) async-start(bf16[1024,2048]{1,0:T(8,128)(2,1)} %param.5), calls=%async_computation.4 | async-start | bytes 7864320 | tf_op jit(solution)/shard_map/slice | solution.py:263
  246.9 4.7 %copy-start = (bf16[1024,2048]{1,0:T(8,128)(2,1)S(1)}, bf16[1024,2048]{1,0:T(8,128)(2,1)}, u32[]{:S(2)}) copy-start(bf16[1024,2048]{1,0:T(8,128)(2,1)} %param.5) | copy-start | bytes 12582916
  330.3 7.3 %collective-permute-start.1 = (bf16[64,2048]{1,0:T(8,128)(2,1)}, bf16[64,2048]{1,0:T(8,128)(2,1)S(1)}, u32[]{:S(2)}, u32[]{:S(2)}) collective-permute-start(bf16[64,2048]{1,0:T(8,128)(2,1)} %mix_last.1), channel_id=1, source_target_pairs={{0,2},{2,4},{4,6},{6,8},{8,10},{10,12},{12,14},{14,16},{16,18},{18... | collective-permute-start | bytes 786440 | tf_op jit(solution)/shard_map/ppermute | solution.py:20
  337.5 0.7 copy-start.1
Sparse Core Ops, SparseCore 0:
  136.9 49.0 all-gather.5
  242.5 49.1 all-gather.3
where the time goes:
time: 361 us; the launch traced here: 360 us
  Pallas kernels  203 us (56%)
  blocking collectives  118 us (33%)
  between operations  13.5 us (4%)
  waiting for transfers between devices  9.55 us (3%)
  other arithmetic  6.36 us (2%)
  starting transfers between devices  5.62 us (2%)
  local copies, waits for them, and re-layouts  3.84 us (1%)
    pallas_call x2, Pallas kernels, pick_blocks(): pl.pallas_call(pick_kernel, grid_spec=pltpu.PrefetchScalarGridSpec(num_sc...  115 us
    all_to_all x2, blocking collectives, shards(): lax.all_to_all(outgoing, 'seq', split_axis=0, concat_axis=0, tiled=True)  94.7 us
    pallas_call x2, Pallas kernels, attend_part(): pl.pallas_call(attend_kernel, grid_spec=pltpu.PrefetchScalarGridSpec(num_...  70.3 us
    all_gather x1, blocking collectives, shards(): lax.all_gather(neighbour_ids, 'seq', axis=0, tiled=True)  23.2 us
    pallas_call x1, Pallas kernels, mix(): pl.pallas_call(mix_kernel, grid_spec=pltpu.PrefetchScalarGridSpec(num_sca...  14.4 us
    ppermute x2, waiting for transfers between devices, passed_along(): return lax.ppermute(x, axis, pairs)  7.7 us
  transfers between devices with their start and end apart: 4, of which 3 were waited for; matrix products, arithmetic and copies ran while one was open for 2% of the time, Pallas kernels for 26%

commit v1 on v0

v1 whole, which is shorter than its diff:
```python
import jax
import jax.numpy as jnp
from jax import lax
from jax.experimental import pallas as pl
from jax.experimental.pallas import tpu as pltpu
from jax.sharding import PartitionSpec as P

HDIM = 128
SPAN = 64
PAIR = 2 * HDIM
INNER = 4
VMEM_LIMIT = 56 * 1024 * 1024


def passed_along(x, axis, by):
    peers = lax.axis_size(axis)
    pairs = [(i, i + by) for i in range(peers) if 0 <= i + by < peers]
    return lax.ppermute(x, axis, pairs)


def swapped(x, axis, offset):
    peers = lax.axis_size(axis)
    return lax.ppermute(x, axis, [(i, i ^ offset) for i in range(peers)])


def slot_ranks(sources):
    positions = sources.shape[-1]
    alike = sources[..., :, None] == sources[..., None, :]
    earlier = jnp.arange(positions)[None, :] < jnp.arange(positions)[:, None]
    return jnp.sum(jnp.where(alike & earlier, 1, 0), axis=-1).astype(jnp.int32)


def windows_kernel(own_ref, next_ref, incoming_ref, out_ref):
    last = pl.program_id(0) == pl.num_programs(0) - 1
    early = lax.broadcasted_iota(jnp.int32, (SPAN, HDIM), 0) < SPAN - 1
    pairs = out_ref.shape[1]
    for pair in range(pairs):
        halves = []
        for head in (2 * pair, 2 * pair + 1):
            cols = slice(head * HDIM, (head + 1) * HDIM)
            later = jnp.where(last, incoming_ref[:, cols], next_ref[:, cols])
            halves.append(
                jnp.where(early, later.astype(jnp.float32), own_ref[:, cols].astype(jnp.float32))
            )
        out_ref[0, pair] = jnp.concatenate(halves, axis=0).astype(jnp.bfloat16).T


def transposed_windows(queries, incoming, span_count):
    columns = queries.shape[-1]
    pairs = columns // PAIR
    return pl.pallas_call(
        windows_kernel,
        grid=(span_count,),
        in_specs=[
            pl.BlockSpec((SPAN, columns), lambda u: (u, 0)),
            pl.BlockSpec((SPAN, columns), lambda u: (jnp.minimum(u + 1, span_count - 1), 0)),
            pl.BlockSpec((SPAN, columns), lambda u: (0, 0)),
        ],
        out_specs=pl.BlockSpec((1, pairs, HDIM, 2 * SPAN), lambda u: (u, 0, 0, 0)),
        out_shape=jax.ShapeDtypeStruct((span_count, pairs, HDIM, 2 * SPAN), jnp.bfloat16),
        compiler_params=pltpu.CompilerParams(vmem_limit_bytes=VMEM_LIMIT),
        name="windows",
    )(queries, queries, incoming)


def pick_kernel(table, *refs):
    outs = refs[-(INNER - 1) :]
    ins = refs[: -(INNER - 1)]
    parts = len(ins) // (INNER - 1)
    for k, out_ref in enumerate(outs):
        for part in range(parts):
            out_ref[0, part] = ins[k * parts + part][0]


def pick_blocks(table, parts):
    ranks = table.shape[-1]
    shape = parts[0].shape[1:]

    def wanted(k):
        return lambda r, table: (table[k, r], 0, 0)

    return pl.pallas_call(
        pick_kernel,
        grid_spec=pltpu.PrefetchScalarGridSpec(
            num_scalar_prefetch=1,
            grid=(ranks,),
            in_specs=[
                pl.BlockSpec((1,) + shape, wanted(k)) for k in range(1, INNER) for _ in parts
            ],
            out_specs=[
                pl.BlockSpec((1, len(parts)) + shape, lambda r, table: (r, 0, 0, 0))
                for _ in range(INNER - 1)
            ],
        ),
        out_shape=[
            jax.ShapeDtypeStruct((ranks, len(parts)) + shape, parts[0].dtype)
            for _ in range(INNER - 1)
        ],
        compiler_params=pltpu.CompilerParams(vmem_limit_bytes=VMEM_LIMIT),
        name="pick_blocks",
    )(table, *(list(parts) * (INNER - 1)))


def attend_kernel(ranks, parts, held, tp_index, picked, spans, *refs):
    cap = INNER * ranks
    own_refs = refs[: ranks * parts]
    got_refs = refs[ranks * parts : ranks * parts + INNER - 1]
    q_refs = refs[ranks * parts + INNER - 1 :][:cap]
    at = ranks * parts + INNER - 1 + cap
    wk_first, wk_odd, wk_even, wv_first, wv_odd, wv_even = refs[at : at + 6]
    out_ref, lse_ref, xt, k_even, v_even, k_odd, v_odd = refs[-7:]
    nlen = own_refs[0].shape[-1]
    step = pl.program_id(0)
    scale = HDIM ** (-0.5)
    low_lanes = lax.broadcasted_iota(jnp.int32, (HDIM, 2 * SPAN), 1) < SPAN

    def project(wk_ref, wv_ref, k_ref, v_ref):
        rows = xt[...]
        k_ref[...] = jnp.dot(rows, wk_ref[...], preferred_element_type=jnp.float32).astype(
            jnp.bfloat16
        )
        v_ref[...] = jnp.dot(rows, wv_ref[...], preferred_element_type=jnp.float32).astype(
            jnp.bfloat16
        )

    def attend(which, k_ref, v_ref):
        cols = slice(which * PAIR, (which + 1) * PAIR)
        none = jnp.zeros((HDIM, 2 * SPAN), jnp.bfloat16)
        for i in range(cap):
            rows = slice(i * nlen, (i + 1) * nlen)
            q = q_refs[i][0, which]
            both = jnp.concatenate(
                [jnp.where(low_lanes, q, none), jnp.where(low_lanes, none, q)], axis=0
            )
            scores = jnp.dot(k_ref[rows, :], both, preferred_element_type=jnp.float32)
            highest = jnp.max(scores, axis=0, keepdims=True)
            exponent = jnp.exp((scores - highest) * scale)
            totals = jnp.sum(exponent, axis=0, keepdims=True)
            weights = (exponent * (1.0 / totals)).astype(jnp.bfloat16)
            blended = lax.dot_general(
                weights,
                v_ref[rows, :],
                (((0,), (0,)), ((), ())),
                preferred_element_type=jnp.float32,
            )
            out_ref[i, :, cols] = jnp.concatenate(
                [blended[:SPAN, :HDIM], blended[SPAN:, HDIM:]], axis=1
            ).astype(jnp.bfloat16)
            lse_ref[i, pl.ds(2 * step + which, 1), :] = highest * scale + jnp.log(totals)

    @pl.when(step == 0)
    def _():
        lse_ref[...] = jnp.zeros_like(lse_ref)
        for i in range(cap):
            if i < ranks:
                pieces = [own_refs[i * parts + part][0] for part in range(parts)]
            else:
                block = got_refs[i // ranks - 1]
                pieces = [block[i % ranks, part] for part in range(parts)]
            if parts == 2:
                lower = tp_index[0] == 0
                pieces = [
                    jnp.where(lower, pieces[0], pieces[1]),
                    jnp.where(lower, pieces[1], pieces[0]),
                ]
            xt[i * nlen : (i + 1) * nlen, :] = jnp.concatenate(pieces, axis=0).T
        project(wk_first, wv_first, k_even, v_even)

    project(wk_odd, wv_odd, k_odd, v_odd)
    attend(0, k_even, v_even)
    project(wk_even, wv_even, k_even, v_even)
    attend(1, k_odd, v_odd)


def attend_part(tp_index, picked, spans, own, got, windows, weights, part_index, slots, held):
    ranks, parts = picked.shape[0], len(own)
    cap = INNER * ranks
    width, nlen = own[0].shape[1:]
    features = width * parts
    span_count, pairs = windows.shape[:2]
    steps = pairs // 2
    stat_rows = max(pairs, 8)

    def own_at(r):
        return lambda t, tp_index, picked, spans: (picked[r], 0, 0)

    def window_at(i):
        return lambda t, tp_index, picked, spans: (spans[i], t, 0, 0)

    in_specs = [pl.BlockSpec((1, width, nlen), own_at(r)) for r in range(ranks) for _ in own]
    operands = list(own) * ranks
    in_specs += [pl.BlockSpec(g.shape, lambda t, *_: (0, 0, 0, 0)) for g in got]
    operands += list(got)
    in_specs += [pl.BlockSpec((1, 2, HDIM, 2 * SPAN), window_at(i)) for i in range(cap)]
    operands += [windows] * cap
    for weight in weights:
        in_specs += [
            pl.BlockSpec((features, PAIR), lambda t, *_: (0, 0)),
            pl.BlockSpec((features, PAIR), lambda t, *_: (0, 2 * t + 1)),
            pl.BlockSpec((features, PAIR), lambda t, *_: (0, jnp.minimum(2 * t + 2, pairs - 1))),
        ]
        operands += [weight] * 3
    aliases = {}
    if held is not None:
        in_specs += [pl.BlockSpec(memory_space=pl.ANY)] * 2
        aliases = {3 + len(operands): 0, 4 + len(operands): 1}
        operands += list(held)
    kv = pltpu.VMEM((cap * nlen, PAIR), jnp.bfloat16)

    def body(*refs):
        attend_kernel(ranks, parts, held, *refs)

    return pl.pallas_call(
        body,
        grid_spec=pltpu.PrefetchScalarGridSpec(
            num_scalar_prefetch=3,
            grid=(steps,),
            in_specs=in_specs,
            out_specs=[
                pl.BlockSpec((cap, SPAN, 2 * PAIR), lambda t, *_: (part_index, 0, t)),
                pl.BlockSpec((cap, stat_rows, 2 * SPAN), lambda t, *_: (part_index, 0, 0)),
            ],
            scratch_shapes=[pltpu.VMEM((cap * nlen, features), jnp.bfloat16), kv, kv, kv, kv],
        ),
        out_shape=[
            jax.ShapeDtypeStruct((slots, SPAN, pairs * PAIR), jnp.bfloat16),
            jax.ShapeDtypeStruct((slots, stat_rows, 2 * SPAN), jnp.float32),
        ],
        input_output_aliases=aliases,
        compiler_params=pltpu.CompilerParams(vmem_limit_bytes=VMEM_LIMIT),
        name="attend_part",
    )(tp_index, picked, spans, *operands)


def first_shares(l0, l1):
    largest = jnp.maximum(l0, l1)
    e0, e1 = jnp.exp(l0 - largest), jnp.exp(l1 - largest)
    return (e0 / (e0 + e1)).T


def mixed(p0, p1, shares, head):
    cols = slice(head * HDIM, (head + 1) * HDIM)
    half = slice((head % 2) * SPAN, (head % 2 + 1) * SPAN)
    share = shares[half, head // 2 : head // 2 + 1]
    return p0[0, :, cols].astype(jnp.float32) * share + p1[0, :, cols].astype(jnp.float32) * (
        1.0 - share
    )


def mix_last_kernel(places, p0, p1, l0, l1, out_ref):
    shares = first_shares(l0[0], l1[0])
    for head in range(out_ref.shape[-1] // HDIM):
        cols = slice(head * HDIM, (head + 1) * HDIM)
        out_ref[:, cols] = mixed(p0, p1, shares, head).astype(jnp.bfloat16)


def mix_kernel(places, p0, p1, l0, l1, carried, out_ref, before):
    @pl.when(pl.program_id(0) == 0)
    def _():
        before[...] = carried[...]

    shares = first_shares(l0[0], l1[0])
    early = lax.broadcasted_iota(jnp.int32, (SPAN, HDIM), 0) < SPAN - 1
    for head in range(out_ref.shape[-1] // HDIM):
        cols = slice(head * HDIM, (head + 1) * HDIM)
        result = mixed(p0, p1, shares, head)
        out_ref[:, cols] = jnp.where(early, before[:, cols].astype(jnp.float32), result).astype(
            jnp.bfloat16
        )
        before[:, cols] = result.astype(jnp.bfloat16)


def mix_specs(partials, log_totals, span_of):
    def place(j, shape):
        return pl.BlockSpec((1,) + shape, lambda k, places: (places[2 * span_of(k) + j], 0, 0))

    rows, stats = partials.shape[1:], log_totals.shape[1:]
    return [place(0, rows), place(1, rows), place(0, stats), place(1, stats)]


def mix_last(places, partials, log_totals, span_count):
    columns = partials.shape[-1]
    return pl.pallas_call(
        mix_last_kernel,
        grid_spec=pltpu.PrefetchScalarGridSpec(
            num_scalar_prefetch=1,
            grid=(1,),
            in_specs=mix_specs(partials, log_totals, lambda k: span_count - 1),
            out_specs=pl.BlockSpec((SPAN, columns), lambda k, places: (0, 0)),
        ),
        out_shape=jax.ShapeDtypeStruct((SPAN, columns), jnp.bfloat16),
        name="mix_last",
    )(places, partials, partials, log_totals, log_totals)


def mix(places, partials, log_totals, carried, span_count):
    columns = partials.shape[-1]
    return pl.pallas_call(
        mix_kernel,
        grid_spec=pltpu.PrefetchScalarGridSpec(
            num_scalar_prefetch=1,
            grid=(span_count,),
            in_specs=mix_specs(partials, log_totals, lambda k: k)
            + [pl.BlockSpec((SPAN, columns), lambda k, places: (0, 0))],
            out_specs=pl.BlockSpec((SPAN, columns), lambda k, places: (k, 0)),
            scratch_shapes=[pltpu.VMEM((SPAN, columns), jnp.bfloat16)],
        ),
        out_shape=jax.ShapeDtypeStruct((span_count * SPAN, columns), jnp.bfloat16),
        compiler_params=pltpu.CompilerParams(vmem_limit_bytes=VMEM_LIMIT),
        name="mix",
    )(places, partials, partials, log_totals, log_totals, carried)


def shards(queries, neighbours, key_weight, value_weight, neighbour_ids):
    span_count = neighbour_ids.shape[0]
    seq_count, tp_count = lax.axis_size("seq"), lax.axis_size("tp")
    block_count = neighbours.shape[0]
    wants = 2 * span_count
    ranks = (wants + seq_count - 1) // seq_count
    outer = seq_count // INNER
    slots = seq_count * ranks
    own_index = lax.axis_index("seq")
    tp_index = lax.axis_index("tp").astype(jnp.int32).reshape(1)

    held_parts = [neighbours]
    for j in range(1, outer):
        low = j & -j
        held_parts.append(swapped(held_parts[j ^ low], "seq", INNER * low))

    def all_features(part):
        if tp_count == 2:
            return [part, swapped(part, "tp", 1)]
        return [lax.all_gather(part, "tp", axis=1, tiled=True)]

    incoming = passed_along(queries[:SPAN], "seq", -1)
    windows = transposed_windows(queries, incoming, span_count)

    all_ids = lax.all_gather(neighbour_ids, "seq", axis=0, tiled=True).reshape(seq_count, wants)
    group_ids = all_ids[own_index ^ jnp.arange(INNER)]
    group_sources = group_ids // block_count
    group_ranks = slot_ranks(group_sources)
    part_sources = own_index ^ (INNER * jnp.arange(outer))
    hit = (group_sources[None, :, None, :] == part_sources[:, None, None, None]) & (
        group_ranks[None, :, None, :] == jnp.arange(ranks)[None, None, :, None]
    )
    table = jnp.sum(jnp.where(hit, (group_ids % block_count)[None, :, None, :], 0), axis=-1)
    table = table.astype(jnp.int32)

    own_ids = neighbour_ids.reshape(wants)
    own_sources = own_ids // block_count
    places = ((own_sources ^ own_index) * ranks + slot_ranks(own_sources)).astype(jnp.int32)
    order = jnp.arange(wants)
    spans = jnp.sum(
        jnp.where(places[None, :] == jnp.arange(slots)[:, None], order[None, :] // 2, 0), axis=1
    ).astype(jnp.int32)
    spans = spans.reshape(outer, INNER * ranks)

    held = None
    for j in range(outer):
        own = all_features(held_parts[j])
        outgoing = pick_blocks(table[j], own)
        got = [swapped(outgoing[k - 1], "seq", k) for k in range(1, INNER)]
        held = attend_part(
            tp_index, table[j, 0], spans[j], own, got, windows,
            (key_weight, value_weight), j, slots, held,
        )
    partials, log_totals = held
    last = mix_last(places, partials, log_totals, span_count)
    carried = passed_along(last, "seq", 1)
    return mix(places, partials, log_totals, carried, span_count)


def solution(mesh):
    in_specs = (P("seq", "tp"), P("seq", "tp", None), P(None, "tp"), P(None, "tp"), P("seq", None))
    out_specs = P("seq", "tp")
    return jax.shard_map(shards, mesh=mesh, in_specs=in_specs, out_specs=out_specs, check_vma=False)
```

time: 361 us -> 283 us (0.78)
  Pallas kernels: 203 us -> 117 us
  waiting for transfers between devices: 9.55 us -> 91.9 us
  blocking collectives: 118 us -> 35.7 us
  starting transfers between devices: 5.62 us -> 26.8 us
  between operations: 13.5 us -> 0.34 us
  other arithmetic: 6.36 us -> 0.88 us
  local copies, waits for them, and re-layouts: 3.84 us -> 9.01 us
    pallas_call x2 -> x4, Pallas kernels: 115 us -> 12.3 us  [pick_blocks(): pl.pallas_call(pick_kernel, grid_spec=pltpu.PrefetchScalarGridSpec(num_sc...]
    all_to_all x2 -> x0, blocking collectives: 94.7 us -> none  [shards(): lax.all_to_all(outgoing, 'seq', split_axis=0, concat_axis=0, tiled=True)]
    ppermute x0 -> x19, waiting for transfers between devices: none -> 88.3 us  [swapped(): return lax.ppermute(x, axis, [(i, i ^ offset) for i in range(peers)])]
    ppermute x0 -> x19, starting transfers between devices: none -> 21.2 us  [swapped(): return lax.ppermute(x, axis, [(i, i ^ offset) for i in range(peers)])]
    pallas_call x2 -> x5, Pallas kernels: 70.3 us -> 86.8 us  [the longest x4 75.1 us: attend_part(): pl.pallas_call(body, grid_spec=pltpu.PrefetchScalarGridSpec(num_scalar_pr...]
    all_gather x1, blocking collectives: 23.2 us -> 35.7 us  [shards(): lax.all_gather(neighbour_ids, 'seq', axis=0, tiled=True)]
    ppermute x2, waiting for transfers between devices: 7.7 us -> 3.61 us  [passed_along(): return lax.ppermute(x, axis, pairs)]
  transfers between devices with their start and end apart: 4 -> 21, of which waited for: 3 -> 7; matrix products, arithmetic and copies ran while one was open for 2% -> 3% of each run, Pallas kernels for 26% -> 29%
where the time goes in v1:
time: 283 us; the launch traced here: 282 us
  Pallas kernels  117 us (41%)
  waiting for transfers between devices  91.9 us (32%)
  blocking collectives  35.7 us (13%)
  starting transfers between devices  26.8 us (9%)
  local copies, waits for them, and re-layouts  9.01 us (3%)
    ppermute x19, waiting for transfers between devices, swapped(): return lax.ppermute(x, axis, [(i, i ^ offset) for i in range(peers)])  88.3 us
    pallas_call x4, Pallas kernels, attend_part(): pl.pallas_call(body, grid_spec=pltpu.PrefetchScalarGridSpec(num_scalar_pr...  75.1 us
    all_gather x1, blocking collectives, shards(): lax.all_gather(neighbour_ids, 'seq', axis=0, tiled=True)  35.7 us
    ppermute x19, starting transfers between devices, swapped(): return lax.ppermute(x, axis, [(i, i ^ offset) for i in range(peers)])  21.2 us
    pallas_call x1, Pallas kernels, mix(): pl.pallas_call(mix_kernel, grid_spec=pltpu.PrefetchScalarGridSpec(num_sca...  15.2 us
    pallas_call x4, Pallas kernels, pick_blocks(): pl.pallas_call(pick_kernel, grid_spec=pltpu.PrefetchScalarGridSpec(num_sc...  12.3 us
    pallas_call x1, Pallas kernels, transposed_windows(): pl.pallas_call(windows_kernel, grid=(span_count,), in_specs=[pl.BlockSpec...  11.6 us
  transfers between devices with their start and end apart: 21, of which 7 were waited for; matrix products, arithmetic and copies ran while one was open for 3% of the time, Pallas kernels for 29%

profile of v1, /device:TPU:1, one launch (start us, length us, event | category | flops | bytes accessed | tf_op | source)
XLA Modules:
  0.0 281.8 jit_solution(1235614513709585533)
XLA Ops:
  0.0 3.1 %collective-permute-start = (bf16[8,448,128]{2,1,0:T(8,128)(2,1)}, bf16[8,448,128]{2,1,0:T(8,128)(2,1)S(1)}, u32[]{:S(2)}, u32[]{:S(2)}) collective-permute-start(bf16[8,448,128]{2,1,0:T(8,128)(2,1)} %refs_5_.1), channel_id=1, source_target_pairs={{0,16},{2,18},{4,20},{6,22},{8,24},{10,26},{12,28},{14,30},{16,0},... | collective-permute-start | bytes 2752520 | tf_op jit(solution)/shard_map/ppermute | solution.py:23
  5.7 37.5 %collective-permute-done.refs_0_.refs_2_.refs_4_.refs_3_.refs_5_ = bf16[8,448,128]{2,1,0:T(8,128)(2,1)S(1)} collective-permute-done((bf16[8,448,128]{2,1,0:T(8,128)(2,1)}, bf16[8,448,128]{2,1,0:T(8,128)(2,1)S(1)}, u32[]{:S(2)}, u32[]{:S(2)}) %collective-permute-start) | collective-permute-done | bytes 917536 | tf_op jit(solution)/shard_map/ppermute | solution.py:23
  44.4 35.7 %all-gather = s32[16,16,2]{1,2,0:T(2,128)S(1)} all-gather(s32[1,16,2]{1,2,0:T(2,128)} %bitcast.14), channel_id=1, replica_groups=mesh['seq'=16,'tp'=2] {'seq'}, dimensions={0}, use_global_device_ids=true | all-gather | bytes 2176 | tf_op jit(solution)/shard_map/all_gather | solution.py:338
  84.9 3.0 %pick_blocks.7 = (bf16[2,2,448,128]{3,2,1,0:T(8,128)(2,1)}, bf16[2,2,448,128]{3,2,1,0:T(8,128)(2,1)}, bf16[2,2,448,128]{3,2,1,0:T(8,128)(2,1)}) custom-call(s32[4,2]{1,0:T(4,128)} %copy.38.table, bf16[8,448,128]{2,1,0:T(8,128)(2,1)} %refs_5_.1, bf16[8,448,128]{2,1,0:T(8,128)(2,1)} %collective-permute-done.16.refs_1_.refs_3_.refs_5_.refs_4_.refs_6_, ...), custom_call_target="tpu_custom_call" | custom-call | tf_op jit(solution)/shard_map/pick_blocks/pallas_call | solution.py:82
  91.6 11.3 %collective-permute-done.12.refs_1_.refs_3_.refs_5_.refs_4_.refs_6_ = bf16[8,448,128]{2,1,0:T(8,128)(2,1)} collective-permute-done((bf16[8,448,128]{2,1,0:T(8,128)(2,1)S(1)}, bf16[8,448,128]{2,1,0:T(8,128)(2,1)}, u32[]{:S(2)}, u32[]{:S(2)}) %collective-permute-start.12) | collective-permute-done | bytes 917536 | tf_op jit(solution)/shard_map/ppermute | solution.py:23
  102.9 3.5 %collective-permute-start.6 = (bf16[64,2048]{1,0:T(8,128)(2,1)}, bf16[64,2048]{1,0:T(8,128)(2,1)S(1)}, u32[]{:S(2)}, u32[]{:S(2)}) collective-permute-start(bf16[64,2048]{1,0:T(8,128)(2,1)} %slice.46), channel_id=1, source_target_pairs={{2,0},{4,2},{6,4},{8,6},{10,8},{12,10},{14,12},{16,14},{18,16},{20... | collective-permute-start | bytes 786440 | tf_op jit(solution)/shard_map/ppermute | solution.py:18
  108.6 3.2 %pick_blocks.6 = (bf16[2,2,448,128]{3,2,1,0:T(8,128)(2,1)}, bf16[2,2,448,128]{3,2,1,0:T(8,128)(2,1)}, bf16[2,2,448,128]{3,2,1,0:T(8,128)(2,1)}) custom-call(s32[4,2]{1,0:T(4,128)} %copy.37.table, bf16[8,448,128]{2,1,0:T(8,128)(2,1)} %copy-done.2, bf16[8,448,128]{2,1,0:T(8,128)(2,1)} %collective-permute-done.12.refs_1_.refs_3_.refs_5_.refs_4_.refs_6_, ...), custom_call_target="tpu_custom_call" | custom-call | tf_op jit(solution)/shard_map/pick_blocks/pallas_call | solution.py:82
  111.9 10.7 %collective-permute-done.7.refs_1_.refs_3_.refs_5_.refs_4_.refs_6_ = bf16[8,448,128]{2,1,0:T(8,128)(2,1)} collective-permute-done((bf16[8,448,128]{2,1,0:T(8,128)(2,1)S(1)}, bf16[8,448,128]{2,1,0:T(8,128)(2,1)}, u32[]{:S(2)}, u32[]{:S(2)}) %collective-permute-start.7) | collective-permute-done | bytes 917536 | tf_op jit(solution)/shard_map/ppermute | solution.py:23
  122.6 2.5 collective-permute-start.19
  125.0 3.0 %pick_blocks.5 = (bf16[2,2,448,128]{3,2,1,0:T(8,128)(2,1)}, bf16[2,2,448,128]{3,2,1,0:T(8,128)(2,1)}, bf16[2,2,448,128]{3,2,1,0:T(8,128)(2,1)}) custom-call(s32[4,2]{1,0:T(4,128)} %copy.36.table, bf16[8,448,128]{2,1,0:T(8,128)(2,1)} %copy-done.1, bf16[8,448,128]{2,1,0:T(8,128)(2,1)} %collective-permute-done.7.refs_1_.refs_3_.refs_5_.refs_4_.refs_6_, ...), custom_call_target="tpu_custom_call" | custom-call | tf_op jit(solution)/shard_map/pick_blocks/pallas_call | solution.py:82
  130.4 11.9 %collective-permute-done.2.refs_1_.refs_3_.refs_5_.refs_4_.refs_6_ = bf16[8,448,128]{2,1,0:T(8,128)(2,1)} collective-permute-done((bf16[8,448,128]{2,1,0:T(8,128)(2,1)S(1)}, bf16[8,448,128]{2,1,0:T(8,128)(2,1)}, u32[]{:S(2)}, u32[]{:S(2)}) %collective-permute-start.2) | collective-permute-done | bytes 917536 | tf_op jit(solution)/shard_map/ppermute | solution.py:23
  142.2 1.9 collective-permute-start.10
  144.3 3.0 %pick_blocks.4 = (bf16[2,2,448,128]{3,2,1,0:T(8,128)(2,1)}, bf16[2,2,448,128]{3,2,1,0:T(8,128)(2,1)}, bf16[2,2,448,128]{3,2,1,0:T(8,128)(2,1)}) custom-call(s32[4,2]{1,0:T(4,128)} %copy.35.table, bf16[8,448,128]{2,1,0:T(8,128)(2,1)} %copy-done, bf16[8,448,128]{2,1,0:T(8,128)(2,1)} %collective-permute-done.2.refs_1_.refs_3_.refs_5_.refs_4_.refs_6_, ...), custom_call_target="tpu_custom_call" | custom-call | tf_op jit(solution)/shard_map/pick_blocks/pallas_call | solution.py:82
  148.7 7.1 %collective-permute-done.15.refs_9_ = bf16[2,2,448,128]{3,2,1,0:T(8,128)(2,1)S(1)} collective-permute-done((bf16[2,2,448,128]{3,2,1,0:T(8,128)(2,1)S(1)}, bf16[2,2,448,128]{3,2,1,0:T(8,128)(2,1)S(1)}, u32[]{:S(2)}, u32[]{:S(2)}) %collective-permute-start.15) | collective-permute-done | bytes 458784 | tf_op jit(solution)/shard_map/ppermute | solution.py:23
  155.9 9.8 %collective-permute-done.10.refs_9_ = bf16[2,2,448,128]{3,2,1,0:T(8,128)(2,1)S(1)} collective-permute-done((bf16[2,2,448,128]{3,2,1,0:T(8,128)(2,1)}, bf16[2,2,448,128]{3,2,1,0:T(8,128)(2,1)S(1)}, u32[]{:S(2)}, u32[]{:S(2)}) %collective-permute-start.10) | collective-permute-done | bytes 458784 | tf_op jit(solution)/shard_map/ppermute | solution.py:23
  168.8 11.6 %windows.1.refs_10_.refs_11_.refs_12_.refs_13_.refs_14_.refs_15_.refs_16_.refs_17_ = bf16[16,8,128,128]{3,2,1,0:T(8,128)(2,1)} custom-call(bf16[1024,2048]{1,0:T(8,128)(2,1)} %next_ref.1, bf16[1024,2048]{1,0:T(8,128)(2,1)} %next_ref.1, bf16[64,2048]{1,0:T(8,128)(2,1)} %copy-done.13), custom_call_target="tpu_custom_call" | custom-call | tf_op jit(solution)/shard_map/windows/pallas_call | solution.py:51
  180.5 18.8 %attend_part.4 = (bf16[32,64,2048]{2,1,0:T(8,128)(2,1)}, f32[32,8,128]{2,1,0:T(8,128)}) custom-call(s32[1]{0:T(128)} %bitcast.refs_0_, s32[2]{0:T(128)} %get-tuple-element.45.refs_1_, s32[8]{0:T(128)} %get-tuple-element.55.refs_2_, bf16[8,448,128]{2,1,0:T(8,128)(2,1)} %refs_5_.1, ...), custom_call_target="tpu_custom_call" | custom-call | tf_op jit(solution)/shard_map/attend_part/pallas_call | solution.py:213
  199.3 18.7 %attend_part.5 = (bf16[32,64,2048]{2,1,0:T(8,128)(2,1)}, f32[32,8,128]{2,1,0:T(8,128)}) custom-call(s32[1]{0:T(128)} %bitcast.refs_0_, s32[2]{0:T(128)} %get-tuple-element.46.refs_1_, s32[8]{0:T(128)} %get-tuple-element.56.refs_2_, bf16[8,448,128]{2,1,0:T(8,128)(2,1)} %copy-done.2, ...), custom_call_target="tpu_custom_call", output_to_operand_aliasing={{0}: (24, {}), {1}: (25, {})} | custom-call | tf_op jit(solution)/shard_map/attend_part/pallas_call | solution.py:213
  218.8 18.9 %attend_part.6 = (bf16[32,64,2048]{2,1,0:T(8,128)(2,1)}, f32[32,8,128]{2,1,0:T(8,128)}) custom-call(s32[1]{0:T(128)} %bitcast.refs_0_, s32[2]{0:T(128)} %get-tuple-element.47.refs_1_, s32[8]{0:T(128)} %get-tuple-element.57.refs_2_, bf16[8,448,128]{2,1,0:T(8,128)(2,1)} %copy-done.1, ...), custom_call_target="tpu_custom_call", output_to_operand_aliasing={{0}: (24, {}), {1}: (25, {})} | custom-call | tf_op jit(solution)/shard_map/attend_part/pallas_call | solution.py:213
  238.6 18.7 %attend_part.7 = (bf16[32,64,2048]{2,1,0:T(8,128)(2,1)}, f32[32,8,128]{2,1,0:T(8,128)}) custom-call(s32[1]{0:T(128)} %bitcast.refs_0_, s32[2]{0:T(128)} %get-tuple-element.48.refs_1_, s32[8]{0:T(128)} %get-tuple-element.58.refs_2_, bf16[8,448,128]{2,1,0:T(8,128)(2,1)} %copy-done, ...), custom_call_target="tpu_custom_call", output_to_operand_aliasing={{0}: (24, {}), {1}: (25, {})} | custom-call | tf_op jit(solution)/shard_map/attend_part/pallas_call | solution.py:213
  257.3 2.9 %mix_last.1 = bf16[64,2048]{1,0:T(8,128)(2,1)} custom-call(s32[32]{0:T(128)} %copy-done.14, bf16[32,64,2048]{2,1,0:T(8,128)(2,1)} %get-tuple-element.43.p0.p1, bf16[32,64,2048]{2,1,0:T(8,128)(2,1)} %get-tuple-element.43.p0.p1, f32[32,8,128]{2,1,0:T(8,128)} %get-tuple-element.44.l0.l1, f32[32,8,128]{2,1,0:T(8,128)} %get-tuple-element.44.l0.l1), custom_call_target="tpu_custom_call" | custom-call | tf_op jit(solution)/shard_map/mix_last/pallas_call | solution.py:283
  260.2 2.1 collective-permute-start.20
  262.3 3.6 %collective-permute-done.20.carried = bf16[64,2048]{1,0:T(8,128)(2,1)S(1)} collective-permute-done((bf16[64,2048]{1,0:T(8,128)(2,1)}, bf16[64,2048]{1,0:T(8,128)(2,1)S(1)}, u32[]{:S(2)}, u32[]{:S(2)}) %collective-permute-start.20) | collective-permute-done | bytes 262176 | tf_op jit(solution)/shard_map/ppermute | solution.py:18
  266.6 15.2 %mix.1 = bf16[1024,2048]{1,0:T(8,128)(2,1)} custom-call(s32[32]{0:T(128)} %copy-done.14, bf16[32,64,2048]{2,1,0:T(8,128)(2,1)} %get-tuple-element.43.p0.p1, bf16[32,64,2048]{2,1,0:T(8,128)(2,1)} %get-tuple-element.43.p0.p1, f32[32,8,128]{2,1,0:T(8,128)} %get-tuple-element.44.l0.l1, f32[32,8,128]{2,1,0:T(8,128)} %get-tuple-element.44.l0.l1, ...), custom_call_target="tpu_custom_call" | custom-call | tf_op jit(solution)/shard_map/mix/pallas_call | solution.py:298
  (97 shorter events, 23.7 us)
Async XLA Ops:
  0.0 106.4 %copy-start.15 = (s32[16,2]{0,1:T(2,128)S(1)}, s32[16,2]{0,1:T(2,128)}, u32[]{:S(2)}) copy-start(s32[16,2]{0,1:T(2,128)} %param.9) | copy-start | bytes 388
  0.0 43.1 %collective-permute-start = (bf16[8,448,128]{2,1,0:T(8,128)(2,1)}, bf16[8,448,128]{2,1,0:T(8,128)(2,1)S(1)}, u32[]{:S(2)}, u32[]{:S(2)}) collective-permute-start(bf16[8,448,128]{2,1,0:T(8,128)(2,1)} %refs_5_.1), channel_id=1, source_target_pairs={{0,16},{2,18},{4,20},{6,22},{8,24},{10,26},{12,28},{14,30},{16,0},... | collective-permute-start | bytes 2752520 | tf_op jit(solution)/shard_map/ppermute | solution.py:23
  3.1 77.8 %collective-permute-start.11 = (bf16[8,448,128]{2,1,0:T(8,128)(2,1)}, bf16[8,448,128]{2,1,0:T(8,128)(2,1)S(1)}, u32[]{:S(2)}, u32[]{:S(2)}) collective-permute-start(bf16[8,448,128]{2,1,0:T(8,128)(2,1)} %refs_5_.1), channel_id=1, source_target_pairs={{0,8},{2,10},{4,12},{6,14},{8,0},{10,2},{12,4},{14,6},{16,24},{18,... | collective-permute-start | bytes 2752520 | tf_op jit(solution)/shard_map/ppermute | solution.py:23
  4.4 80.4 %collective-permute-start.16 = (bf16[8,448,128]{2,1,0:T(8,128)(2,1)}, bf16[8,448,128]{2,1,0:T(8,128)(2,1)}, u32[]{:S(2)}, u32[]{:S(2)}) collective-permute-start(bf16[8,448,128]{2,1,0:T(8,128)(2,1)} %refs_5_.1), channel_id=1, source_target_pairs={{0,1},{1,0},{2,3},{3,2},{4,5},{5,4},{6,7},{7,6},{8,9},{9,8},{10,11... | collective-permute-start | bytes 2752520 | tf_op jit(solution)/shard_map/ppermute | solution.py:23
  43.1 68.7 %copy-start.1 = (bf16[8,448,128]{2,1,0:T(8,128)(2,1)}, bf16[8,448,128]{2,1,0:T(8,128)(2,1)S(1)}, u32[]{:S(2)}) copy-start(bf16[8,448,128]{2,1,0:T(8,128)(2,1)S(1)} %collective-permute-done.refs_0_.refs_2_.refs_4_.refs_3_.refs_5_) | copy-start | bytes 2752516
  43.1 39.7 %collective-permute-start.1 = (bf16[8,448,128]{2,1,0:T(8,128)(2,1)S(1)}, bf16[8,448,128]{2,1,0:T(8,128)(2,1)S(1)}, u32[]{:S(2)}, u32[]{:S(2)}) collective-permute-start(bf16[8,448,128]{2,1,0:T(8,128)(2,1)S(1)} %collective-permute-done.refs_0_.refs_2_.refs_4_.refs_3_.refs_5_), channel_id=1, source_target_pairs={{0,8},{2,10},{4,12},{6,14},{8,0},{10,2},{12,4},{14,6},{16,24},{18,... | collective-permute-start | bytes 2752520 | tf_op jit(solution)/shard_map/ppermute | solution.py:23
  81.0 21.9 %collective-permute-start.12 = (bf16[8,448,128]{2,1,0:T(8,128)(2,1)S(1)}, bf16[8,448,128]{2,1,0:T(8,128)(2,1)}, u32[]{:S(2)}, u32[]{:S(2)}) collective-permute-start(bf16[8,448,128]{2,1,0:T(8,128)(2,1)S(1)} %collective-permute-done.11.refs_0_.refs_2_.refs_4_.refs_3_.refs_5_), channel_id=1, source_target_pairs={{0,1},{1,0},{2,3},{3,2},{4,5},{5,4},{6,7},{7,6},{8,9},{9,8},{10,11... | collective-permute-start | bytes 2752520 | tf_op jit(solution)/shard_map/ppermute | solution.py:23
  82.5 40.1 %collective-permute-start.7 = (bf16[8,448,128]{2,1,0:T(8,128)(2,1)S(1)}, bf16[8,448,128]{2,1,0:T(8,128)(2,1)}, u32[]{:S(2)}, u32[]{:S(2)}) collective-permute-start(bf16[8,448,128]{2,1,0:T(8,128)(2,1)S(1)} %collective-permute-done.refs_0_.refs_2_.refs_4_.refs_3_.refs_5_), channel_id=1, source_target_pairs={{0,1},{1,0},{2,3},{3,2},{4,5},{5,4},{6,7},{7,6},{8,9},{9,8},{10,11... | collective-permute-start | bytes 2752520 | tf_op jit(solution)/shard_map/ppermute | solution.py:23
  82.8 59.4 %collective-permute-start.2 = (bf16[8,448,128]{2,1,0:T(8,128)(2,1)S(1)}, bf16[8,448,128]{2,1,0:T(8,128)(2,1)}, u32[]{:S(2)}, u32[]{:S(2)}) collective-permute-start(bf16[8,448,128]{2,1,0:T(8,128)(2,1)S(1)} %collective-permute-done.1.refs_0_.refs_2_.refs_4_.refs_3_.refs_5_), channel_id=1, source_target_pairs={{0,1},{1,0},{2,3},{3,2},{4,5},{5,4},{6,7},{7,6},{8,9},{9,8},{10,11... | collective-permute-start | bytes 2752520 | tf_op jit(solution)/shard_map/ppermute | solution.py:23
  87.9 40.2 %collective-permute-start.17 = (bf16[2,2,448,128]{3,2,1,0:T(8,128)(2,1)}, bf16[2,2,448,128]{3,2,1,0:T(8,128)(2,1)S(1)}, u32[]{:S(2)}, u32[]{:S(2)}) collective-permute-start(bf16[2,2,448,128]{3,2,1,0:T(8,128)(2,1)} %get-tuple-element.34), channel_id=1, source_target_pairs={{0,2},{2,0},{4,6},{6,4},{8,10},{10,8},{12,14},{14,12},{16,18},{18,... | collective-permute-start | bytes 1376264 | tf_op jit(solution)/shard_map/ppermute | solution.py:23
  88.9 39.8 %collective-permute-start.18 = (bf16[2,2,448,128]{3,2,1,0:T(8,128)(2,1)}, bf16[2,2,448,128]{3,2,1,0:T(8,128)(2,1)}, u32[]{:S(2)}, u32[]{:S(2)}) collective-permute-start(bf16[2,2,448,128]{3,2,1,0:T(8,128)(2,1)} %get-tuple-element.35), channel_id=1, source_target_pairs={{0,4},{2,6},{4,0},{6,2},{8,12},{10,14},{12,8},{14,10},{16,20},{18,... | collective-permute-start | bytes 1376264 | tf_op jit(solution)/shard_map/ppermute | solution.py:23
  102.9 25.2 %collective-permute-start.6 = (bf16[64,2048]{1,0:T(8,128)(2,1)}, bf16[64,2048]{1,0:T(8,128)(2,1)S(1)}, u32[]{:S(2)}, u32[]{:S(2)}) collective-permute-start(bf16[64,2048]{1,0:T(8,128)(2,1)} %slice.46), channel_id=1, source_target_pairs={{2,0},{4,2},{6,4},{8,6},{10,8},{12,10},{14,12},{16,14},{18,16},{20... | collective-permute-start | bytes 786440 | tf_op jit(solution)/shard_map/ppermute | solution.py:18
  122.6 24.8 %collective-permute-start.19 = (bf16[2,2,448,128]{3,2,1,0:T(8,128)(2,1)S(1)}, bf16[2,2,448,128]{3,2,1,0:T(8,128)(2,1)S(1)}, u32[]{:S(2)}, u32[]{:S(2)}) collective-permute-start(bf16[2,2,448,128]{3,2,1,0:T(8,128)(2,1)S(1)} %copy-done.16), channel_id=1, source_target_pairs={{0,6},{2,4},{4,2},{6,0},{8,14},{10,12},{12,10},{14,8},{16,22},{18,... | collective-permute-start | bytes 1376264 | tf_op jit(solution)/shard_map/ppermute | solution.py:23
  128.1 40.7 %copy-start.13 = (bf16[64,2048]{1,0:T(8,128)(2,1)}, bf16[64,2048]{1,0:T(8,128)(2,1)S(1)}, u32[]{:S(2)}) copy-start(bf16[64,2048]{1,0:T(8,128)(2,1)S(1)} %collective-permute-done.6.incoming_ref) | copy-start | bytes 786436
  128.1 19.4 %collective-permute-start.13 = (bf16[2,2,448,128]{3,2,1,0:T(8,128)(2,1)S(1)}, bf16[2,2,448,128]{3,2,1,0:T(8,128)(2,1)S(1)}, u32[]{:S(2)}, u32[]{:S(2)}) collective-permute-start(bf16[2,2,448,128]{3,2,1,0:T(8,128)(2,1)S(1)} %copy-done.19), channel_id=1, source_target_pairs={{0,2},{2,0},{4,6},{6,4},{8,10},{10,8},{12,14},{14,12},{16,18},{18,... | collective-permute-start | bytes 1376264 | tf_op jit(solution)/shard_map/ppermute | solution.py:23
  128.2 19.8 %collective-permute-start.14 = (bf16[2,2,448,128]{3,2,1,0:T(8,128)(2,1)S(1)}, bf16[2,2,448,128]{3,2,1,0:T(8,128)(2,1)S(1)}, u32[]{:S(2)}, u32[]{:S(2)}) collective-permute-start(bf16[2,2,448,128]{3,2,1,0:T(8,128)(2,1)S(1)} %copy-done.18), channel_id=1, source_target_pairs={{0,4},{2,6},{4,0},{6,2},{8,12},{10,14},{12,8},{14,10},{16,20},{18,... | collective-permute-start | bytes 1376264 | tf_op jit(solution)/shard_map/ppermute | solution.py:23
  128.8 27.1 %collective-permute-start.15 = (bf16[2,2,448,128]{3,2,1,0:T(8,128)(2,1)S(1)}, bf16[2,2,448,128]{3,2,1,0:T(8,128)(2,1)S(1)}, u32[]{:S(2)}, u32[]{:S(2)}) collective-permute-start(bf16[2,2,448,128]{3,2,1,0:T(8,128)(2,1)S(1)} %copy-done.17), channel_id=1, source_target_pairs={{0,6},{2,4},{4,2},{6,0},{8,14},{10,12},{12,10},{14,8},{16,22},{18,... | collective-permute-start | bytes 1376264 | tf_op jit(solution)/shard_map/ppermute | solution.py:23
  142.2 23.5 %collective-permute-start.10 = (bf16[2,2,448,128]{3,2,1,0:T(8,128)(2,1)}, bf16[2,2,448,128]{3,2,1,0:T(8,128)(2,1)S(1)}, u32[]{:S(2)}, u32[]{:S(2)}) collective-permute-start(bf16[2,2,448,128]{3,2,1,0:T(8,128)(2,1)} %get-tuple-element.30), channel_id=1, source_target_pairs={{0,6},{2,4},{4,2},{6,0},{8,14},{10,12},{12,10},{14,8},{16,22},{18,... | collective-permute-start | bytes 1376264 | tf_op jit(solution)/shard_map/ppermute | solution.py:23
  147.4 70.6 %collective-permute-start.8 = (bf16[2,2,448,128]{3,2,1,0:T(8,128)(2,1)}, bf16[2,2,448,128]{3,2,1,0:T(8,128)(2,1)S(1)}, u32[]{:S(2)}, u32[]{:S(2)}) collective-permute-start(bf16[2,2,448,128]{3,2,1,0:T(8,128)(2,1)} %get-tuple-element.28), channel_id=1, source_target_pairs={{0,2},{2,0},{4,6},{6,4},{8,10},{10,8},{12,14},{14,12},{16,18},{18,... | collective-permute-start | bytes 1376264 | tf_op jit(solution)/shard_map/ppermute | solution.py:23
  147.5 70.6 %collective-permute-start.9 = (bf16[2,2,448,128]{3,2,1,0:T(8,128)(2,1)}, bf16[2,2,448,128]{3,2,1,0:T(8,128)(2,1)}, u32[]{:S(2)}, u32[]{:S(2)}) collective-permute-start(bf16[2,2,448,128]{3,2,1,0:T(8,128)(2,1)} %get-tuple-element.29), channel_id=1, source_target_pairs={{0,4},{2,6},{4,0},{6,2},{8,12},{10,14},{12,8},{14,10},{16,20},{18,... | collective-permute-start | bytes 1376264 | tf_op jit(solution)/shard_map/ppermute | solution.py:23
  148.0 89.7 %collective-permute-start.3 = (bf16[2,2,448,128]{3,2,1,0:T(8,128)(2,1)}, bf16[2,2,448,128]{3,2,1,0:T(8,128)(2,1)S(1)}, u32[]{:S(2)}, u32[]{:S(2)}) collective-permute-start(bf16[2,2,448,128]{3,2,1,0:T(8,128)(2,1)} %get-tuple-element.25), channel_id=1, source_target_pairs={{0,2},{2,0},{4,6},{6,4},{8,10},{10,8},{12,14},{14,12},{16,18},{18,... | collective-permute-start | bytes 1376264 | tf_op jit(solution)/shard_map/ppermute | solution.py:23
  155.9 81.8 %collective-permute-start.4 = (bf16[2,2,448,128]{3,2,1,0:T(8,128)(2,1)}, bf16[2,2,448,128]{3,2,1,0:T(8,128)(2,1)S(1)}, u32[]{:S(2)}, u32[]{:S(2)}) collective-permute-start(bf16[2,2,448,128]{3,2,1,0:T(8,128)(2,1)} %get-tuple-element.26), channel_id=1, source_target_pairs={{0,4},{2,6},{4,0},{6,2},{8,12},{10,14},{12,8},{14,10},{16,20},{18,... | collective-permute-start | bytes 1376264 | tf_op jit(solution)/shard_map/ppermute | solution.py:23
  165.7 72.0 %collective-permute-start.5 = (bf16[2,2,448,128]{3,2,1,0:T(8,128)(2,1)}, bf16[2,2,448,128]{3,2,1,0:T(8,128)(2,1)}, u32[]{:S(2)}, u32[]{:S(2)}) collective-permute-start(bf16[2,2,448,128]{3,2,1,0:T(8,128)(2,1)} %get-tuple-element.27), channel_id=1, source_target_pairs={{0,6},{2,4},{4,2},{6,0},{8,14},{10,12},{12,10},{14,8},{16,22},{18,... | collective-permute-start | bytes 1376264 | tf_op jit(solution)/shard_map/ppermute | solution.py:23
  260.2 5.7 %collective-permute-start.20 = (bf16[64,2048]{1,0:T(8,128)(2,1)}, bf16[64,2048]{1,0:T(8,128)(2,1)S(1)}, u32[]{:S(2)}, u32[]{:S(2)}) collective-permute-start(bf16[64,2048]{1,0:T(8,128)(2,1)} %mix_last.1), channel_id=1, source_target_pairs={{0,2},{2,4},{4,6},{6,8},{8,10},{10,12},{12,14},{14,16},{16,18},{18... | collective-permute-start | bytes 786440 | tf_op jit(solution)/shard_map/ppermute | solution.py:18
  (17 other events, 291.9 us)

commit v2 on v1

--- a/solution.py
+++ b/solution.py
@@ -63,100 +63,97 @@
     )(queries, queries, incoming)
 
 
-def pick_kernel(table, *refs):
-    outs = refs[-(INNER - 1) :]
-    ins = refs[: -(INNER - 1)]
-    parts = len(ins) // (INNER - 1)
+def pick_kernel(count, table, *refs):
+    outs = refs[-count:]
+    ins = refs[:-count]
+    parts = len(ins) // count
     for k, out_ref in enumerate(outs):
         for part in range(parts):
             out_ref[0, part] = ins[k * parts + part][0]
 
 
 def pick_blocks(table, parts):
-    ranks = table.shape[-1]
+    count, ranks = table.shape
     shape = parts[0].shape[1:]
 
     def wanted(k):
         return lambda r, table: (table[k, r], 0, 0)
 
-    return pl.pallas_call(
-        pick_kernel,
+    def body(*refs):
+        pick_kernel(count, *refs)
+
+    return pl.pallas_call(
+        body,
         grid_spec=pltpu.PrefetchScalarGridSpec(
             num_scalar_prefetch=1,
             grid=(ranks,),
-            in_specs=[
-                pl.BlockSpec((1,) + shape, wanted(k)) for k in range(1, INNER) for _ in parts
-            ],
+            in_specs=[pl.BlockSpec((1,) + shape, wanted(k)) for k in range(count) for _ in parts],
             out_specs=[
                 pl.BlockSpec((1, len(parts)) + shape, lambda r, table: (r, 0, 0, 0))
-                for _ in range(INNER - 1)
+                for _ in range(count)
             ],
         ),
         out_shape=[
-            jax.ShapeDtypeStruct((ranks, len(parts)) + shape, parts[0].dtype)
-            for _ in range(INNER - 1)
+            jax.ShapeDtypeStruct((ranks, len(parts)) + shape, parts[0].dtype) for _ in range(count)
         ],
         compiler_params=pltpu.CompilerParams(vmem_limit_bytes=VMEM_LIMIT),
         name="pick_blocks",
-    )(table, *(list(parts) * (INNER - 1)))
-
-
-def attend_kernel(ranks, parts, held, tp_index, picked, spans, *refs):
-    cap = INNER * ranks
-    own_refs = refs[: ranks * parts]
-    got_refs = refs[ranks * parts : ranks * parts + INNER - 1]
-    q_refs = refs[ranks * parts + INNER - 1 :][:cap]
-    at = ranks * parts + INNER - 1 + cap
-    wk_first, wk_odd, wk_even, wv_first, wv_odd, wv_even = refs[at : at + 6]
-    out_ref, lse_ref, xt, k_even, v_even, k_odd, v_odd = refs[-7:]
-    nlen = own_refs[0].shape[-1]
+    )(table, *(list(parts) * count))
+
+
+def attend_kernel(cap, piece_of, count, parts, tp_index, picked, spans, *refs):
+    x_refs = refs[:count]
+    q_refs = refs[count : count + cap]
+    wk_first, wk_odd, wk_even, wv_first, wv_odd, wv_even = refs[count + cap : count + cap + 6]
+    out_ref, lse_ref, xt, scores_ref, weights_ref, k_even, v_even, k_odd, v_odd = refs[-9:]
+    nlen = scores_ref.shape[1]
     step = pl.program_id(0)
     scale = HDIM ** (-0.5)
     low_lanes = lax.broadcasted_iota(jnp.int32, (HDIM, 2 * SPAN), 1) < SPAN
 
-    def project(wk_ref, wv_ref, k_ref, v_ref):
-        rows = xt[...]
-        k_ref[...] = jnp.dot(rows, wk_ref[...], preferred_element_type=jnp.float32).astype(
+    def project(w_ref, out):
+        out[...] = jnp.dot(xt[...], w_ref[...], preferred_element_type=jnp.float32).astype(
             jnp.bfloat16
         )
-        v_ref[...] = jnp.dot(rows, wv_ref[...], preferred_element_type=jnp.float32).astype(
-            jnp.bfloat16
-        )
-
-    def attend(which, k_ref, v_ref):
-        cols = slice(which * PAIR, (which + 1) * PAIR)
+
+    def score(which, k_ref):
         none = jnp.zeros((HDIM, 2 * SPAN), jnp.bfloat16)
         for i in range(cap):
-            rows = slice(i * nlen, (i + 1) * nlen)
             q = q_refs[i][0, which]
             both = jnp.concatenate(
                 [jnp.where(low_lanes, q, none), jnp.where(low_lanes, none, q)], axis=0
             )
-            scores = jnp.dot(k_ref[rows, :], both, preferred_element_type=jnp.float32)
+            scores_ref[i] = jnp.dot(
+                k_ref[i * nlen : (i + 1) * nlen, :], both, preferred_element_type=jnp.float32
+            )
+
+    def soften(which):
+        for i in range(cap):
+            scores = scores_ref[i]
             highest = jnp.max(scores, axis=0, keepdims=True)
             exponent = jnp.exp((scores - highest) * scale)
             totals = jnp.sum(exponent, axis=0, keepdims=True)
-            weights = (exponent * (1.0 / totals)).astype(jnp.bfloat16)
+            weights_ref[i] = (exponent * (1.0 / totals)).astype(jnp.bfloat16)
+            lse_ref[i, pl.ds(2 * step + which, 1), :] = highest * scale + jnp.log(totals)
+
+    def blend(which, v_ref):
+        cols = slice(which * PAIR, (which + 1) * PAIR)
+        for i in range(cap):
             blended = lax.dot_general(
-                weights,
-                v_ref[rows, :],
+                weights_ref[i],
+                v_ref[i * nlen : (i + 1) * nlen, :],
                 (((0,), (0,)), ((), ())),
                 preferred_element_type=jnp.float32,
             )
             out_ref[i, :, cols] = jnp.concatenate(
                 [blended[:SPAN, :HDIM], blended[SPAN:, HDIM:]], axis=1
             ).astype(jnp.bfloat16)
-            lse_ref[i, pl.ds(2 * step + which, 1), :] = highest * scale + jnp.log(totals)
 
     @pl.when(step == 0)
     def _():
         lse_ref[...] = jnp.zeros_like(lse_ref)
         for i in range(cap):
-            if i < ranks:
-                pieces = [own_refs[i * parts + part][0] for part in range(parts)]
-            else:
-                block = got_refs[i // ranks - 1]
-                pieces = [block[i % ranks, part] for part in range(parts)]
+            pieces = [piece_of(x_refs, i, part) for part in range(parts)]
             if parts == 2:
                 lower = tp_index[0] == 0
                 pieces = [
@@ -164,21 +161,27 @@
                     jnp.where(lower, pieces[1], pieces[0]),
                 ]
             xt[i * nlen : (i + 1) * nlen, :] = jnp.concatenate(pieces, axis=0).T
-        project(wk_first, wv_first, k_even, v_even)
-
-    project(wk_odd, wv_odd, k_odd, v_odd)
-    attend(0, k_even, v_even)
-    project(wk_even, wv_even, k_even, v_even)
-    attend(1, k_odd, v_odd)
+        project(wk_first, k_even)
+        project(wv_first, v_even)
+
+    score(0, k_even)
+    project(wk_odd, k_odd)
+    soften(0)
+    project(wv_odd, v_odd)
+    blend(0, v_even)
+    score(1, k_odd)
+    project(wk_even, k_even)
+    soften(1)
+    project(wv_even, v_even)
+    blend(1, v_odd)
 
 
 def attend_part(tp_index, picked, spans, own, got, windows, weights, part_index, slots, held):
     ranks, parts = picked.shape[0], len(own)
-    cap = INNER * ranks
+    cap = spans.shape[0]
     width, nlen = own[0].shape[1:]
     features = width * parts
-    span_count, pairs = windows.shape[:2]
-    steps = pairs // 2
+    pairs = windows.shape[1]
     stat_rows = max(pairs, 8)
 
     def own_at(r):
@@ -187,10 +190,25 @@
     def window_at(i):
         return lambda t, tp_index, picked, spans: (spans[i], t, 0, 0)
 
-    in_specs = [pl.BlockSpec((1, width, nlen), own_at(r)) for r in range(ranks) for _ in own]
-    operands = list(own) * ranks
-    in_specs += [pl.BlockSpec(g.shape, lambda t, *_: (0, 0, 0, 0)) for g in got]
-    operands += list(got)
+    if got is None:
+        in_specs = [pl.BlockSpec(x.shape, lambda t, *_: (0, 0, 0)) for x in own]
+        operands = list(own)
+
+        def piece_of(refs, i, part):
+            return refs[part][i]
+
+    else:
+        in_specs = [pl.BlockSpec((1, width, nlen), own_at(r)) for r in range(ranks) for _ in own]
+        operands = list(own) * ranks
+        in_specs += [pl.BlockSpec(g.shape, lambda t, *_: (0, 0, 0, 0)) for g in got]
+        operands += list(got)
+
+        def piece_of(refs, i, part):
+            if i < ranks:
+                return refs[i * parts + part][0]
+            return refs[ranks * parts + i // ranks - 1][i % ranks, part]
+
+    count = len(operands)
     in_specs += [pl.BlockSpec((1, 2, HDIM, 2 * SPAN), window_at(i)) for i in range(cap)]
     operands += [windows] * cap
     for weight in weights:
@@ -208,19 +226,24 @@
     kv = pltpu.VMEM((cap * nlen, PAIR), jnp.bfloat16)
 
     def body(*refs):
-        attend_kernel(ranks, parts, held, *refs)
+        attend_kernel(cap, piece_of, count, parts, *refs)
 
     return pl.pallas_call(
         body,
         grid_spec=pltpu.PrefetchScalarGridSpec(
             num_scalar_prefetch=3,
-            grid=(steps,),
+            grid=(pairs // 2,),
             in_specs=in_specs,
             out_specs=[
                 pl.BlockSpec((cap, SPAN, 2 * PAIR), lambda t, *_: (part_index, 0, t)),
                 pl.BlockSpec((cap, stat_rows, 2 * SPAN), lambda t, *_: (part_index, 0, 0)),
             ],
-            scratch_shapes=[pltpu.VMEM((cap * nlen, features), jnp.bfloat16), kv, kv, kv, kv],
+            scratch_shapes=[
+                pltpu.VMEM((cap * nlen, features), jnp.bfloat16),
+                pltpu.VMEM((cap, nlen, 2 * SPAN), jnp.float32),
+                pltpu.VMEM((cap, nlen, 2 * SPAN), jnp.bfloat16),
+                kv, kv, kv, kv,
+            ],
         ),
         out_shape=[
             jax.ShapeDtypeStruct((slots, SPAN, pairs * PAIR), jnp.bfloat16),
@@ -254,20 +277,24 @@
         out_ref[:, cols] = mixed(p0, p1, shares, head).astype(jnp.bfloat16)
 
 
-def mix_kernel(places, p0, p1, l0, l1, carried, out_ref, before):
-    @pl.when(pl.program_id(0) == 0)
-    def _():
-        before[...] = carried[...]
-
-    shares = first_shares(l0[0], l1[0])
-    early = lax.broadcasted_iota(jnp.int32, (SPAN, HDIM), 0) < SPAN - 1
-    for head in range(out_ref.shape[-1] // HDIM):
-        cols = slice(head * HDIM, (head + 1) * HDIM)
-        result = mixed(p0, p1, shares, head)
-        out_ref[:, cols] = jnp.where(early, before[:, cols].astype(jnp.float32), result).astype(
-            jnp.bfloat16
-        )
-        before[:, cols] = result.astype(jnp.bfloat16)
+def mix_kernel(places, *refs):
+    ins, (out_ref, before) = refs[:-2], refs[-2:]
+    heads = out_ref.shape[-1] // HDIM
+    tile = 16
+    late = lax.broadcasted_iota(jnp.int32, (tile, HDIM), 0) == tile - 1
+    for n in range(len(ins) // 4):
+        p0, p1, l0, l1 = ins[4 * n : 4 * n + 4]
+        shares = first_shares(l0[0], l1[0])
+        top = n * SPAN
+        cut = top + SPAN - tile
+        out_ref[top:cut, :] = before[: SPAN - tile, :]
+        for head in range(heads):
+            cols = slice(head * HDIM, (head + 1) * HDIM)
+            result = mixed(p0, p1, shares, head)
+            out_ref[cut : cut + tile, cols] = jnp.where(
+                late, result[SPAN - tile :], before[SPAN - tile :, cols].astype(jnp.float32)
+            ).astype(jnp.bfloat16)
+            before[:, cols] = result.astype(jnp.bfloat16)
 
 
 def mix_specs(partials, log_totals, span_of):
@@ -293,22 +320,49 @@
     )(places, partials, partials, log_totals, log_totals)
 
 
-def mix(places, partials, log_totals, carried, span_count):
+def mix(places, partials, log_totals, span_count):
     columns = partials.shape[-1]
+    per = 2
+    in_specs = []
+    for n in range(per):
+        in_specs += mix_specs(partials, log_totals, lambda k, n=n: per * k + n)
     return pl.pallas_call(
         mix_kernel,
         grid_spec=pltpu.PrefetchScalarGridSpec(
             num_scalar_prefetch=1,
-            grid=(span_count,),
-            in_specs=mix_specs(partials, log_totals, lambda k: k)
-            + [pl.BlockSpec((SPAN, columns), lambda k, places: (0, 0))],
-            out_specs=pl.BlockSpec((SPAN, columns), lambda k, places: (k, 0)),
+            grid=(span_count // per,),
+            in_specs=in_specs,
+            out_specs=pl.BlockSpec((per * SPAN, columns), lambda k, places: (k, 0)),
             scratch_shapes=[pltpu.VMEM((SPAN, columns), jnp.bfloat16)],
         ),
         out_shape=jax.ShapeDtypeStruct((span_count * SPAN, columns), jnp.bfloat16),
         compiler_params=pltpu.CompilerParams(vmem_limit_bytes=VMEM_LIMIT),
         name="mix",
-    )(places, partials, partials, log_totals, log_totals, carried)
+    )(places, *([partials, partials, log_totals, log_totals] * per))
+
+
+def head_kernel(carried, rows, out_ref):
+    early = lax.broadcasted_iota(jnp.int32, out_ref.shape, 0) < SPAN - 1
+    out_ref[...] = jnp.where(
+        early, carried[...].astype(jnp.float32), rows[...].astype(jnp.float32)
+    ).astype(jnp.bfloat16)
+
+
+def with_head(carried, mixed_rows):
+    spec = pl.BlockSpec((SPAN, mixed_rows.shape[-1]), lambda k: (0, 0))
+    return pl.pallas_call(
+        head_kernel,
+        grid=(1,),
+        in_specs=[spec, spec],
+        out_specs=spec,
+        out_shape=jax.ShapeDtypeStruct(mixed_rows.shape, mixed_rows.dtype),
+        input_output_aliases={1: 0},
+        name="with_head",
+    )(carried, mixed_rows)
+
+
+def after(values, *others):
+    return lax.optimization_barrier((values, others))[0]
 
 
 def shards(queries, neighbours, key_weight, value_weight, neighbour_ids):
@@ -322,6 +376,10 @@
     own_index = lax.axis_index("seq")
     tp_index = lax.axis_index("tp").astype(jnp.int32).reshape(1)
 
+    own_ids = neighbour_ids.reshape(wants)
+    group_ids = jnp.stack([own_ids] + [swapped(own_ids, "seq", k) for k in range(1, INNER)])
+    incoming = passed_along(queries[:SPAN], "seq", -1)
+
     held_parts = [neighbours]
     for j in range(1, outer):
         low = j & -j
@@ -332,11 +390,8 @@
             return [part, swapped(part, "tp", 1)]
         return [lax.all_gather(part, "tp", axis=1, tiled=True)]
 
-    incoming = passed_along(queries[:SPAN], "seq", -1)
     windows = transposed_windows(queries, incoming, span_count)
 
-    all_ids = lax.all_gather(neighbour_ids, "seq", axis=0, tiled=True).reshape(seq_count, wants)
-    group_ids = all_ids[own_index ^ jnp.arange(INNER)]
     group_sources = group_ids // block_count
     group_ranks = slot_ranks(group_sources)
     part_sources = own_index ^ (INNER * jnp.arange(outer))
@@ -346,7 +401,6 @@
     table = jnp.sum(jnp.where(hit, (group_ids % block_count)[None, :, None, :], 0), axis=-1)
     table = table.astype(jnp.int32)
 
-    own_ids = neighbour_ids.reshape(wants)
     own_sources = own_ids // block_count
     places = ((own_sources ^ own_index) * ranks + slot_ranks(own_sources)).astype(jnp.int32)
     order = jnp.arange(wants)
@@ -355,19 +409,40 @@
     ).astype(jnp.int32)
     spans = spans.reshape(outer, INNER * ranks)
 
-    held = None
-    for j in range(outer):
+    weights = (key_weight, value_weight)
+
+    def attend(j, own, got, held):
+        return attend_part(
+            tp_index, table[j, 0], spans[j], own, got, windows, weights, j, slots, held
+        )
+
+    def features_first(j, *others):
         own = all_features(held_parts[j])
-        outgoing = pick_blocks(table[j], own)
-        got = [swapped(outgoing[k - 1], "seq", k) for k in range(1, INNER)]
-        held = attend_part(
-            tp_index, table[j, 0], spans[j], own, got, windows,
-            (key_weight, value_weight), j, slots, held,
-        )
+        outgoing = pick_blocks(table[j, 1:], after(own, *others))
+        return own, [swapped(outgoing[k - 1], "seq", k) for k in range(1, INNER)]
+
+    def wanted_first(j, *others):
+        outgoing = pick_blocks(table[j], after([held_parts[j]], *others))
+        wanted = [outgoing[0]] + [swapped(outgoing[k], "seq", k) for k in range(1, INNER)]
+        return outgoing, jnp.concatenate([w[:, 0] for w in wanted], axis=0)
+
+    own, got = features_first(0, windows)
+    picked, wanted = wanted_first(2)
+    held = attend(0, own, after(got, picked), None)
+    later = [(2, all_features(wanted))]
+    for j in range(3, outer):
+        _, wanted = wanted_first(j, held)
+        later.append((j, all_features(wanted)))
+    own, got = features_first(1, held)
+    held = attend(1, own, after(got, wanted), held)
+    for j, own in later:
+        held = attend(j, own, None, held)
+
     partials, log_totals = held
     last = mix_last(places, partials, log_totals, span_count)
     carried = passed_along(last, "seq", 1)
-    return mix(places, partials, log_totals, carried, span_count)
+    rows = mix(places, partials, log_totals, span_count)
+    return with_head(carried, rows)
 
 
 def solution(mesh):

time: 283 us -> 233 us (0.82)
  waiting for transfers between devices: 91.9 us -> 44.8 us
  blocking collectives: 35.7 us -> 0 us
  starting transfers between devices: 26.8 us -> 62.2 us
  Pallas kernels: 117 us -> 111 us
  other arithmetic: 0.88 us -> 4.01 us
    ppermute x19 -> x22, waiting for transfers between devices: 88.3 us -> 40.7 us  [swapped(): return lax.ppermute(x, axis, [(i, i ^ offset) for i in range(peers)])]
    all_gather x1 -> x0, blocking collectives: 35.7 us -> none  [shards(): lax.all_gather(neighbour_ids, 'seq', axis=0, tiled=True)]
    ppermute x19 -> x22, starting transfers between devices: 21.2 us -> 55.8 us  [swapped(): return lax.ppermute(x, axis, [(i, i ^ offset) for i in range(peers)])]
    pallas_call x1, Pallas kernels: 15.2 us -> 11.2 us  [mix(): pl.pallas_call(mix_kernel, grid_spec=pltpu.PrefetchScalarGridSpec(num_sca...]
    pallas_call x4, Pallas kernels: 75.1 us -> 71.9 us  [attend_part(): pl.pallas_call(body, grid_spec=pltpu.PrefetchScalarGridSpec(num_scalar_pr...]
    concatenate x0 -> x2, other arithmetic: none -> 3.13 us  [wanted_first(): return (outgoing, jnp.concatenate([w[:, 0] for w in wanted], axis=0))]
    pallas_call x4 -> x5, Pallas kernels: 12.3 us -> 13.5 us  [the longest x4 11.7 us: pick_blocks(): pl.pallas_call(body, grid_spec=pltpu.PrefetchScalarGridSpec(num_scalar_pr...]
  transfers between devices with their start and end apart: 21 -> 24, of which waited for: 7 -> 7; matrix products, arithmetic and copies ran while one was open for 3% -> 4% of each run, Pallas kernels for 29% -> 38%
where the time goes in v2:
time: 233 us; the launch traced here: 232 us
  Pallas kernels  111 us (48%)
  starting transfers between devices  62.2 us (27%)
  waiting for transfers between devices  44.8 us (19%)
  local copies, waits for them, and re-layouts  9.91 us (4%)
  other arithmetic  4.01 us (2%)
    pallas_call x4, Pallas kernels, attend_part(): pl.pallas_call(body, grid_spec=pltpu.PrefetchScalarGridSpec(num_scalar_pr...  71.9 us
    ppermute x22, starting transfers between devices, swapped(): return lax.ppermute(x, axis, [(i, i ^ offset) for i in range(peers)])  55.8 us
    ppermute x22, waiting for transfers between devices, swapped(): return lax.ppermute(x, axis, [(i, i ^ offset) for i in range(peers)])  40.7 us
    pallas_call x4, Pallas kernels, pick_blocks(): pl.pallas_call(body, grid_spec=pltpu.PrefetchScalarGridSpec(num_scalar_pr...  11.7 us
    pallas_call x1, Pallas kernels, transposed_windows(): pl.pallas_call(windows_kernel, grid=(span_count,), in_specs=[pl.BlockSpec...  11.6 us
    pallas_call x1, Pallas kernels, mix(): pl.pallas_call(mix_kernel, grid_spec=pltpu.PrefetchScalarGridSpec(num_sca...  11.2 us
    ppermute x2, starting transfers between devices, passed_along(): return lax.ppermute(x, axis, pairs)  6.44 us
    unnamed x29, local copies, waits for them, and re-layouts  4.82 us
  transfers between devices with their start and end apart: 24, of which 7 were waited for; matrix products, arithmetic and copies ran while one was open for 4% of the time, Pallas kernels for 38%

profile of v2, /device:TPU:1, one launch (start us, length us, event | category | flops | bytes accessed | tf_op | source)
XLA Modules:
  0.0 232.3 jit_solution(11405268195685086025)
XLA Ops:
  1.0 2.7 %collective-permute-start.1 = (s32[32]{0:T(128)S(1)}, s32[32]{0:T(128)S(1)}, u32[]{:S(2)}, u32[]{:S(2)}) collective-permute-start(s32[32]{0:T(128)S(1)} %reshape.601), channel_id=1, source_target_pairs={{0,4},{2,6},{4,0},{6,2},{8,12},{10,14},{12,8},{14,10},{16,20},{18,... | collective-permute-start | bytes 392 | tf_op jit(solution)/shard_map/ppermute | solution.py:23
  5.3 2.3 collective-permute-start.3
  10.3 2.9 %collective-permute-start.6 = (bf16[64,2048]{1,0:T(8,128)(2,1)S(1)}, bf16[64,2048]{1,0:T(8,128)(2,1)S(1)}, u32[]{:S(2)}, u32[]{:S(2)}) collective-permute-start(bf16[64,2048]{1,0:T(8,128)(2,1)S(1)} %slice.49), channel_id=1, source_target_pairs={{2,0},{4,2},{6,4},{8,6},{10,8},{12,10},{14,12},{16,14},{18,16},{20... | collective-permute-start | bytes 786440 | tf_op jit(solution)/shard_map/ppermute | solution.py:18
  14.5 4.1 %collective-permute-done.6.incoming_ref = bf16[64,2048]{1,0:T(8,128)(2,1)S(1)} collective-permute-done((bf16[64,2048]{1,0:T(8,128)(2,1)S(1)}, bf16[64,2048]{1,0:T(8,128)(2,1)S(1)}, u32[]{:S(2)}, u32[]{:S(2)}) %collective-permute-start.6) | collective-permute-done | bytes 262176 | tf_op jit(solution)/shard_map/ppermute | solution.py:18
  19.4 11.6 %windows.1.refs_10_.refs_11_.refs_12_.refs_13_.refs_14_.refs_15_.refs_16_.refs_17_.refs_5_.refs_6_.refs_7_.refs_8_.refs_9_ = bf16[16,8,128,128]{3,2,1,0:T(8,128)(2,1)} custom-call(bf16[1024,2048]{1,0:T(8,128)(2,1)} %next_ref.1, bf16[1024,2048]{1,0:T(8,128)(2,1)} %next_ref.1, bf16[64,2048]{1,0:T(8,128)(2,1)} %copy-done.10), custom_call_target="tpu_custom_call" | custom-call | tf_op jit(solution)/shard_map/windows/pallas_call | solution.py:51
  32.0 3.1 %pick_blocks.4 = (bf16[2,2,448,128]{3,2,1,0:T(8,128)(2,1)}, bf16[2,2,448,128]{3,2,1,0:T(8,128)(2,1)}, bf16[2,2,448,128]{3,2,1,0:T(8,128)(2,1)}) custom-call(s32[3,2]{1,0:T(4,128)} %copy.39.refs_0_, bf16[8,448,128]{2,1,0:T(8,128)(2,1)} %refs_5_.2, bf16[8,448,128]{2,1,0:T(8,128)(2,1)} %copy-done.1, bf16[8,448,128]{2,1,0:T(8,128)(2,1)} %refs_5_.2, ...), custom_call_target="tpu_custom_call" | custom-call | tf_op jit(solution)/shard_map/pick_blocks/pallas_call | solution.py:85
  35.0 35.2 %collective-permute-start.8 = (bf16[2,2,448,128]{3,2,1,0:T(8,128)(2,1)}, bf16[2,2,448,128]{3,2,1,0:T(8,128)(2,1)S(1)}, u32[]{:S(2)}, u32[]{:S(2)}) collective-permute-start(bf16[2,2,448,128]{3,2,1,0:T(8,128)(2,1)} %get-tuple-element.41), channel_id=1, source_target_pairs={{0,4},{2,6},{4,0},{6,2},{8,12},{10,14},{12,8},{14,10},{16,20},{18,... | collective-permute-start | bytes 1376264 | tf_op jit(solution)/shard_map/ppermute | solution.py:23
  71.9 2.8 %pick_blocks.5 = (bf16[2,1,448,128]{3,2,1,0:T(8,128)(2,1)}, bf16[2,1,448,128]{3,2,1,0:T(8,128)(2,1)}, bf16[2,1,448,128]{3,2,1,0:T(8,128)(2,1)}, bf16[2,1,448,128]{3,2,1,0:T(8,128)(2,1)}) custom-call(s32[4,2]{1,0:T(4,128)} %copy.40.refs_0_, bf16[8,448,128]{2,1,0:T(8,128)(2,1)} %copy-done.3, bf16[8,448,128]{2,1,0:T(8,128)(2,1)} %copy-done.3, ...), custom_call_target="tpu_custom_call" | custom-call | tf_op jit(solution)/shard_map/pick_blocks/pallas_call | solution.py:85
  76.3 4.8 %collective-permute-done.8.refs_8_ = bf16[2,2,448,128]{3,2,1,0:T(8,128)(2,1)S(1)} collective-permute-done((bf16[2,2,448,128]{3,2,1,0:T(8,128)(2,1)}, bf16[2,2,448,128]{3,2,1,0:T(8,128)(2,1)S(1)}, u32[]{:S(2)}, u32[]{:S(2)}) %collective-permute-start.8) | collective-permute-done | bytes 458784 | tf_op jit(solution)/shard_map/ppermute | solution.py:23
  81.1 3.1 %collective-permute-start.16 = (bf16[2,1,448,128]{3,2,0,1:T(8,128)(2,1)}, bf16[2,1,448,128]{3,2,0,1:T(8,128)(2,1)}, u32[]{:S(2)}, u32[]{:S(2)}) collective-permute-start(bf16[2,1,448,128]{3,2,0,1:T(8,128)(2,1)} %bitcast.35), channel_id=1, source_target_pairs={{0,6},{2,4},{4,2},{6,0},{8,14},{10,12},{12,10},{14,8},{16,22},{18,... | collective-permute-start | bytes 688136 | tf_op jit(solution)/shard_map/ppermute | solution.py:23
  85.4 6.6 %collective-permute-done.9.refs_9_ = bf16[2,2,448,128]{3,2,1,0:T(8,128)(2,1)} collective-permute-done((bf16[2,2,448,128]{3,2,1,0:T(8,128)(2,1)}, bf16[2,2,448,128]{3,2,1,0:T(8,128)(2,1)}, u32[]{:S(2)}, u32[]{:S(2)}) %collective-permute-start.9) | collective-permute-done | bytes 458784 | tf_op jit(solution)/shard_map/ppermute | solution.py:23
  93.0 18.1 %attend_part.4 = (bf16[32,64,2048]{2,1,0:T(8,128)(2,1)}, f32[32,8,128]{2,1,0:T(8,128)}) custom-call(s32[1]{0:T(128)} %bitcast.refs_0_, s32[2]{0:T(128)} %get-tuple-element.73.refs_1_, s32[8]{0:T(128)} %get-tuple-element.83.refs_2_, bf16[8,448,128]{2,1,0:T(8,128)(2,1)} %refs_5_.2, bf16[8,448,128]{2,1,0:T(8,128)(2,1)} %copy-done.1, ...), custom_call_target="tpu_custom_call" | custom-call | tf_op jit(solution)/shard_map/attend_part/pallas_call | solution.py:231
  111.1 2.8 %pick_blocks.6 = (bf16[2,1,448,128]{3,2,1,0:T(8,128)(2,1)}, bf16[2,1,448,128]{3,2,1,0:T(8,128)(2,1)}, bf16[2,1,448,128]{3,2,1,0:T(8,128)(2,1)}, bf16[2,1,448,128]{3,2,1,0:T(8,128)(2,1)}) custom-call(s32[4,2]{1,0:T(4,128)} %copy.41.refs_0_, bf16[8,448,128]{2,1,0:T(8,128)(2,1)} %collective-permute-done.4.refs_1_.refs_2_.refs_3_.refs_4_, ...), custom_call_target="tpu_custom_call" | custom-call | tf_op jit(solution)/shard_map/pick_blocks/pallas_call | solution.py:85
  118.5 2.9 %collective-permute-done.11 = bf16[2,1,448,128]{3,2,0,1:T(8,128)(2,1)S(1)} collective-permute-done((bf16[2,1,448,128]{3,2,0,1:T(8,128)(2,1)}, bf16[2,1,448,128]{3,2,0,1:T(8,128)(2,1)S(1)}, u32[]{:S(2)}, u32[]{:S(2)}) %collective-permute-start.11) | collective-permute-done | bytes 229408 | tf_op jit(solution)/shard_map/ppermute | solution.py:23
  121.4 5.5 %collective-permute-done.12 = bf16[2,1,448,128]{3,2,0,1:T(8,128)(2,1)S(1)} collective-permute-done((bf16[2,1,448,128]{3,2,0,1:T(8,128)(2,1)}, bf16[2,1,448,128]{3,2,0,1:T(8,128)(2,1)S(1)}, u32[]{:S(2)}, u32[]{:S(2)}) %collective-permute-start.12) | collective-permute-done | bytes 229408 | tf_op jit(solution)/shard_map/ppermute | solution.py:23
  131.6 3.0 %pick_blocks.7 = (bf16[2,2,448,128]{3,2,1,0:T(8,128)(2,1)}, bf16[2,2,448,128]{3,2,1,0:T(8,128)(2,1)}, bf16[2,2,448,128]{3,2,1,0:T(8,128)(2,1)}) custom-call(s32[3,2]{1,0:T(4,128)} %copy.48.refs_0_, bf16[8,448,128]{2,1,0:T(8,128)(2,1)} %copy-done, bf16[8,448,128]{2,1,0:T(8,128)(2,1)} %copy-done.2, bf16[8,448,128]{2,1,0:T(8,128)(2,1)} %copy-done, ...), custom_call_target="tpu_custom_call" | custom-call | tf_op jit(solution)/shard_map/pick_blocks/pallas_call | solution.py:85
  136.8 10.2 %collective-permute-done.21.refs_8_ = bf16[2,2,448,128]{3,2,1,0:T(8,128)(2,1)S(1)} collective-permute-done((bf16[2,2,448,128]{3,2,1,0:T(8,128)(2,1)}, bf16[2,2,448,128]{3,2,1,0:T(8,128)(2,1)S(1)}, u32[]{:S(2)}, u32[]{:S(2)}) %collective-permute-start.21) | collective-permute-done | bytes 458784 | tf_op jit(solution)/shard_map/ppermute | solution.py:23
  147.0 10.6 %collective-permute-done.22.refs_9_ = bf16[2,2,448,128]{3,2,1,0:T(8,128)(2,1)S(1)} collective-permute-done((bf16[2,2,448,128]{3,2,1,0:T(8,128)(2,1)}, bf16[2,2,448,128]{3,2,1,0:T(8,128)(2,1)S(1)}, u32[]{:S(2)}, u32[]{:S(2)}) %collective-permute-start.22) | collective-permute-done | bytes 458784 | tf_op jit(solution)/shard_map/ppermute | solution.py:23
  158.4 17.9 %attend_part.5 = (bf16[32,64,2048]{2,1,0:T(8,128)(2,1)}, f32[32,8,128]{2,1,0:T(8,128)}) custom-call(s32[1]{0:T(128)} %bitcast.refs_0_, s32[2]{0:T(128)} %get-tuple-element.71.refs_1_, s32[8]{0:T(128)} %get-tuple-element.81.refs_2_, bf16[8,448,128]{2,1,0:T(8,128)(2,1)} %copy-done, ...), custom_call_target="tpu_custom_call", output_to_operand_aliasing={{0}: (24, {}), {1}: (25, {})} | custom-call | tf_op jit(solution)/shard_map/attend_part/pallas_call | solution.py:231
  176.3 18.0 %attend_part.6 = (bf16[32,64,2048]{2,1,0:T(8,128)(2,1)}, f32[32,8,128]{2,1,0:T(8,128)}) custom-call(s32[1]{0:T(128)} %bitcast.refs_0_, s32[2]{0:T(128)} %get-tuple-element.72.refs_1_, s32[8]{0:T(128)} %get-tuple-element.82.refs_2_, bf16[8,448,128]{2,1,0:T(8,128)(2,1)} %copy-done.4, ...), custom_call_target="tpu_custom_call", output_to_operand_aliasing={{0}: (19, {}), {1}: (20, {})} | custom-call | tf_op jit(solution)/shard_map/attend_part/pallas_call | solution.py:231
  194.3 17.9 %attend_part.7 = (bf16[32,64,2048]{2,1,0:T(8,128)(2,1)}, f32[32,8,128]{2,1,0:T(8,128)}) custom-call(s32[1]{0:T(128)} %bitcast.refs_0_, s32[2]{0:T(128)} %get-tuple-element.74.refs_1_, s32[8]{0:T(128)} %get-tuple-element.84.refs_2_, bf16[8,448,128]{2,1,0:T(8,128)(2,1)} %pad_maximum_fusion.refs_3_, ...), custom_call_target="tpu_custom_call", output_to_operand_aliasing={{0}: (19, {}), {1}: (20, {})} | custom-call | tf_op jit(solution)/shard_map/attend_part/pallas_call | solution.py:231
  212.2 2.9 %mix_last.1 = bf16[64,2048]{1,0:T(8,128)(2,1)} custom-call(s32[32]{0:T(128)} %copy-done.13, bf16[32,64,2048]{2,1,0:T(8,128)(2,1)} %get-tuple-element.69.p0.p1.refs_0_.refs_1_.refs_4_.refs_5_, bf16[32,64,2048]{2,1,0:T(8,128)(2,1)} %get-tuple-element.69.p0.p1.refs_0_.refs_1_.refs_4_.refs_5_, ...), custom_call_target="tpu_custom_call" | custom-call | tf_op jit(solution)/shard_map/mix_last/pallas_call | solution.py:310
  215.1 3.5 %collective-permute-start.23 = (bf16[64,2048]{1,0:T(8,128)(2,1)}, bf16[64,2048]{1,0:T(8,128)(2,1)S(1)}, u32[]{:S(2)}, u32[]{:S(2)}) collective-permute-start(bf16[64,2048]{1,0:T(8,128)(2,1)} %mix_last.1), channel_id=1, source_target_pairs={{0,2},{2,4},{4,6},{6,8},{8,10},{10,12},{12,14},{14,16},{16,18},{18... | collective-permute-start | bytes 786440 | tf_op jit(solution)/shard_map/ppermute | solution.py:18
  218.7 11.2 %mix.1.rows = bf16[1024,2048]{1,0:T(8,128)(2,1)} custom-call(s32[32]{0:T(128)} %copy-done.13, bf16[32,64,2048]{2,1,0:T(8,128)(2,1)} %get-tuple-element.69.p0.p1.refs_0_.refs_1_.refs_4_.refs_5_, bf16[32,64,2048]{2,1,0:T(8,128)(2,1)} %get-tuple-element.69.p0.p1.refs_0_.refs_1_.refs_4_.refs_5_, ...), custom_call_target="tpu_custom_call" | custom-call | tf_op jit(solution)/shard_map/mix/pallas_call | solution.py:329
  (90 shorter events, 28.2 us)
Async XLA Ops:
  0.8 8.1 %collective-permute-start = (s32[32]{0:T(128)S(1)}, s32[32]{0:T(128)S(1)}, u32[]{:S(2)}, u32[]{:S(2)}) collective-permute-start(s32[32]{0:T(128)S(1)} %reshape.601), channel_id=1, source_target_pairs={{0,2},{2,0},{4,6},{6,4},{8,10},{10,8},{12,14},{14,12},{16,18},{18,... | collective-permute-start | bytes 392 | tf_op jit(solution)/shard_map/ppermute | solution.py:23
  1.0 9.3 %collective-permute-start.1 = (s32[32]{0:T(128)S(1)}, s32[32]{0:T(128)S(1)}, u32[]{:S(2)}, u32[]{:S(2)}) collective-permute-start(s32[32]{0:T(128)S(1)} %reshape.601), channel_id=1, source_target_pairs={{0,4},{2,6},{4,0},{6,2},{8,12},{10,14},{12,8},{14,10},{16,20},{18,... | collective-permute-start | bytes 392 | tf_op jit(solution)/shard_map/ppermute | solution.py:23
  3.7 9.6 %collective-permute-start.2 = (s32[32]{0:T(128)S(1)}, s32[32]{0:T(128)S(1)}, u32[]{:S(2)}, u32[]{:S(2)}) collective-permute-start(s32[32]{0:T(128)S(1)} %reshape.601), channel_id=1, source_target_pairs={{0,6},{2,4},{4,2},{6,0},{8,14},{10,12},{12,10},{14,8},{16,22},{18,... | collective-permute-start | bytes 392 | tf_op jit(solution)/shard_map/ppermute | solution.py:23
  3.7 27.3 %collective-permute-start.5 = (bf16[8,448,128]{2,1,0:T(8,128)(2,1)}, bf16[8,448,128]{2,1,0:T(8,128)(2,1)S(1)}, u32[]{:S(2)}, u32[]{:S(2)}) collective-permute-start(bf16[8,448,128]{2,1,0:T(8,128)(2,1)} %refs_5_.2), channel_id=1, source_target_pairs={{0,1},{1,0},{2,3},{3,2},{4,5},{5,4},{6,7},{7,6},{8,9},{9,8},{10,11... | collective-permute-start | bytes 2752520 | tf_op jit(solution)/shard_map/ppermute | solution.py:23
  5.3 64.9 %collective-permute-start.3 = (bf16[8,448,128]{2,1,0:T(8,128)(2,1)}, bf16[8,448,128]{2,1,0:T(8,128)(2,1)S(1)}, u32[]{:S(2)}, u32[]{:S(2)}) collective-permute-start(bf16[8,448,128]{2,1,0:T(8,128)(2,1)} %refs_5_.2), channel_id=1, source_target_pairs={{0,16},{2,18},{4,20},{6,22},{8,24},{10,26},{12,28},{14,30},{16,0},... | collective-permute-start | bytes 2752520 | tf_op jit(solution)/shard_map/ppermute | solution.py:23
  8.9 65.7 %collective-permute-start.18 = (bf16[8,448,128]{2,1,0:T(8,128)(2,1)}, bf16[8,448,128]{2,1,0:T(8,128)(2,1)S(1)}, u32[]{:S(2)}, u32[]{:S(2)}) collective-permute-start(bf16[8,448,128]{2,1,0:T(8,128)(2,1)} %refs_5_.2), channel_id=1, source_target_pairs={{0,8},{2,10},{4,12},{6,14},{8,0},{10,2},{12,4},{14,6},{16,24},{18,... | collective-permute-start | bytes 2752520 | tf_op jit(solution)/shard_map/ppermute | solution.py:23
  10.3 8.4 %collective-permute-start.6 = (bf16[64,2048]{1,0:T(8,128)(2,1)S(1)}, bf16[64,2048]{1,0:T(8,128)(2,1)S(1)}, u32[]{:S(2)}, u32[]{:S(2)}) collective-permute-start(bf16[64,2048]{1,0:T(8,128)(2,1)S(1)} %slice.49), channel_id=1, source_target_pairs={{2,0},{4,2},{6,4},{8,6},{10,8},{12,10},{14,12},{16,14},{18,16},{20... | collective-permute-start | bytes 786440 | tf_op jit(solution)/shard_map/ppermute | solution.py:18
  35.0 39.8 %collective-permute-start.7 = (bf16[2,2,448,128]{3,2,1,0:T(8,128)(2,1)}, bf16[2,2,448,128]{3,2,1,0:T(8,128)(2,1)S(1)}, u32[]{:S(2)}, u32[]{:S(2)}) collective-permute-start(bf16[2,2,448,128]{3,2,1,0:T(8,128)(2,1)} %get-tuple-element.40), channel_id=1, source_target_pairs={{0,2},{2,0},{4,6},{6,4},{8,10},{10,8},{12,14},{14,12},{16,18},{18,... | collective-permute-start | bytes 1376264 | tf_op jit(solution)/shard_map/ppermute | solution.py:23
  35.0 46.1 %collective-permute-start.8 = (bf16[2,2,448,128]{3,2,1,0:T(8,128)(2,1)}, bf16[2,2,448,128]{3,2,1,0:T(8,128)(2,1)S(1)}, u32[]{:S(2)}, u32[]{:S(2)}) collective-permute-start(bf16[2,2,448,128]{3,2,1,0:T(8,128)(2,1)} %get-tuple-element.41), channel_id=1, source_target_pairs={{0,4},{2,6},{4,0},{6,2},{8,12},{10,14},{12,8},{14,10},{16,20},{18,... | collective-permute-start | bytes 1376264 | tf_op jit(solution)/shard_map/ppermute | solution.py:23
  70.3 40.8 %collective-permute-start.4 = (bf16[8,448,128]{2,1,0:T(8,128)(2,1)S(1)}, bf16[8,448,128]{2,1,0:T(8,128)(2,1)}, u32[]{:S(2)}, u32[]{:S(2)}) collective-permute-start(bf16[8,448,128]{2,1,0:T(8,128)(2,1)S(1)} %collective-permute-done.3.refs_1_.refs_2_.refs_3_.refs_4_), channel_id=1, source_target_pairs={{0,8},{2,10},{4,12},{6,14},{8,0},{10,2},{12,4},{14,6},{16,24},{18,... | collective-permute-start | bytes 2752520 | tf_op jit(solution)/shard_map/ppermute | solution.py:23
  70.3 21.7 %collective-permute-start.9 = (bf16[2,2,448,128]{3,2,1,0:T(8,128)(2,1)}, bf16[2,2,448,128]{3,2,1,0:T(8,128)(2,1)}, u32[]{:S(2)}, u32[]{:S(2)}) collective-permute-start(bf16[2,2,448,128]{3,2,1,0:T(8,128)(2,1)} %get-tuple-element.42), channel_id=1, source_target_pairs={{0,6},{2,4},{4,2},{6,0},{8,14},{10,12},{12,10},{14,8},{16,22},{18,... | collective-permute-start | bytes 1376264 | tf_op jit(solution)/shard_map/ppermute | solution.py:23
  74.7 40.8 %collective-permute-start.14 = (bf16[2,1,448,128]{3,2,0,1:T(8,128)(2,1)}, bf16[2,1,448,128]{3,2,0,1:T(8,128)(2,1)S(1)}, u32[]{:S(2)}, u32[]{:S(2)}) collective-permute-start(bf16[2,1,448,128]{3,2,0,1:T(8,128)(2,1)} %bitcast.37), channel_id=1, source_target_pairs={{0,2},{2,0},{4,6},{6,4},{8,10},{10,8},{12,14},{14,12},{16,18},{18,... | collective-permute-start | bytes 688136 | tf_op jit(solution)/shard_map/ppermute | solution.py:23
  74.9 41.0 %collective-permute-start.15 = (bf16[2,1,448,128]{3,2,0,1:T(8,128)(2,1)}, bf16[2,1,448,128]{3,2,0,1:T(8,128)(2,1)}, u32[]{:S(2)}, u32[]{:S(2)}) collective-permute-start(bf16[2,1,448,128]{3,2,0,1:T(8,128)(2,1)} %bitcast.36), channel_id=1, source_target_pairs={{0,4},{2,6},{4,0},{6,2},{8,12},{10,14},{12,8},{14,10},{16,20},{18,... | collective-permute-start | bytes 688136 | tf_op jit(solution)/shard_map/ppermute | solution.py:23
  81.1 34.8 %collective-permute-start.16 = (bf16[2,1,448,128]{3,2,0,1:T(8,128)(2,1)}, bf16[2,1,448,128]{3,2,0,1:T(8,128)(2,1)}, u32[]{:S(2)}, u32[]{:S(2)}) collective-permute-start(bf16[2,1,448,128]{3,2,0,1:T(8,128)(2,1)} %bitcast.35), channel_id=1, source_target_pairs={{0,6},{2,4},{4,2},{6,0},{8,14},{10,12},{12,10},{14,8},{16,22},{18,... | collective-permute-start | bytes 688136 | tf_op jit(solution)/shard_map/ppermute | solution.py:23
  92.1 38.6 %collective-permute-start.19 = (bf16[8,448,128]{2,1,0:T(8,128)(2,1)S(1)}, bf16[8,448,128]{2,1,0:T(8,128)(2,1)S(1)}, u32[]{:S(2)}, u32[]{:S(2)}) collective-permute-start(bf16[8,448,128]{2,1,0:T(8,128)(2,1)S(1)} %collective-permute-done.18.refs_1_.refs_3_.refs_5_), channel_id=1, source_target_pairs={{0,1},{1,0},{2,3},{3,2},{4,5},{5,4},{6,7},{7,6},{8,9},{9,8},{10,11... | collective-permute-start | bytes 2752520 | tf_op jit(solution)/shard_map/ppermute | solution.py:23
  113.9 7.5 %collective-permute-start.11 = (bf16[2,1,448,128]{3,2,0,1:T(8,128)(2,1)}, bf16[2,1,448,128]{3,2,0,1:T(8,128)(2,1)S(1)}, u32[]{:S(2)}, u32[]{:S(2)}) collective-permute-start(bf16[2,1,448,128]{3,2,0,1:T(8,128)(2,1)} %bitcast.40), channel_id=1, source_target_pairs={{0,4},{2,6},{4,0},{6,2},{8,12},{10,14},{12,8},{14,10},{16,20},{18,... | collective-permute-start | bytes 688136 | tf_op jit(solution)/shard_map/ppermute | solution.py:23
  115.5 11.4 %collective-permute-start.12 = (bf16[2,1,448,128]{3,2,0,1:T(8,128)(2,1)}, bf16[2,1,448,128]{3,2,0,1:T(8,128)(2,1)S(1)}, u32[]{:S(2)}, u32[]{:S(2)}) collective-permute-start(bf16[2,1,448,128]{3,2,0,1:T(8,128)(2,1)} %bitcast.39), channel_id=1, source_target_pairs={{0,6},{2,4},{4,2},{6,0},{8,14},{10,12},{12,10},{14,8},{16,22},{18,... | collective-permute-start | bytes 688136 | tf_op jit(solution)/shard_map/ppermute | solution.py:23
  115.8 11.0 %collective-permute-start.10 = (bf16[2,1,448,128]{3,2,0,1:T(8,128)(2,1)}, bf16[2,1,448,128]{3,2,0,1:T(8,128)(2,1)S(1)}, u32[]{:S(2)}, u32[]{:S(2)}) collective-permute-start(bf16[2,1,448,128]{3,2,0,1:T(8,128)(2,1)} %bitcast.38), channel_id=1, source_target_pairs={{0,2},{2,0},{4,6},{6,4},{8,10},{10,8},{12,14},{14,12},{16,18},{18,... | collective-permute-start | bytes 688136 | tf_op jit(solution)/shard_map/ppermute | solution.py:23
  117.1 59.2 %collective-permute-start.17 = (bf16[8,448,128]{2,1,0:T(8,128)(2,1)S(1)}, bf16[8,448,128]{2,1,0:T(8,128)(2,1)}, u32[]{:S(2)}, u32[]{:S(2)}) collective-permute-start(bf16[8,448,128]{2,1,0:T(8,128)(2,1)S(1)} %pad_maximum_fusion.1.refs_3_), channel_id=1, source_target_pairs={{0,1},{1,0},{2,3},{3,2},{4,5},{5,4},{6,7},{7,6},{8,9},{9,8},{10,11... | collective-permute-start | bytes 2752520 | tf_op jit(solution)/shard_map/ppermute | solution.py:23
  128.8 65.5 %collective-permute-start.13 = (bf16[8,448,128]{2,1,0:T(8,128)(2,1)}, bf16[8,448,128]{2,1,0:T(8,128)(2,1)}, u32[]{:S(2)}, u32[]{:S(2)}) collective-permute-start(bf16[8,448,128]{2,1,0:T(8,128)(2,1)} %pad_maximum_fusion.refs_3_), channel_id=1, source_target_pairs={{0,1},{1,0},{2,3},{3,2},{4,5},{5,4},{6,7},{7,6},{8,9},{9,8},{10,11... | collective-permute-start | bytes 2752520 | tf_op jit(solution)/shard_map/ppermute | solution.py:23
  134.7 2.1 collective-permute-start.20
  134.7 12.3 %collective-permute-start.21 = (bf16[2,2,448,128]{3,2,1,0:T(8,128)(2,1)}, bf16[2,2,448,128]{3,2,1,0:T(8,128)(2,1)S(1)}, u32[]{:S(2)}, u32[]{:S(2)}) collective-permute-start(bf16[2,2,448,128]{3,2,1,0:T(8,128)(2,1)} %get-tuple-element.60), channel_id=1, source_target_pairs={{0,4},{2,6},{4,0},{6,2},{8,12},{10,14},{12,8},{14,10},{16,20},{18,... | collective-permute-start | bytes 1376264 | tf_op jit(solution)/shard_map/ppermute | solution.py:23
  136.4 21.2 %collective-permute-start.22 = (bf16[2,2,448,128]{3,2,1,0:T(8,128)(2,1)}, bf16[2,2,448,128]{3,2,1,0:T(8,128)(2,1)S(1)}, u32[]{:S(2)}, u32[]{:S(2)}) collective-permute-start(bf16[2,2,448,128]{3,2,1,0:T(8,128)(2,1)} %get-tuple-element.61), channel_id=1, source_target_pairs={{0,6},{2,4},{4,2},{6,0},{8,14},{10,12},{12,10},{14,8},{16,22},{18,... | collective-permute-start | bytes 1376264 | tf_op jit(solution)/shard_map/ppermute | solution.py:23
  215.1 14.7 %collective-permute-start.23 = (bf16[64,2048]{1,0:T(8,128)(2,1)}, bf16[64,2048]{1,0:T(8,128)(2,1)S(1)}, u32[]{:S(2)}, u32[]{:S(2)}) collective-permute-start(bf16[64,2048]{1,0:T(8,128)(2,1)} %mix_last.1), channel_id=1, source_target_pairs={{0,2},{2,4},{4,6},{6,8},{8,10},{10,12},{12,14},{14,16},{16,18},{18... | collective-permute-start | bytes 786440 | tf_op jit(solution)/shard_map/ppermute | solution.py:18
  (14 other events, 218.7 us)

commit v3 on v2

v3 whole, which is shorter than its diff:
```python
import jax
import jax.numpy as jnp
from jax import lax
from jax.experimental import pallas as pl
from jax.experimental.pallas import tpu as pltpu
from jax.sharding import PartitionSpec as P

HDIM = 128
SPAN = 64
PAIR = 2 * HDIM
INNER = 4
LANES = 128
VMEM_LIMIT = 56 * 1024 * 1024


def passed_along(x, axis, by):
    peers = lax.axis_size(axis)
    pairs = [(i, i + by) for i in range(peers) if 0 <= i + by < peers]
    return lax.ppermute(x, axis, pairs)


def swapped(x, axis, offset):
    peers = lax.axis_size(axis)
    return lax.ppermute(x, axis, [(i, i ^ offset) for i in range(peers)])


def slot_ranks(sources):
    positions = sources.shape[-1]
    alike = sources[..., :, None] == sources[..., None, :]
    earlier = jnp.arange(positions)[None, :] < jnp.arange(positions)[:, None]
    return jnp.sum(jnp.where(alike & earlier, 1, 0), axis=-1).astype(jnp.int32)


def windows_kernel(own_ref, next_ref, incoming_ref, out_ref):
    spans = out_ref.shape[0]
    last = pl.program_id(0) == pl.num_programs(0) - 1
    tile = 16
    cut = SPAN - tile
    late = lax.broadcasted_iota(jnp.int32, (tile, out_ref.shape[-1]), 0) == tile - 1
    for n in range(spans):
        if n + 1 < spans:
            later = own_ref[(n + 1) * SPAN : (n + 2) * SPAN, :]
        else:
            later = jnp.where(last, incoming_ref[...], next_ref[...])
        out_ref[n, :cut, :] = later[:cut]
        own = own_ref[n * SPAN + cut : (n + 1) * SPAN, :]
        out_ref[n, cut:, :] = jnp.where(
            late, own.astype(jnp.float32), later[cut:].astype(jnp.float32)
        ).astype(jnp.bfloat16)


def span_windows(queries, incoming, span_count):
    columns = queries.shape[-1]
    per = 4
    steps = span_count // per
    return pl.pallas_call(
        windows_kernel,
        grid=(steps,),
        in_specs=[
            pl.BlockSpec((per * SPAN, columns), lambda u: (u, 0)),
            pl.BlockSpec(
                (SPAN, columns), lambda u: (jnp.minimum(per * (u + 1), span_count - 1), 0)
            ),
            pl.BlockSpec((SPAN, columns), lambda u: (0, 0)),
        ],
        out_specs=pl.BlockSpec((per, SPAN, columns), lambda u: (u, 0, 0)),
        out_shape=jax.ShapeDtypeStruct((span_count, SPAN, columns), jnp.bfloat16),
        compiler_params=pltpu.CompilerParams(vmem_limit_bytes=VMEM_LIMIT),
        name="windows",
    )(queries, queries, incoming)


def pick_kernel(count, which, table, *refs):
    options = len(refs) - count - 3
    sources, outs = refs[:options], refs[options : options + count]
    held, in_sems, out_sems = refs[-3:]
    ranks = table.shape[1]
    places = [(k, r) for k in range(count) for r in range(ranks)]

    def fetch(source, n):
        return pltpu.make_async_copy(source.at[table[places[n]]], held.at[n], in_sems.at[n])

    for option, source in enumerate(sources):

        @pl.when(which[0] == option)
        def _(source=source):
            for n in range(len(places)):
                fetch(source, n).start()

    stores = []
    for n, (k, r) in enumerate(places):
        fetch(sources[0], n).wait()
        stores.append(pltpu.make_async_copy(held.at[n], outs[k].at[r], out_sems.at[n]))
        stores[-1].start()
    for store in stores:
        store.wait()


def pick_blocks(which, table, sources):
    count, ranks = table.shape
    shape = sources[0].shape[1:]
    copies = count * ranks

    def body(*refs):
        pick_kernel(count, *refs)

    return pl.pallas_call(
        body,
        grid_spec=pltpu.PrefetchScalarGridSpec(
            num_scalar_prefetch=2,
            grid=(1,),
            in_specs=[pl.BlockSpec(memory_space=pl.ANY)] * len(sources),
            out_specs=[pl.BlockSpec(memory_space=pl.ANY)] * count,
            scratch_shapes=[
                pltpu.VMEM((copies,) + shape, sources[0].dtype),
                pltpu.SemaphoreType.DMA((copies,)),
                pltpu.SemaphoreType.DMA((copies,)),
            ],
        ),
        out_shape=[jax.ShapeDtypeStruct((ranks,) + shape, sources[0].dtype) for _ in range(count)],
        compiler_params=pltpu.CompilerParams(vmem_limit_bytes=VMEM_LIMIT),
        name="pick_blocks",
    )(which, table, *sources)


def attend_kernel(cap, parts, steps, tp_index, spans, *refs):
    x_refs = refs[:parts]
    q_ref, wk_first, wk_next, wv_first, wv_next = refs[parts : parts + 5]
    out_ref, lse_ref, x_all, weights_ref, k_even, v_even, k_odd, v_odd = refs[-8:]
    nlen = x_refs[0].shape[-1]
    width = x_refs[0].shape[1]
    columns = q_ref.shape[-1]
    pairs = columns // PAIR
    step = pl.program_id(0)
    scale = HDIM ** (-0.5)
    lanes = lax.broadcasted_iota(jnp.int32, (SPAN, LANES), 1)
    rows = 2 * SPAN

    def two_slots(n):
        return pl.ds(pl.multiple_of(n * 2 * nlen, 2 * nlen), 2 * nlen)

    def project(n, w_ref, out):
        out[:, two_slots(n)] = jnp.dot(
            w_ref[...], x_all[:, two_slots(n)], preferred_element_type=jnp.float32
        ).astype(jnp.bfloat16)

    def window(slot, pair):
        q = q_ref[spans[slot], :, pair * PAIR : (pair + 1) * PAIR]
        none = jnp.zeros((SPAN, HDIM), jnp.bfloat16)
        upper = jnp.concatenate([q[:, :HDIM], none], axis=1)
        lower = jnp.concatenate([none, q[:, HDIM:]], axis=1)
        return [upper, lower]

    def soften(n, pair, both):
        for a in range(2):
            scores = both[a * rows : (a + 1) * rows, a * nlen : (a + 1) * nlen]
            highest = jnp.max(scores, axis=1, keepdims=True)
            exponent = jnp.exp((scores - highest) * scale)
            totals = jnp.sum(exponent, axis=1, keepdims=True)
            weights_ref[pair, a * rows : (a + 1) * rows, a * nlen : (a + 1) * nlen] = (
                exponent * (1.0 / totals)
            ).astype(jnp.bfloat16)
            lse = highest * scale + jnp.log(totals)
            at = pairs * step + pair
            held = jnp.where(lanes == at, lse[:SPAN], lse_ref[2 * n + a])
            lse_ref[2 * n + a] = jnp.where(lanes == LANES // 8 + at, lse[SPAN:], held)

    def attend(n, k_now, v_now, between):
        scores = []
        for pair in range(pairs):
            q = jnp.concatenate(window(2 * n, pair) + window(2 * n + 1, pair), axis=0)
            keys = k_now[pair * PAIR : (pair + 1) * PAIR, two_slots(n)]
            scores.append(jnp.dot(q, keys, preferred_element_type=jnp.float32))
        between[0]()
        for pair in range(pairs):
            soften(n, pair, scores[pair])
        between[1]()
        for pair in range(pairs):
            cols = slice(pair * PAIR, (pair + 1) * PAIR)
            blended = lax.dot_general(
                weights_ref[pair],
                v_now[cols, two_slots(n)],
                (((1,), (1,)), ((), ())),
                preferred_element_type=jnp.float32,
            )
            for a in range(2):
                top = a * rows
                out_ref[2 * n + a, :, cols] = jnp.concatenate(
                    [blended[top : top + SPAN, :HDIM], blended[top + SPAN : top + rows, HDIM:]],
                    axis=1,
                ).astype(jnp.bfloat16)

    def over_slots(body):
        def one(n, carry):
            body(n)
            return carry

        lax.fori_loop(0, cap // 2, one, 0)

    @pl.when(step == 0)
    def _():
        lse_ref[...] = jnp.zeros_like(lse_ref)
        weights_ref[...] = jnp.zeros_like(weights_ref)
        for part, x_ref in enumerate(x_refs):
            top = 0
            if parts == 2:
                top = pl.multiple_of((tp_index[0] if part == 0 else 1 - tp_index[0]) * width, 16)
            for i in range(cap):
                x_all[pl.ds(top, width), i * nlen : (i + 1) * nlen] = x_ref[i]

        def first(n):
            project(n, wk_first, k_even)
            project(n, wv_first, v_even)

        over_slots(first)

    def work(k_now, v_now, k_later, v_later):
        def body(n):
            between = [
                lambda: project(n, wk_next, k_later),
                lambda: project(n, wv_next, v_later),
            ]
            attend(n, k_now, v_now, between)

        over_slots(body)

    def finish(k_now, v_now):
        over_slots(lambda n: attend(n, k_now, v_now, [lambda: None] * 2))

    if steps > 1:
        pl.when((step < steps - 1) & (step % 2 == 0))(lambda: work(k_even, v_even, k_odd, v_odd))
    if steps > 2:
        pl.when((step < steps - 1) & (step % 2 == 1))(lambda: work(k_odd, v_odd, k_even, v_even))
    ends = (k_even, v_even) if steps % 2 == 1 else (k_odd, v_odd)
    pl.when(step == steps - 1)(lambda: finish(*ends))


def attend_part(tp_index, spans, blocks, windows, weights, part_index, slots, held):
    parts, cap = len(blocks), spans.shape[0]
    width, nlen = blocks[0].shape[1:]
    features = width * parts
    columns = 2 * PAIR
    steps = windows.shape[-1] // columns

    in_specs = [pl.BlockSpec(x.shape, lambda t, *_: (0, 0, 0)) for x in blocks]
    in_specs += [pl.BlockSpec((windows.shape[0], SPAN, columns), lambda t, *_: (0, 0, t))]
    operands = list(blocks) + [windows]
    for weight in weights:
        in_specs += [
            pl.BlockSpec((columns, features), lambda t, *_: (0, 0)),
            pl.BlockSpec((columns, features), lambda t, *_: (jnp.minimum(t + 1, steps - 1), 0)),
        ]
        operands += [weight] * 2
    aliases = {}
    if held is not None:
        in_specs += [pl.BlockSpec(memory_space=pl.ANY)] * 2
        aliases = {2 + len(operands): 0, 3 + len(operands): 1}
        operands += list(held)
    kv = pltpu.VMEM((columns, cap * nlen), jnp.bfloat16)

    def body(*refs):
        attend_kernel(cap, parts, steps, *refs)

    return pl.pallas_call(
        body,
        grid_spec=pltpu.PrefetchScalarGridSpec(
            num_scalar_prefetch=2,
            grid=(steps,),
            in_specs=in_specs,
            out_specs=[
                pl.BlockSpec((cap, SPAN, columns), lambda t, *_: (part_index, 0, t)),
                pl.BlockSpec((cap, SPAN, LANES), lambda t, *_: (part_index, 0, 0)),
            ],
            scratch_shapes=[
                pltpu.VMEM((features, cap * nlen), jnp.bfloat16),
                pltpu.VMEM((2, 4 * SPAN, 2 * nlen), jnp.bfloat16),
                kv, kv, kv, kv,
            ],
        ),
        out_shape=[
            jax.ShapeDtypeStruct((slots,) + windows.shape[1:], jnp.bfloat16),
            jax.ShapeDtypeStruct((slots, SPAN, LANES), jnp.float32),
        ],
        input_output_aliases=aliases,
        compiler_params=pltpu.CompilerParams(vmem_limit_bytes=VMEM_LIMIT),
        name="attend_part",
    )(tp_index, spans, *operands)


def spread_matrix(columns):
    per = LANES // 8
    row = lax.broadcasted_iota(jnp.int32, (4 * per, columns), 0)
    head = lax.broadcasted_iota(jnp.int32, (4 * per, columns), 1) // HDIM
    own = 2 * (row % per) + (row // per) % 2
    return jnp.where(head == own, 1.0, 0.0).astype(jnp.bfloat16)


def first_shares(l0, l1):
    largest = jnp.maximum(l0, l1)
    e0, e1 = jnp.exp(l0 - largest), jnp.exp(l1 - largest)
    share = e0 / (e0 + e1)
    high = share.astype(jnp.bfloat16).astype(jnp.float32)
    low = pltpu.roll(share - high, LANES // 4, 1)
    lanes = lax.broadcasted_iota(jnp.int32, share.shape, 1)
    return jnp.where(lanes < LANES // 4, high, low).astype(jnp.bfloat16)[:, : LANES // 2]


def mixed(p0, p1, shares, spread, cols):
    share = jnp.dot(shares, spread[:, cols], preferred_element_type=jnp.float32)
    return p0[0, :, cols].astype(jnp.float32) * share + p1[0, :, cols].astype(jnp.float32) * (
        1.0 - share
    )


def mix_last_kernel(places, p0, p1, l0, l1, out_ref, spread):
    spread[...] = spread_matrix(out_ref.shape[-1])
    shares = first_shares(l0[0], l1[0])
    for pair in range(out_ref.shape[-1] // PAIR):
        cols = slice(pair * PAIR, (pair + 1) * PAIR)
        out_ref[:, cols] = mixed(p0, p1, shares, spread, cols).astype(jnp.bfloat16)


def mix_kernel(places, *refs):
    ins, (out_ref, before, spread) = refs[:-3], refs[-3:]
    tile = 16
    late = lax.broadcasted_iota(jnp.int32, (tile, PAIR), 0) == tile - 1

    @pl.when(pl.program_id(0) == 0)
    def _():
        spread[...] = spread_matrix(out_ref.shape[-1])

    for n in range(len(ins) // 4):
        p0, p1, l0, l1 = ins[4 * n : 4 * n + 4]
        shares = first_shares(l0[0], l1[0])
        top = n * SPAN
        cut = top + SPAN - tile
        out_ref[top:cut, :] = before[: SPAN - tile, :]
        for pair in range(out_ref.shape[-1] // PAIR):
            cols = slice(pair * PAIR, (pair + 1) * PAIR)
            result = mixed(p0, p1, shares, spread, cols)
            out_ref[cut : cut + tile, cols] = jnp.where(
                late, result[SPAN - tile :], before[SPAN - tile :, cols].astype(jnp.float32)
            ).astype(jnp.bfloat16)
            before[:, cols] = result.astype(jnp.bfloat16)


def mix_specs(partials, log_totals, span_of):
    def place(j, shape):
        return pl.BlockSpec((1,) + shape, lambda k, places: (places[2 * span_of(k) + j], 0, 0))

    rows, stats = partials.shape[1:], log_totals.shape[1:]
    return [place(0, rows), place(1, rows), place(0, stats), place(1, stats)]


def mix_last(places, partials, log_totals, span_count):
    columns = partials.shape[-1]
    return pl.pallas_call(
        mix_last_kernel,
        grid_spec=pltpu.PrefetchScalarGridSpec(
            num_scalar_prefetch=1,
            grid=(1,),
            in_specs=mix_specs(partials, log_totals, lambda k: span_count - 1),
            out_specs=pl.BlockSpec((SPAN, columns), lambda k, places: (0, 0)),
            scratch_shapes=[pltpu.VMEM((LANES // 2, columns), jnp.bfloat16)],
        ),
        out_shape=jax.ShapeDtypeStruct((SPAN, columns), jnp.bfloat16),
        name="mix_last",
    )(places, partials, partials, log_totals, log_totals)


def mix(places, partials, log_totals, span_count):
    columns = partials.shape[-1]
    per = 4
    in_specs = []
    for n in range(per):
        in_specs += mix_specs(partials, log_totals, lambda k, n=n: per * k + n)
    return pl.pallas_call(
        mix_kernel,
        grid_spec=pltpu.PrefetchScalarGridSpec(
            num_scalar_prefetch=1,
            grid=(span_count // per,),
            in_specs=in_specs,
            out_specs=pl.BlockSpec((per * SPAN, columns), lambda k, places: (k, 0)),
            scratch_shapes=[
                pltpu.VMEM((SPAN, columns), jnp.bfloat16),
                pltpu.VMEM((LANES // 2, columns), jnp.bfloat16),
            ],
        ),
        out_shape=jax.ShapeDtypeStruct((span_count * SPAN, columns), jnp.bfloat16),
        compiler_params=pltpu.CompilerParams(vmem_limit_bytes=VMEM_LIMIT),
        name="mix",
    )(places, *([partials, partials, log_totals, log_totals] * per))


def head_kernel(carried, rows, out_ref):
    early = lax.broadcasted_iota(jnp.int32, out_ref.shape, 0) < SPAN - 1
    out_ref[...] = jnp.where(
        early, carried[...].astype(jnp.float32), rows[...].astype(jnp.float32)
    ).astype(jnp.bfloat16)


def with_head(carried, mixed_rows):
    spec = pl.BlockSpec((SPAN, mixed_rows.shape[-1]), lambda k: (0, 0))
    return pl.pallas_call(
        head_kernel,
        grid=(1,),
        in_specs=[spec, spec],
        out_specs=spec,
        out_shape=jax.ShapeDtypeStruct(mixed_rows.shape, mixed_rows.dtype),
        input_output_aliases={1: 0},
        name="with_head",
    )(carried, mixed_rows)


def after(values, *others):
    return lax.optimization_barrier((values, others))[0]


def shards(queries, neighbours, key_weight, value_weight, neighbour_ids):
    span_count = neighbour_ids.shape[0]
    seq_count, tp_count = lax.axis_size("seq"), lax.axis_size("tp")
    block_count = neighbours.shape[0]
    wants = 2 * span_count
    ranks = (wants + seq_count - 1) // seq_count
    outer = seq_count // INNER
    slots = seq_count * ranks
    own_index = lax.axis_index("seq")
    tp_index = lax.axis_index("tp").astype(jnp.int32).reshape(1)

    own_ids = neighbour_ids.reshape(wants)
    group_ids = jnp.stack([own_ids] + [swapped(own_ids, "seq", k) for k in range(1, INNER)])
    incoming = passed_along(queries[:SPAN], "seq", -1)

    def all_features(part):
        if tp_count == 2:
            return [part, swapped(part, "tp", 1)]
        return [lax.all_gather(part, "tp", axis=1, tiled=True)]

    group_sources = group_ids // block_count
    group_ranks = slot_ranks(group_sources)
    part_sources = own_index ^ (INNER * jnp.arange(outer))
    hit = (group_sources[None, :, None, :] == part_sources[:, None, None, None]) & (
        group_ranks[None, :, None, :] == jnp.arange(ranks)[None, None, :, None]
    )
    table = jnp.sum(jnp.where(hit, (group_ids % block_count)[None, :, None, :], 0), axis=-1)
    table = table.astype(jnp.int32)

    own_sources = own_ids // block_count
    places = ((own_sources ^ own_index) * ranks + slot_ranks(own_sources)).astype(jnp.int32)
    order = jnp.arange(wants)
    spans = jnp.sum(
        jnp.where(places[None, :] == jnp.arange(slots)[:, None], order[None, :] // 2, 0), axis=1
    ).astype(jnp.int32)
    spans = spans.reshape(outer, INNER * ranks)

    def along(x, offset, senders):
        pairs = [(i, i ^ offset) for i in range(seq_count) if i // INNER in senders]
        return lax.ppermute(x, "seq", pairs)

    first = jnp.zeros((1,), jnp.int32)
    held_parts = [([neighbours], first)]
    near = swapped(neighbours, "seq", INNER)
    if outer == 4:
        across = along(neighbours, 3 * INNER, (1, 2))

    def fetch(j, *others):
        sources, which = held_parts[j]
        picked = pick_blocks(which, after(table[j], *others), sources)
        wanted = [picked[0]] + [swapped(picked[k], "seq", k) for k in range(1, INNER)]
        return picked, jnp.concatenate(wanted, axis=0)

    picked, wanted = fetch(0)
    weights = tuple(after(w, picked).T for w in (key_weight, value_weight))

    if outer == 4:
        near, across = after((near, across), weights)
        outer_index = own_index // INNER
        inside = ((outer_index == 1) | (outer_index == 2)).astype(jnp.int32).reshape(1)
        second = along(near, 3 * INNER, (1, 2))
        outward = along(across, INNER, (1, 2))
        third = along(second, INNER, (1, 2))
        held_parts += [([near], first), ([outward, second], inside), ([third, across], inside)]
    else:
        held_parts.append(([near], first))
        for j in range(2, outer):
            low = j & -j
            part = swapped(held_parts[j ^ low][0][0], "seq", INNER * low)
            held_parts.append(([part], first))

    def attend(j, blocks, held, *others):
        return attend_part(
            tp_index, after(spans[j], *others), blocks, windows, weights, j, slots, held
        )

    held = None
    blocks = [all_features(wanted)]
    picked, wanted = fetch(1, wanted)
    windows = span_windows(after(queries, picked), incoming, span_count)
    for j in range(2, outer):
        blocks.append(all_features(wanted))
        picked, wanted_next = fetch(j, windows if held is None else held)
        held = attend(j - 2, blocks[j - 2], held, picked, wanted)
        wanted = wanted_next
    blocks.append(all_features(wanted))
    held = attend(outer - 2, blocks[outer - 2], held, wanted)
    held = attend(outer - 1, blocks[outer - 1], held)

    partials, log_totals = held
    last = mix_last(places, partials, log_totals, span_count)
    carried = passed_along(last, "seq", 1)
    rows = mix(places, partials, log_totals, span_count)
    return with_head(carried, rows)


def solution(mesh):
    in_specs = (P("seq", "tp"), P("seq", "tp", None), P(None, "tp"), P(None, "tp"), P("seq", None))
    out_specs = P("seq", "tp")
    return jax.shard_map(shards, mesh=mesh, in_specs=in_specs, out_specs=out_specs, check_vma=False)
```

time: 233 us -> 197 us (0.85)
  starting transfers between devices: 62.2 us -> 35 us
  waiting for transfers between devices: 44.8 us -> 20.4 us
  local copies, waits for them, and re-layouts: 9.91 us -> 24.2 us
  other arithmetic: 4.01 us -> 0.88 us
  Pallas kernels: 111 us -> 114 us
    ppermute x22 -> x20, starting transfers between devices: 55.8 us -> 25.2 us  [swapped(): return lax.ppermute(x, axis, [(i, i ^ offset) for i in range(peers)])]
    ppermute x22 -> x20, waiting for transfers between devices: 40.7 us -> 17 us  [swapped(): return lax.ppermute(x, axis, [(i, i ^ offset) for i in range(peers)])]
    optimization_barrier x0 -> x6, local copies, waits for them, and re-layouts: none -> 14.9 us  [after(): return lax.optimization_barrier((values, others))[0]]
    pallas_call x4, Pallas kernels: 71.9 us -> 85.1 us  [attend_part(): pl.pallas_call(body, grid_spec=pltpu.PrefetchScalarGridSpec(num_scalar_pr...]
    pallas_call x1, Pallas kernels: 11.6 us -> 4.95 us  [span_windows(): pl.pallas_call(windows_kernel, grid=(steps,), in_specs=[pl.BlockSpec((per...]
    ppermute x0 -> x4, starting transfers between devices: none -> 5.06 us  [along(): return lax.ppermute(x, 'seq', pairs)]
    ppermute x2, waiting for transfers between devices: 4.15 us -> 0.01 us  [passed_along(): return lax.ppermute(x, axis, pairs)]
    ppermute x0 -> x4, waiting for transfers between devices: none -> 3.37 us  [along(): return lax.ppermute(x, 'seq', pairs)]
  transfers between devices with their start and end apart: 24 -> 26, of which waited for: 7 -> 5; matrix products, arithmetic and copies ran while one was open for 4% -> 11% of each run, Pallas kernels for 38% -> 45%
where the time goes in v3:
time: 197 us; the launch traced here: 195 us
  Pallas kernels  114 us (58%)
  starting transfers between devices  35 us (18%)
  local copies, waits for them, and re-layouts  24.2 us (12%)
  waiting for transfers between devices  20.4 us (10%)
    pallas_call x4, Pallas kernels, attend_part(): pl.pallas_call(body, grid_spec=pltpu.PrefetchScalarGridSpec(num_scalar_pr...  85.1 us
    ppermute x20, starting transfers between devices, swapped(): return lax.ppermute(x, axis, [(i, i ^ offset) for i in range(peers)])  25.2 us
    ppermute x20, waiting for transfers between devices, swapped(): return lax.ppermute(x, axis, [(i, i ^ offset) for i in range(peers)])  17 us
    optimization_barrier x6, local copies, waits for them, and re-layouts, after(): return lax.optimization_barrier((values, others))[0]  14.9 us
    pallas_call x4, Pallas kernels, pick_blocks(): pl.pallas_call(body, grid_spec=pltpu.PrefetchScalarGridSpec(num_scalar_pr...  11.1 us
    pallas_call x1, Pallas kernels, mix(): pl.pallas_call(mix_kernel, grid_spec=pltpu.PrefetchScalarGridSpec(num_sca...  8.22 us
    unnamed x43, local copies, waits for them, and re-layouts  7.4 us
    ppermute x4, starting transfers between devices, along(): return lax.ppermute(x, 'seq', pairs)  5.06 us
  transfers between devices with their start and end apart: 26, of which 5 were waited for; matrix products, arithmetic and copies ran while one was open for 11% of the time, Pallas kernels for 45%

profile of v3, /device:TPU:1, one launch (start us, length us, event | category | flops | bytes accessed | tf_op | source)
XLA Modules:
  0.0 194.9 jit_solution(15262634844982779196)
XLA Ops:
  1.0 2.7 %collective-permute-start.1 = (s32[32]{0:T(128)S(1)}, s32[32]{0:T(128)S(1)}, u32[]{:S(2)}, u32[]{:S(2)}) collective-permute-start(s32[32]{0:T(128)S(1)} %reshape.606), channel_id=1, source_target_pairs={{0,4},{2,6},{4,0},{6,2},{8,12},{10,14},{12,8},{14,10},{16,20},{18,... | collective-permute-start | bytes 392 | tf_op jit(solution)/shard_map/ppermute | solution.py:24
  3.7 1.7 collective-permute-start.6
  7.4 2.4 %collective-permute-start.8 = (bf16[64,2048]{1,0:T(8,128)(2,1)S(1)}, bf16[64,2048]{1,0:T(8,128)(2,1)S(1)}, u32[]{:S(2)}, u32[]{:S(2)}) collective-permute-start(bf16[64,2048]{1,0:T(8,128)(2,1)S(1)} %slice.37), channel_id=1, source_target_pairs={{2,0},{4,2},{6,4},{8,6},{10,8},{12,10},{14,12},{16,14},{18,16},{20... | collective-permute-start | bytes 786440 | tf_op jit(solution)/shard_map/ppermute | solution.py:19
  11.1 2.7 %pick_blocks.4 = (bf16[2,448,128]{2,1,0:T(8,128)(2,1)}, bf16[2,448,128]{2,1,0:T(8,128)(2,1)}, bf16[2,448,128]{2,1,0:T(8,128)(2,1)}, bf16[2,448,128]{2,1,0:T(8,128)(2,1)}) custom-call(s32[1]{0:T(128)} %constant.76.clone.1.refs_0_, s32[4,2]{1,0:T(4,128)} %copy.31.refs_1_, bf16[8,448,128]{2,1,0:T(8,128)(2,1)} %refs_2_.1), custom_call_target="tpu_custom_call" | custom-call | tf_op jit(solution)/shard_map/pick_blocks/pallas_call | solution.py:107
  13.9 6.0 %copy.33 = bf16[896,2048]{0,1:T(8,128)(2,1)} copy(bf16[896,2048]{1,0:T(8,128)(2,1)} %param.8) | data formatting | bytes 7340032 | tf_op jit(solution)/shard_map/optimization_barrier | solution.py:416
  19.9 6.1 %copy.32 = bf16[896,2048]{0,1:T(8,128)(2,1)} copy(bf16[896,2048]{1,0:T(8,128)(2,1)} %param.7) | data formatting | bytes 7340032 | tf_op jit(solution)/shard_map/optimization_barrier | solution.py:416
  31.3 3.1 %collective-permute-done.4 = bf16[2,448,128]{2,1,0:T(8,128)(2,1)S(1)} collective-permute-done((bf16[2,448,128]{2,1,0:T(8,128)(2,1)}, bf16[2,448,128]{2,1,0:T(8,128)(2,1)S(1)}, u32[]{:S(2)}, u32[]{:S(2)}) %collective-permute-start.4) | collective-permute-done | bytes 229408 | tf_op jit(solution)/shard_map/ppermute | solution.py:24
  35.7 4.6 %collective-permute-done.5 = bf16[2,448,128]{2,1,0:T(8,128)(2,1)S(1)} collective-permute-done((bf16[2,448,128]{2,1,0:T(8,128)(2,1)}, bf16[2,448,128]{2,1,0:T(8,128)(2,1)S(1)}, u32[]{:S(2)}, u32[]{:S(2)}) %collective-permute-start.5) | collective-permute-done | bytes 229408 | tf_op jit(solution)/shard_map/ppermute | solution.py:24
  42.4 2.9 %pick_blocks.5 = (bf16[2,448,128]{2,1,0:T(8,128)(2,1)}, bf16[2,448,128]{2,1,0:T(8,128)(2,1)}, bf16[2,448,128]{2,1,0:T(8,128)(2,1)}, bf16[2,448,128]{2,1,0:T(8,128)(2,1)}) custom-call(s32[1]{0:T(128)} %constant.76.clone.1.refs_0_, s32[4,2]{1,0:T(4,128)} %copy.34.refs_1_, bf16[8,448,128]{2,1,0:T(8,128)(2,1)} %copy-done.5), custom_call_target="tpu_custom_call" | custom-call | tf_op jit(solution)/shard_map/pick_blocks/pallas_call | solution.py:107
  49.0 5.0 %windows.1.refs_4_ = bf16[16,64,2048]{2,1,0:T(8,128)(2,1)} custom-call(bf16[1024,2048]{1,0:T(8,128)(2,1)} %next_ref, bf16[1024,2048]{1,0:T(8,128)(2,1)} %next_ref, bf16[64,2048]{1,0:T(8,128)(2,1)} %copy-done.9), custom_call_target="tpu_custom_call" | custom-call | tf_op jit(solution)/shard_map/windows/pallas_call | solution.py:56
  56.7 3.4 %collective-permute-done.9.refs_2_ = bf16[8,448,128]{2,1,0:T(8,128)(2,1)} collective-permute-done((bf16[8,448,128]{2,1,0:T(8,128)(2,1)S(1)}, bf16[8,448,128]{2,1,0:T(8,128)(2,1)}, u32[]{:S(2)}, u32[]{:S(2)}) %collective-permute-start.9) | collective-permute-done | bytes 917536 | tf_op jit(solution)/shard_map/ppermute | solution.py:458
  60.1 2.7 %pick_blocks.6 = (bf16[2,448,128]{2,1,0:T(8,128)(2,1)}, bf16[2,448,128]{2,1,0:T(8,128)(2,1)}, bf16[2,448,128]{2,1,0:T(8,128)(2,1)}, bf16[2,448,128]{2,1,0:T(8,128)(2,1)}) custom-call(s32[1]{0:T(128)} %bitcast.1.refs_0_, s32[4,2]{1,0:T(4,128)} %copy.35.refs_1_, bf16[8,448,128]{2,1,0:T(8,128)(2,1)} %collective-permute-done.9.refs_2_, ...), custom_call_target="tpu_custom_call" | custom-call | tf_op jit(solution)/shard_map/pick_blocks/pallas_call | solution.py:107
  62.8 6.9 %collective-permute-start.20 = (bf16[2,448,128]{2,1,0:T(8,128)(2,1)}, bf16[2,448,128]{2,1,0:T(8,128)(2,1)S(1)}, u32[]{:S(2)}, u32[]{:S(2)}) collective-permute-start(bf16[2,448,128]{2,1,0:T(8,128)(2,1)} %get-tuple-element.56), channel_id=1, source_target_pairs={{0,2},{2,0},{4,6},{6,4},{8,10},{10,8},{12,14},{14,12},{16,18},{18,... | collective-permute-start | bytes 688136 | tf_op jit(solution)/shard_map/ppermute | solution.py:24
  73.0 21.3 %attend_part.4 = (bf16[32,64,2048]{2,1,0:T(8,128)(2,1)}, f32[32,64,128]{2,1,0:T(8,128)}) custom-call(s32[1]{0:T(128)} %bitcast.refs_0_, s32[8]{0:T(128)} %get-tuple-element.59.refs_1_, bf16[8,448,128]{2,1,0:T(8,128)(2,1)} %copy-done.3, bf16[8,448,128]{2,1,0:T(8,128)(2,1)} %collective-permute-done.14.refs_3_, bf16[16,64,2048]{2,1,0:T(8,128)(2,1)} %windows.1.refs_4_, ...), custom_call_target="tpu_custom_call" | custom-call | tf_op jit(solution)/shard_map/attend_part/pallas_call | solution.py:264
  95.1 2.7 %pick_blocks.7 = (bf16[2,448,128]{2,1,0:T(8,128)(2,1)}, bf16[2,448,128]{2,1,0:T(8,128)(2,1)}, bf16[2,448,128]{2,1,0:T(8,128)(2,1)}, bf16[2,448,128]{2,1,0:T(8,128)(2,1)}) custom-call(s32[1]{0:T(128)} %bitcast.1.refs_0_, s32[4,2]{1,0:T(4,128)} %copy.36.refs_1_, bf16[8,448,128]{2,1,0:T(8,128)(2,1)} %collective-permute-done.15.refs_2_, ...), custom_call_target="tpu_custom_call" | custom-call | tf_op jit(solution)/shard_map/pick_blocks/pallas_call | solution.py:107
  101.7 3.2 %collective-permute-done.17 = bf16[2,448,128]{2,1,0:T(8,128)(2,1)S(1)} collective-permute-done((bf16[2,448,128]{2,1,0:T(8,128)(2,1)}, bf16[2,448,128]{2,1,0:T(8,128)(2,1)S(1)}, u32[]{:S(2)}, u32[]{:S(2)}) %collective-permute-start.17) | collective-permute-done | bytes 229408 | tf_op jit(solution)/shard_map/ppermute | solution.py:24
  104.9 6.1 %collective-permute-done.18 = bf16[2,448,128]{2,1,0:T(8,128)(2,1)S(1)} collective-permute-done((bf16[2,448,128]{2,1,0:T(8,128)(2,1)}, bf16[2,448,128]{2,1,0:T(8,128)(2,1)S(1)}, u32[]{:S(2)}, u32[]{:S(2)}) %collective-permute-start.18) | collective-permute-done | bytes 229408 | tf_op jit(solution)/shard_map/ppermute | solution.py:24
  113.3 21.2 %attend_part.5 = (bf16[32,64,2048]{2,1,0:T(8,128)(2,1)}, f32[32,64,128]{2,1,0:T(8,128)}) custom-call(s32[1]{0:T(128)} %bitcast.refs_0_, s32[8]{0:T(128)} %get-tuple-element.68.refs_1_, bf16[8,448,128]{2,1,0:T(8,128)(2,1)} %copy-done, bf16[8,448,128]{2,1,0:T(8,128)(2,1)} %copy-done.6, ...), custom_call_target="tpu_custom_call", output_to_operand_aliasing={{0}: (9, {}), {1}: (10, {})} | custom-call | tf_op jit(solution)/shard_map/attend_part/pallas_call | solution.py:264
  135.4 21.2 %attend_part.6 = (bf16[32,64,2048]{2,1,0:T(8,128)(2,1)}, f32[32,64,128]{2,1,0:T(8,128)}) custom-call(s32[1]{0:T(128)} %bitcast.refs_0_, s32[8]{0:T(128)} %get-tuple-element.67.refs_1_, bf16[8,448,128]{2,1,0:T(8,128)(2,1)} %copy-done.1, bf16[8,448,128]{2,1,0:T(8,128)(2,1)} %copy-done.7, ...), custom_call_target="tpu_custom_call", output_to_operand_aliasing={{0}: (9, {}), {1}: (10, {})} | custom-call | tf_op jit(solution)/shard_map/attend_part/pallas_call | solution.py:264
  157.6 21.4 %attend_part.7 = (bf16[32,64,2048]{2,1,0:T(8,128)(2,1)}, f32[32,64,128]{2,1,0:T(8,128)}) custom-call(s32[1]{0:T(128)} %bitcast.refs_0_, s32[8]{0:T(128)} %get-tuple-element.84.refs_1_, bf16[8,448,128]{2,1,0:T(8,128)(2,1)} %copy-done.2, bf16[8,448,128]{2,1,0:T(8,128)(2,1)} %copy-done.8, ...), custom_call_target="tpu_custom_call", output_to_operand_aliasing={{0}: (9, {}), {1}: (10, {})} | custom-call | tf_op jit(solution)/shard_map/attend_part/pallas_call | solution.py:264
  179.0 2.8 %mix_last.1 = bf16[64,2048]{1,0:T(8,128)(2,1)} custom-call(s32[32]{0:T(128)} %copy-done.14, bf16[32,64,2048]{2,1,0:T(8,128)(2,1)} %get-tuple-element.73.p0.p1.refs_0_.refs_1_.refs_4_.refs_5_.refs_8_.refs_9_.refs_12_.refs_13_, bf16[32,64,2048]{2,1,0:T(8,128)(2,1)} %get-tuple-element.73.p0.p1.refs_0_.refs_1_.refs_4_.refs_5_.refs_8_.refs_9_.refs_12_.refs_13_, ...), custom_call_target="tpu_custom_call" | custom-call | tf_op jit(solution)/shard_map/mix_last/pallas_call | solution.py:357
  181.7 2.4 %collective-permute-start.25 = (bf16[64,2048]{1,0:T(8,128)(2,1)}, bf16[64,2048]{1,0:T(8,128)(2,1)S(1)}, u32[]{:S(2)}, u32[]{:S(2)}) collective-permute-start(bf16[64,2048]{1,0:T(8,128)(2,1)} %mix_last.1), channel_id=1, source_target_pairs={{0,2},{2,4},{4,6},{6,8},{8,10},{10,12},{12,14},{14,16},{16,18},{18... | collective-permute-start | bytes 786440 | tf_op jit(solution)/shard_map/ppermute | solution.py:19
  184.2 8.2 %mix.1.rows = bf16[1024,2048]{1,0:T(8,128)(2,1)} custom-call(s32[32]{0:T(128)} %copy-done.14, bf16[32,64,2048]{2,1,0:T(8,128)(2,1)} %get-tuple-element.73.p0.p1.refs_0_.refs_1_.refs_4_.refs_5_.refs_8_.refs_9_.refs_12_.refs_13_, bf16[32,64,2048]{2,1,0:T(8,128)(2,1)} %get-tuple-element.73.p0.p1.refs_0_.refs_1_.refs_4_.refs_5_.refs_8_.refs_9_.refs_12_.refs_13_, ...), custom_call_target="tpu_custom_call" | custom-call | tf_op jit(solution)/shard_map/mix/pallas_call | solution.py:377
  193.1 1.8 with_head.1
  (110 shorter events, 32.0 us)
Async XLA Ops:
  0.8 6.6 %collective-permute-start = (s32[32]{0:T(128)S(1)}, s32[32]{0:T(128)S(1)}, u32[]{:S(2)}, u32[]{:S(2)}) collective-permute-start(s32[32]{0:T(128)S(1)} %reshape.606), channel_id=1, source_target_pairs={{0,2},{2,0},{4,6},{6,4},{8,10},{10,8},{12,14},{14,12},{16,18},{18,... | collective-permute-start | bytes 392 | tf_op jit(solution)/shard_map/ppermute | solution.py:24
  1.0 8.8 %collective-permute-start.1 = (s32[32]{0:T(128)S(1)}, s32[32]{0:T(128)S(1)}, u32[]{:S(2)}, u32[]{:S(2)}) collective-permute-start(s32[32]{0:T(128)S(1)} %reshape.606), channel_id=1, source_target_pairs={{0,4},{2,6},{4,0},{6,2},{8,12},{10,14},{12,8},{14,10},{16,20},{18,... | collective-permute-start | bytes 392 | tf_op jit(solution)/shard_map/ppermute | solution.py:24
  3.7 22.4 %collective-permute-start.6 = (bf16[8,448,128]{2,1,0:T(8,128)(2,1)}, bf16[8,448,128]{2,1,0:T(8,128)(2,1)S(1)}, u32[]{:S(2)}, u32[]{:S(2)}) collective-permute-start(bf16[8,448,128]{2,1,0:T(8,128)(2,1)} %refs_2_.1), channel_id=1, source_target_pairs={{0,8},{2,10},{4,12},{6,14},{8,0},{10,2},{12,4},{14,6},{16,24},{18,... | collective-permute-start | bytes 2752520 | tf_op jit(solution)/shard_map/ppermute | solution.py:24
  5.4 20.6 %collective-permute-start.7 = (bf16[8,448,128]{2,1,0:T(8,128)(2,1)}, bf16[8,448,128]{2,1,0:T(8,128)(2,1)S(1)}, u32[]{:S(2)}, u32[]{:S(2)}) collective-permute-start(bf16[8,448,128]{2,1,0:T(8,128)(2,1)} %refs_2_.1), channel_id=1, source_target_pairs={{8,16},{10,18},{12,20},{14,22},{16,8},{18,10},{20,12},{22,14},{9,1... | collective-permute-start | bytes 2752520 | tf_op jit(solution)/shard_map/ppermute | solution.py:458
  7.4 40.3 %collective-permute-start.8 = (bf16[64,2048]{1,0:T(8,128)(2,1)S(1)}, bf16[64,2048]{1,0:T(8,128)(2,1)S(1)}, u32[]{:S(2)}, u32[]{:S(2)}) collective-permute-start(bf16[64,2048]{1,0:T(8,128)(2,1)S(1)} %slice.37), channel_id=1, source_target_pairs={{2,0},{4,2},{6,4},{8,6},{10,8},{12,10},{14,12},{16,14},{18,16},{20... | collective-permute-start | bytes 786440 | tf_op jit(solution)/shard_map/ppermute | solution.py:19
  13.8 16.5 %collective-permute-start.3 = (bf16[2,448,128]{2,1,0:T(8,128)(2,1)}, bf16[2,448,128]{2,1,0:T(8,128)(2,1)}, u32[]{:S(2)}, u32[]{:S(2)}) collective-permute-start(bf16[2,448,128]{2,1,0:T(8,128)(2,1)} %get-tuple-element.41), channel_id=1, source_target_pairs={{0,2},{2,0},{4,6},{6,4},{8,10},{10,8},{12,14},{14,12},{16,18},{18,... | collective-permute-start | bytes 688136 | tf_op jit(solution)/shard_map/ppermute | solution.py:24
  26.1 19.5 %collective-permute-start.10 = (bf16[8,448,128]{2,1,0:T(8,128)(2,1)S(1)}, bf16[8,448,128]{2,1,0:T(8,128)(2,1)}, u32[]{:S(2)}, u32[]{:S(2)}) collective-permute-start(bf16[8,448,128]{2,1,0:T(8,128)(2,1)S(1)} %collective-permute-done.6.refs_2_), channel_id=1, source_target_pairs={{8,16},{10,18},{12,20},{14,22},{16,8},{18,10},{20,12},{22,14},{9,1... | collective-permute-start | bytes 2752520 | tf_op jit(solution)/shard_map/ppermute | solution.py:458
  27.7 6.6 %collective-permute-start.4 = (bf16[2,448,128]{2,1,0:T(8,128)(2,1)}, bf16[2,448,128]{2,1,0:T(8,128)(2,1)S(1)}, u32[]{:S(2)}, u32[]{:S(2)}) collective-permute-start(bf16[2,448,128]{2,1,0:T(8,128)(2,1)} %get-tuple-element.42), channel_id=1, source_target_pairs={{0,4},{2,6},{4,0},{6,2},{8,12},{10,14},{12,8},{14,10},{16,20},{18,... | collective-permute-start | bytes 688136 | tf_op jit(solution)/shard_map/ppermute | solution.py:24
  29.3 11.0 %collective-permute-start.5 = (bf16[2,448,128]{2,1,0:T(8,128)(2,1)}, bf16[2,448,128]{2,1,0:T(8,128)(2,1)S(1)}, u32[]{:S(2)}, u32[]{:S(2)}) collective-permute-start(bf16[2,448,128]{2,1,0:T(8,128)(2,1)} %get-tuple-element.43), channel_id=1, source_target_pairs={{0,6},{2,4},{4,2},{6,0},{8,14},{10,12},{12,10},{14,8},{16,22},{18,... | collective-permute-start | bytes 688136 | tf_op jit(solution)/shard_map/ppermute | solution.py:24
  34.4 25.7 %collective-permute-start.9 = (bf16[8,448,128]{2,1,0:T(8,128)(2,1)S(1)}, bf16[8,448,128]{2,1,0:T(8,128)(2,1)}, u32[]{:S(2)}, u32[]{:S(2)}) collective-permute-start(bf16[8,448,128]{2,1,0:T(8,128)(2,1)S(1)} %collective-permute-done.7.refs_3_), channel_id=1, source_target_pairs={{8,0},{10,2},{12,4},{14,6},{16,24},{18,26},{20,28},{22,30},{9,1},{... | collective-permute-start | bytes 2752520 | tf_op jit(solution)/shard_map/ppermute | solution.py:458
  40.3 31.9 %collective-permute-start.14 = (bf16[8,448,128]{2,1,0:T(8,128)(2,1)S(1)}, bf16[8,448,128]{2,1,0:T(8,128)(2,1)}, u32[]{:S(2)}, u32[]{:S(2)}) collective-permute-start(bf16[8,448,128]{2,1,0:T(8,128)(2,1)S(1)} %constant_dynamic-update-slice_fusion.refs_2_), channel_id=1, source_target_pairs={{0,1},{1,0},{2,3},{3,2},{4,5},{5,4},{6,7},{7,6},{8,9},{9,8},{10,11... | collective-permute-start | bytes 2752520 | tf_op jit(solution)/shard_map/ppermute | solution.py:24
  45.3 9.3 %collective-permute-start.11 = (bf16[2,448,128]{2,1,0:T(8,128)(2,1)}, bf16[2,448,128]{2,1,0:T(8,128)(2,1)S(1)}, u32[]{:S(2)}, u32[]{:S(2)}) collective-permute-start(bf16[2,448,128]{2,1,0:T(8,128)(2,1)} %get-tuple-element.49), channel_id=1, source_target_pairs={{0,2},{2,0},{4,6},{6,4},{8,10},{10,8},{12,14},{14,12},{16,18},{18,... | collective-permute-start | bytes 688136 | tf_op jit(solution)/shard_map/ppermute | solution.py:24
  45.6 49.5 %collective-permute-start.15 = (bf16[8,448,128]{2,1,0:T(8,128)(2,1)}, bf16[8,448,128]{2,1,0:T(8,128)(2,1)}, u32[]{:S(2)}, u32[]{:S(2)}) collective-permute-start(bf16[8,448,128]{2,1,0:T(8,128)(2,1)} %collective-permute-done.10.refs_3_), channel_id=1, source_target_pairs={{8,0},{10,2},{12,4},{14,6},{16,24},{18,26},{20,28},{22,30},{9,1},{... | collective-permute-start | bytes 2752520 | tf_op jit(solution)/shard_map/ppermute | solution.py:458
  47.7 8.0 %collective-permute-start.12 = (bf16[2,448,128]{2,1,0:T(8,128)(2,1)}, bf16[2,448,128]{2,1,0:T(8,128)(2,1)}, u32[]{:S(2)}, u32[]{:S(2)}) collective-permute-start(bf16[2,448,128]{2,1,0:T(8,128)(2,1)} %get-tuple-element.50), channel_id=1, source_target_pairs={{0,4},{2,6},{4,0},{6,2},{8,12},{10,14},{12,8},{14,10},{16,20},{18,... | collective-permute-start | bytes 688136 | tf_op jit(solution)/shard_map/ppermute | solution.py:24
  54.6 15.1 %collective-permute-start.13 = (bf16[2,448,128]{2,1,0:T(8,128)(2,1)}, bf16[2,448,128]{2,1,0:T(8,128)(2,1)S(1)}, u32[]{:S(2)}, u32[]{:S(2)}) collective-permute-start(bf16[2,448,128]{2,1,0:T(8,128)(2,1)} %get-tuple-element.51), channel_id=1, source_target_pairs={{0,6},{2,4},{4,2},{6,0},{8,14},{10,12},{12,10},{14,8},{16,22},{18,... | collective-permute-start | bytes 688136 | tf_op jit(solution)/shard_map/ppermute | solution.py:24
  62.8 32.1 %collective-permute-start.20 = (bf16[2,448,128]{2,1,0:T(8,128)(2,1)}, bf16[2,448,128]{2,1,0:T(8,128)(2,1)S(1)}, u32[]{:S(2)}, u32[]{:S(2)}) collective-permute-start(bf16[2,448,128]{2,1,0:T(8,128)(2,1)} %get-tuple-element.56), channel_id=1, source_target_pairs={{0,2},{2,0},{4,6},{6,4},{8,10},{10,8},{12,14},{14,12},{16,18},{18,... | collective-permute-start | bytes 688136 | tf_op jit(solution)/shard_map/ppermute | solution.py:24
  69.7 42.6 %collective-permute-start.24 = (bf16[8,448,128]{2,1,0:T(8,128)(2,1)S(1)}, bf16[8,448,128]{2,1,0:T(8,128)(2,1)S(1)}, u32[]{:S(2)}, u32[]{:S(2)}) collective-permute-start(bf16[8,448,128]{2,1,0:T(8,128)(2,1)S(1)} %constant_dynamic-update-slice_fusion.4.refs_2_), channel_id=1, source_target_pairs={{0,1},{1,0},{2,3},{3,2},{4,5},{5,4},{6,7},{7,6},{8,9},{9,8},{10,11... | collective-permute-start | bytes 2752520 | tf_op jit(solution)/shard_map/ppermute | solution.py:24
  71.0 24.0 %collective-permute-start.21 = (bf16[2,448,128]{2,1,0:T(8,128)(2,1)}, bf16[2,448,128]{2,1,0:T(8,128)(2,1)S(1)}, u32[]{:S(2)}, u32[]{:S(2)}) collective-permute-start(bf16[2,448,128]{2,1,0:T(8,128)(2,1)} %get-tuple-element.57), channel_id=1, source_target_pairs={{0,4},{2,6},{4,0},{6,2},{8,12},{10,14},{12,8},{14,10},{16,20},{18,... | collective-permute-start | bytes 688136 | tf_op jit(solution)/shard_map/ppermute | solution.py:24
  72.3 25.7 %collective-permute-start.22 = (bf16[2,448,128]{2,1,0:T(8,128)(2,1)}, bf16[2,448,128]{2,1,0:T(8,128)(2,1)S(1)}, u32[]{:S(2)}, u32[]{:S(2)}) collective-permute-start(bf16[2,448,128]{2,1,0:T(8,128)(2,1)} %get-tuple-element.58), channel_id=1, source_target_pairs={{0,6},{2,4},{4,2},{6,0},{8,14},{10,12},{12,10},{14,8},{16,22},{18,... | collective-permute-start | bytes 688136 | tf_op jit(solution)/shard_map/ppermute | solution.py:24
  98.0 36.5 %collective-permute-start.23 = (bf16[8,448,128]{2,1,0:T(8,128)(2,1)S(1)}, bf16[8,448,128]{2,1,0:T(8,128)(2,1)S(1)}, u32[]{:S(2)}, u32[]{:S(2)}) collective-permute-start(bf16[8,448,128]{2,1,0:T(8,128)(2,1)S(1)} %constant_dynamic-update-slice_fusion.12.refs_2_), channel_id=1, source_target_pairs={{0,1},{1,0},{2,3},{3,2},{4,5},{5,4},{6,7},{7,6},{8,9},{9,8},{10,11... | collective-permute-start | bytes 2752520 | tf_op jit(solution)/shard_map/ppermute | solution.py:24
  98.3 6.6 %collective-permute-start.17 = (bf16[2,448,128]{2,1,0:T(8,128)(2,1)}, bf16[2,448,128]{2,1,0:T(8,128)(2,1)S(1)}, u32[]{:S(2)}, u32[]{:S(2)}) collective-permute-start(bf16[2,448,128]{2,1,0:T(8,128)(2,1)} %get-tuple-element.65), channel_id=1, source_target_pairs={{0,4},{2,6},{4,0},{6,2},{8,12},{10,14},{12,8},{14,10},{16,20},{18,... | collective-permute-start | bytes 688136 | tf_op jit(solution)/shard_map/ppermute | solution.py:24
  99.5 11.5 %collective-permute-start.18 = (bf16[2,448,128]{2,1,0:T(8,128)(2,1)}, bf16[2,448,128]{2,1,0:T(8,128)(2,1)S(1)}, u32[]{:S(2)}, u32[]{:S(2)}) collective-permute-start(bf16[2,448,128]{2,1,0:T(8,128)(2,1)} %get-tuple-element.66), channel_id=1, source_target_pairs={{0,6},{2,4},{4,2},{6,0},{8,14},{10,12},{12,10},{14,8},{16,22},{18,... | collective-permute-start | bytes 688136 | tf_op jit(solution)/shard_map/ppermute | solution.py:24
  111.1 45.5 %collective-permute-start.19 = (bf16[8,448,128]{2,1,0:T(8,128)(2,1)S(1)}, bf16[8,448,128]{2,1,0:T(8,128)(2,1)S(1)}, u32[]{:S(2)}, u32[]{:S(2)}) collective-permute-start(bf16[8,448,128]{2,1,0:T(8,128)(2,1)S(1)} %constant_dynamic-update-slice_fusion.8.refs_2_), channel_id=1, source_target_pairs={{0,1},{1,0},{2,3},{3,2},{4,5},{5,4},{6,7},{7,6},{8,9},{9,8},{10,11... | collective-permute-start | bytes 2752520 | tf_op jit(solution)/shard_map/ppermute | solution.py:24
  181.7 10.7 %collective-permute-start.25 = (bf16[64,2048]{1,0:T(8,128)(2,1)}, bf16[64,2048]{1,0:T(8,128)(2,1)S(1)}, u32[]{:S(2)}, u32[]{:S(2)}) collective-permute-start(bf16[64,2048]{1,0:T(8,128)(2,1)} %mix_last.1), channel_id=1, source_target_pairs={{0,2},{2,4},{4,6},{6,8},{8,10},{10,12},{12,14},{14,16},{16,18},{18... | collective-permute-start | bytes 786440 | tf_op jit(solution)/shard_map/ppermute | solution.py:19
  (17 other events, 222.4 us)

commit v4 on v3

--- a/solution.py
+++ b/solution.py
@@ -137,7 +137,7 @@
     rows = 2 * SPAN
 
     def two_slots(n):
-        return pl.ds(pl.multiple_of(n * 2 * nlen, 2 * nlen), 2 * nlen)
+        return pl.ds(n * 2 * nlen, 2 * nlen)
 
     def project(n, w_ref, out):
         out[:, two_slots(n)] = jnp.dot(
@@ -191,11 +191,8 @@
                 ).astype(jnp.bfloat16)
 
     def over_slots(body):
-        def one(n, carry):
+        for n in range(cap // 2):
             body(n)
-            return carry
-
-        lax.fori_loop(0, cap // 2, one, 0)
 
     @pl.when(step == 0)
     def _():
@@ -429,7 +426,6 @@
 
     own_ids = neighbour_ids.reshape(wants)
     group_ids = jnp.stack([own_ids] + [swapped(own_ids, "seq", k) for k in range(1, INNER)])
-    incoming = passed_along(queries[:SPAN], "seq", -1)
 
     def all_features(part):
         if tp_count == 2:
@@ -459,9 +455,6 @@
 
     first = jnp.zeros((1,), jnp.int32)
     held_parts = [([neighbours], first)]
-    near = swapped(neighbours, "seq", INNER)
-    if outer == 4:
-        across = along(neighbours, 3 * INNER, (1, 2))
 
     def fetch(j, *others):
         sources, which = held_parts[j]
@@ -470,6 +463,11 @@
         return picked, jnp.concatenate(wanted, axis=0)
 
     picked, wanted = fetch(0)
+    own_blocks, edge = after((neighbours, queries[:SPAN]), picked)
+    near = swapped(own_blocks, "seq", INNER)
+    if outer == 4:
+        across = along(own_blocks, 3 * INNER, (1, 2))
+    incoming = passed_along(edge, "seq", -1)
     weights = tuple(after(w, picked).T for w in (key_weight, value_weight))
 
     if outer == 4:

time: 197 us -> 211 us (1.071)
  starting transfers between devices: 35 us -> 50.7 us
  Pallas kernels: 114 us -> 103 us
  waiting for transfers between devices: 20.4 us -> 28.1 us
    ppermute x20, starting transfers between devices: 25.2 us -> 40.9 us  [swapped(): return lax.ppermute(x, axis, [(i, i ^ offset) for i in range(peers)])]
    ppermute x20, waiting for transfers between devices: 17 us -> 28 us  [swapped(): return lax.ppermute(x, axis, [(i, i ^ offset) for i in range(peers)])]
    pallas_call x4, Pallas kernels: 85.1 us -> 74.2 us  [attend_part(): pl.pallas_call(body, grid_spec=pltpu.PrefetchScalarGridSpec(num_scalar_pr...]
    ppermute x4, waiting for transfers between devices: 3.37 us -> 0.01 us  [along(): return lax.ppermute(x, 'seq', pairs)]
  transfers between devices with their start and end apart: 26 -> 26, of which waited for: 5 -> 7; matrix products, arithmetic and copies ran while one was open for 11% -> 9% of each run, Pallas kernels for 45% -> 37%
where the time goes in v4:
time: 211 us; the launch traced here: 207 us
  Pallas kernels  103 us (49%)
  starting transfers between devices  50.7 us (24%)
  waiting for transfers between devices  28.1 us (13%)
  local copies, waits for them, and re-layouts  24.2 us (11%)
    pallas_call x4, Pallas kernels, attend_part(): pl.pallas_call(body, grid_spec=pltpu.PrefetchScalarGridSpec(num_scalar_pr...  74.2 us
    ppermute x20, starting transfers between devices, swapped(): return lax.ppermute(x, axis, [(i, i ^ offset) for i in range(peers)])  40.9 us
    ppermute x20, waiting for transfers between devices, swapped(): return lax.ppermute(x, axis, [(i, i ^ offset) for i in range(peers)])  28 us
    optimization_barrier x6, local copies, waits for them, and re-layouts, after(): return lax.optimization_barrier((values, others))[0]  14.9 us
    pallas_call x4, Pallas kernels, pick_blocks(): pl.pallas_call(body, grid_spec=pltpu.PrefetchScalarGridSpec(num_scalar_pr...  11 us
    pallas_call x1, Pallas kernels, mix(): pl.pallas_call(mix_kernel, grid_spec=pltpu.PrefetchScalarGridSpec(num_sca...  8.24 us
    unnamed x43, local copies, waits for them, and re-layouts  7.4 us
    ppermute x4, starting transfers between devices, along(): return lax.ppermute(x, 'seq', pairs)  5.41 us
  transfers between devices with their start and end apart: 26, of which 7 were waited for; matrix products, arithmetic and copies ran while one was open for 9% of the time, Pallas kernels for 37%

profile of v4, /device:TPU:1, one launch (start us, length us, event | category | flops | bytes accessed | tf_op | source)
XLA Modules:
  0.0 207.5 jit_solution(11345815601018829379)
XLA Ops:
  1.0 2.7 %collective-permute-start.1 = (s32[32]{0:T(128)S(1)}, s32[32]{0:T(128)S(1)}, u32[]{:S(2)}, u32[]{:S(2)}) collective-permute-start(s32[32]{0:T(128)S(1)} %reshape.606), channel_id=1, source_target_pairs={{0,4},{2,6},{4,0},{6,2},{8,12},{10,14},{12,8},{14,10},{16,20},{18,... | collective-permute-start | bytes 392 | tf_op jit(solution)/shard_map/ppermute | solution.py:24
  7.9 2.8 %pick_blocks.4 = (bf16[2,448,128]{2,1,0:T(8,128)(2,1)}, bf16[2,448,128]{2,1,0:T(8,128)(2,1)}, bf16[2,448,128]{2,1,0:T(8,128)(2,1)}, bf16[2,448,128]{2,1,0:T(8,128)(2,1)}) custom-call(s32[1]{0:T(128)} %constant.76.clone.1.refs_0_, s32[4,2]{1,0:T(4,128)} %copy.31.refs_1_, bf16[8,448,128]{2,1,0:T(8,128)(2,1)} %refs_2_.1), custom_call_target="tpu_custom_call" | custom-call | tf_op jit(solution)/shard_map/pick_blocks/pallas_call | solution.py:107
  13.6 6.0 %copy.33 = bf16[896,2048]{0,1:T(8,128)(2,1)} copy(bf16[896,2048]{1,0:T(8,128)(2,1)} %param.8) | data formatting | bytes 7340032 | tf_op jit(solution)/shard_map/optimization_barrier | solution.py:413
  19.6 6.1 %copy.32 = bf16[896,2048]{0,1:T(8,128)(2,1)} copy(bf16[896,2048]{1,0:T(8,128)(2,1)} %param.7) | data formatting | bytes 7340032 | tf_op jit(solution)/shard_map/optimization_barrier | solution.py:413
  25.7 6.5 %collective-permute-done.6.refs_2_ = bf16[8,448,128]{2,1,0:T(8,128)(2,1)S(1)} collective-permute-done((bf16[8,448,128]{2,1,0:T(8,128)(2,1)}, bf16[8,448,128]{2,1,0:T(8,128)(2,1)S(1)}, u32[]{:S(2)}, u32[]{:S(2)}) %collective-permute-start.6) | collective-permute-done | bytes 917536 | tf_op jit(solution)/shard_map/ppermute | solution.py:24
  34.3 2.7 %collective-permute-start.5 = (bf16[2,448,128]{2,1,0:T(8,128)(2,1)}, bf16[2,448,128]{2,1,0:T(8,128)(2,1)S(1)}, u32[]{:S(2)}, u32[]{:S(2)}) collective-permute-start(bf16[2,448,128]{2,1,0:T(8,128)(2,1)} %get-tuple-element.45), channel_id=1, source_target_pairs={{0,6},{2,4},{4,2},{6,0},{8,14},{10,12},{12,10},{14,8},{16,22},{18,... | collective-permute-start | bytes 688136 | tf_op jit(solution)/shard_map/ppermute | solution.py:24
  37.1 2.8 %collective-permute-done.4 = bf16[2,448,128]{2,1,0:T(8,128)(2,1)S(1)} collective-permute-done((bf16[2,448,128]{2,1,0:T(8,128)(2,1)}, bf16[2,448,128]{2,1,0:T(8,128)(2,1)S(1)}, u32[]{:S(2)}, u32[]{:S(2)}) %collective-permute-start.4) | collective-permute-done | bytes 229408 | tf_op jit(solution)/shard_map/ppermute | solution.py:24
  41.2 5.2 %collective-permute-done.5 = bf16[2,448,128]{2,1,0:T(8,128)(2,1)S(1)} collective-permute-done((bf16[2,448,128]{2,1,0:T(8,128)(2,1)}, bf16[2,448,128]{2,1,0:T(8,128)(2,1)S(1)}, u32[]{:S(2)}, u32[]{:S(2)}) %collective-permute-start.5) | collective-permute-done | bytes 229408 | tf_op jit(solution)/shard_map/ppermute | solution.py:24
  47.8 1.9 collective-permute-start.8
  50.5 2.8 %pick_blocks.5 = (bf16[2,448,128]{2,1,0:T(8,128)(2,1)}, bf16[2,448,128]{2,1,0:T(8,128)(2,1)}, bf16[2,448,128]{2,1,0:T(8,128)(2,1)}, bf16[2,448,128]{2,1,0:T(8,128)(2,1)}) custom-call(s32[1]{0:T(128)} %constant.76.clone.1.refs_0_, s32[4,2]{1,0:T(4,128)} %copy.34.refs_1_, bf16[8,448,128]{2,1,0:T(8,128)(2,1)} %copy-done.5), custom_call_target="tpu_custom_call" | custom-call | tf_op jit(solution)/shard_map/pick_blocks/pallas_call | solution.py:107
  55.9 23.5 %collective-permute-start.12 = (bf16[2,448,128]{2,1,0:T(8,128)(2,1)}, bf16[2,448,128]{2,1,0:T(8,128)(2,1)}, u32[]{:S(2)}, u32[]{:S(2)}) collective-permute-start(bf16[2,448,128]{2,1,0:T(8,128)(2,1)} %get-tuple-element.53), channel_id=1, source_target_pairs={{0,4},{2,6},{4,0},{6,2},{8,12},{10,14},{12,8},{14,10},{16,20},{18,... | collective-permute-start | bytes 688136 | tf_op jit(solution)/shard_map/ppermute | solution.py:24
  79.3 5.0 %windows.1.refs_4_ = bf16[16,64,2048]{2,1,0:T(8,128)(2,1)} custom-call(bf16[1024,2048]{1,0:T(8,128)(2,1)} %next_ref, bf16[1024,2048]{1,0:T(8,128)(2,1)} %next_ref, bf16[64,2048]{1,0:T(8,128)(2,1)} %copy-done.9), custom_call_target="tpu_custom_call" | custom-call | tf_op jit(solution)/shard_map/windows/pallas_call | solution.py:56
  86.1 2.7 %pick_blocks.6 = (bf16[2,448,128]{2,1,0:T(8,128)(2,1)}, bf16[2,448,128]{2,1,0:T(8,128)(2,1)}, bf16[2,448,128]{2,1,0:T(8,128)(2,1)}, bf16[2,448,128]{2,1,0:T(8,128)(2,1)}) custom-call(s32[1]{0:T(128)} %bitcast.1.refs_0_, s32[4,2]{1,0:T(4,128)} %copy.35.refs_1_, bf16[8,448,128]{2,1,0:T(8,128)(2,1)} %collective-permute-done.9.refs_2_, ...), custom_call_target="tpu_custom_call" | custom-call | tf_op jit(solution)/shard_map/pick_blocks/pallas_call | solution.py:107
  90.0 1.8 collective-permute-done.13
  94.6 18.5 %attend_part.4 = (bf16[32,64,2048]{2,1,0:T(8,128)(2,1)}, f32[32,64,128]{2,1,0:T(8,128)}) custom-call(s32[1]{0:T(128)} %bitcast.refs_0_, s32[8]{0:T(128)} %get-tuple-element.63.refs_1_, bf16[8,448,128]{2,1,0:T(8,128)(2,1)} %copy-done.3, bf16[8,448,128]{2,1,0:T(8,128)(2,1)} %collective-permute-done.14.refs_3_, bf16[16,64,2048]{2,1,0:T(8,128)(2,1)} %windows.1.refs_4_, ...), custom_call_target="tpu_custom_call" | custom-call | tf_op jit(solution)/shard_map/attend_part/pallas_call | solution.py:261
  114.8 2.7 %pick_blocks.7 = (bf16[2,448,128]{2,1,0:T(8,128)(2,1)}, bf16[2,448,128]{2,1,0:T(8,128)(2,1)}, bf16[2,448,128]{2,1,0:T(8,128)(2,1)}, bf16[2,448,128]{2,1,0:T(8,128)(2,1)}) custom-call(s32[1]{0:T(128)} %bitcast.1.refs_0_, s32[4,2]{1,0:T(4,128)} %copy.36.refs_1_, bf16[8,448,128]{2,1,0:T(8,128)(2,1)} %collective-permute-done.15.refs_2_, ...), custom_call_target="tpu_custom_call" | custom-call | tf_op jit(solution)/shard_map/pick_blocks/pallas_call | solution.py:107
  121.4 4.2 %collective-permute-done.17 = bf16[2,448,128]{2,1,0:T(8,128)(2,1)S(1)} collective-permute-done((bf16[2,448,128]{2,1,0:T(8,128)(2,1)}, bf16[2,448,128]{2,1,0:T(8,128)(2,1)S(1)}, u32[]{:S(2)}, u32[]{:S(2)}) %collective-permute-start.17) | collective-permute-done | bytes 229408 | tf_op jit(solution)/shard_map/ppermute | solution.py:24
  125.6 5.6 %collective-permute-done.18 = bf16[2,448,128]{2,1,0:T(8,128)(2,1)S(1)} collective-permute-done((bf16[2,448,128]{2,1,0:T(8,128)(2,1)}, bf16[2,448,128]{2,1,0:T(8,128)(2,1)S(1)}, u32[]{:S(2)}, u32[]{:S(2)}) %collective-permute-start.18) | collective-permute-done | bytes 229408 | tf_op jit(solution)/shard_map/ppermute | solution.py:24
  133.6 18.5 %attend_part.5 = (bf16[32,64,2048]{2,1,0:T(8,128)(2,1)}, f32[32,64,128]{2,1,0:T(8,128)}) custom-call(s32[1]{0:T(128)} %bitcast.refs_0_, s32[8]{0:T(128)} %get-tuple-element.72.refs_1_, bf16[8,448,128]{2,1,0:T(8,128)(2,1)} %copy-done, bf16[8,448,128]{2,1,0:T(8,128)(2,1)} %copy-done.6, ...), custom_call_target="tpu_custom_call", output_to_operand_aliasing={{0}: (9, {}), {1}: (10, {})} | custom-call | tf_op jit(solution)/shard_map/attend_part/pallas_call | solution.py:261
  153.1 18.6 %attend_part.6 = (bf16[32,64,2048]{2,1,0:T(8,128)(2,1)}, f32[32,64,128]{2,1,0:T(8,128)}) custom-call(s32[1]{0:T(128)} %bitcast.refs_0_, s32[8]{0:T(128)} %get-tuple-element.71.refs_1_, bf16[8,448,128]{2,1,0:T(8,128)(2,1)} %copy-done.1, bf16[8,448,128]{2,1,0:T(8,128)(2,1)} %copy-done.7, ...), custom_call_target="tpu_custom_call", output_to_operand_aliasing={{0}: (9, {}), {1}: (10, {})} | custom-call | tf_op jit(solution)/shard_map/attend_part/pallas_call | solution.py:261
  172.6 18.6 %attend_part.7 = (bf16[32,64,2048]{2,1,0:T(8,128)(2,1)}, f32[32,64,128]{2,1,0:T(8,128)}) custom-call(s32[1]{0:T(128)} %bitcast.refs_0_, s32[8]{0:T(128)} %get-tuple-element.88.refs_1_, bf16[8,448,128]{2,1,0:T(8,128)(2,1)} %copy-done.2, bf16[8,448,128]{2,1,0:T(8,128)(2,1)} %copy-done.8, ...), custom_call_target="tpu_custom_call", output_to_operand_aliasing={{0}: (9, {}), {1}: (10, {})} | custom-call | tf_op jit(solution)/shard_map/attend_part/pallas_call | solution.py:261
  191.2 2.8 %mix_last.1 = bf16[64,2048]{1,0:T(8,128)(2,1)} custom-call(s32[32]{0:T(128)} %copy-done.14, bf16[32,64,2048]{2,1,0:T(8,128)(2,1)} %get-tuple-element.77.p0.p1.refs_0_.refs_1_.refs_4_.refs_5_.refs_8_.refs_9_.refs_12_.refs_13_, bf16[32,64,2048]{2,1,0:T(8,128)(2,1)} %get-tuple-element.77.p0.p1.refs_0_.refs_1_.refs_4_.refs_5_.refs_8_.refs_9_.refs_12_.refs_13_, ...), custom_call_target="tpu_custom_call" | custom-call | tf_op jit(solution)/shard_map/mix_last/pallas_call | solution.py:354
  194.0 2.5 %collective-permute-start.25 = (bf16[64,2048]{1,0:T(8,128)(2,1)}, bf16[64,2048]{1,0:T(8,128)(2,1)S(1)}, u32[]{:S(2)}, u32[]{:S(2)}) collective-permute-start(bf16[64,2048]{1,0:T(8,128)(2,1)} %mix_last.1), channel_id=1, source_target_pairs={{0,2},{2,4},{4,6},{6,8},{8,10},{10,12},{12,14},{14,16},{16,18},{18... | collective-permute-start | bytes 786440 | tf_op jit(solution)/shard_map/ppermute | solution.py:19
  196.5 8.2 %mix.1.rows = bf16[1024,2048]{1,0:T(8,128)(2,1)} custom-call(s32[32]{0:T(128)} %copy-done.14, bf16[32,64,2048]{2,1,0:T(8,128)(2,1)} %get-tuple-element.77.p0.p1.refs_0_.refs_1_.refs_4_.refs_5_.refs_8_.refs_9_.refs_12_.refs_13_, bf16[32,64,2048]{2,1,0:T(8,128)(2,1)} %get-tuple-element.77.p0.p1.refs_0_.refs_1_.refs_4_.refs_5_.refs_8_.refs_9_.refs_12_.refs_13_, ...), custom_call_target="tpu_custom_call" | custom-call | tf_op jit(solution)/shard_map/mix/pallas_call | solution.py:374
  (110 shorter events, 34.0 us)
Async XLA Ops:
  0.8 4.0 %collective-permute-start = (s32[32]{0:T(128)S(1)}, s32[32]{0:T(128)S(1)}, u32[]{:S(2)}, u32[]{:S(2)}) collective-permute-start(s32[32]{0:T(128)S(1)} %reshape.606), channel_id=1, source_target_pairs={{0,2},{2,0},{4,6},{6,4},{8,10},{10,8},{12,14},{14,12},{16,18},{18,... | collective-permute-start | bytes 392 | tf_op jit(solution)/shard_map/ppermute | solution.py:24
  1.0 3.9 %collective-permute-start.1 = (s32[32]{0:T(128)S(1)}, s32[32]{0:T(128)S(1)}, u32[]{:S(2)}, u32[]{:S(2)}) collective-permute-start(s32[32]{0:T(128)S(1)} %reshape.606), channel_id=1, source_target_pairs={{0,4},{2,6},{4,0},{6,2},{8,12},{10,14},{12,8},{14,10},{16,20},{18,... | collective-permute-start | bytes 392 | tf_op jit(solution)/shard_map/ppermute | solution.py:24
  10.6 21.7 %collective-permute-start.6 = (bf16[8,448,128]{2,1,0:T(8,128)(2,1)}, bf16[8,448,128]{2,1,0:T(8,128)(2,1)S(1)}, u32[]{:S(2)}, u32[]{:S(2)}) collective-permute-start(bf16[8,448,128]{2,1,0:T(8,128)(2,1)} %refs_2_.1), channel_id=1, source_target_pairs={{0,8},{2,10},{4,12},{6,14},{8,0},{10,2},{12,4},{14,6},{16,24},{18,... | collective-permute-start | bytes 2752520 | tf_op jit(solution)/shard_map/ppermute | solution.py:24
  12.0 20.3 %collective-permute-start.7 = (bf16[8,448,128]{2,1,0:T(8,128)(2,1)}, bf16[8,448,128]{2,1,0:T(8,128)(2,1)S(1)}, u32[]{:S(2)}, u32[]{:S(2)}) collective-permute-start(bf16[8,448,128]{2,1,0:T(8,128)(2,1)} %refs_2_.1), channel_id=1, source_target_pairs={{8,16},{10,18},{12,20},{14,22},{16,8},{18,10},{20,12},{22,14},{9,1... | collective-permute-start | bytes 2752520 | tf_op jit(solution)/shard_map/ppermute | solution.py:454
  12.9 24.1 %collective-permute-start.3 = (bf16[2,448,128]{2,1,0:T(8,128)(2,1)}, bf16[2,448,128]{2,1,0:T(8,128)(2,1)S(1)}, u32[]{:S(2)}, u32[]{:S(2)}) collective-permute-start(bf16[2,448,128]{2,1,0:T(8,128)(2,1)} %get-tuple-element.43), channel_id=1, source_target_pairs={{0,2},{2,0},{4,6},{6,4},{8,10},{10,8},{12,14},{14,12},{16,18},{18,... | collective-permute-start | bytes 688136 | tf_op jit(solution)/shard_map/ppermute | solution.py:24
  32.3 21.0 %collective-permute-start.10 = (bf16[8,448,128]{2,1,0:T(8,128)(2,1)S(1)}, bf16[8,448,128]{2,1,0:T(8,128)(2,1)}, u32[]{:S(2)}, u32[]{:S(2)}) collective-permute-start(bf16[8,448,128]{2,1,0:T(8,128)(2,1)S(1)} %collective-permute-done.6.refs_2_), channel_id=1, source_target_pairs={{8,16},{10,18},{12,20},{14,22},{16,8},{18,10},{20,12},{22,14},{9,1... | collective-permute-start | bytes 2752520 | tf_op jit(solution)/shard_map/ppermute | solution.py:454
  33.9 6.0 %collective-permute-start.4 = (bf16[2,448,128]{2,1,0:T(8,128)(2,1)}, bf16[2,448,128]{2,1,0:T(8,128)(2,1)S(1)}, u32[]{:S(2)}, u32[]{:S(2)}) collective-permute-start(bf16[2,448,128]{2,1,0:T(8,128)(2,1)} %get-tuple-element.44), channel_id=1, source_target_pairs={{0,4},{2,6},{4,0},{6,2},{8,12},{10,14},{12,8},{14,10},{16,20},{18,... | collective-permute-start | bytes 688136 | tf_op jit(solution)/shard_map/ppermute | solution.py:24
  34.3 12.1 %collective-permute-start.5 = (bf16[2,448,128]{2,1,0:T(8,128)(2,1)}, bf16[2,448,128]{2,1,0:T(8,128)(2,1)S(1)}, u32[]{:S(2)}, u32[]{:S(2)}) collective-permute-start(bf16[2,448,128]{2,1,0:T(8,128)(2,1)} %get-tuple-element.45), channel_id=1, source_target_pairs={{0,6},{2,4},{4,2},{6,0},{8,14},{10,12},{12,10},{14,8},{16,22},{18,... | collective-permute-start | bytes 688136 | tf_op jit(solution)/shard_map/ppermute | solution.py:24
  39.9 46.2 %collective-permute-start.9 = (bf16[8,448,128]{2,1,0:T(8,128)(2,1)S(1)}, bf16[8,448,128]{2,1,0:T(8,128)(2,1)}, u32[]{:S(2)}, u32[]{:S(2)}) collective-permute-start(bf16[8,448,128]{2,1,0:T(8,128)(2,1)S(1)} %collective-permute-done.7.refs_3_), channel_id=1, source_target_pairs={{8,0},{10,2},{12,4},{14,6},{16,24},{18,26},{20,28},{22,30},{9,1},{... | collective-permute-start | bytes 2752520 | tf_op jit(solution)/shard_map/ppermute | solution.py:454
  46.5 47.6 %collective-permute-start.14 = (bf16[8,448,128]{2,1,0:T(8,128)(2,1)S(1)}, bf16[8,448,128]{2,1,0:T(8,128)(2,1)}, u32[]{:S(2)}, u32[]{:S(2)}) collective-permute-start(bf16[8,448,128]{2,1,0:T(8,128)(2,1)S(1)} %constant_dynamic-update-slice_fusion.refs_2_), channel_id=1, source_target_pairs={{0,1},{1,0},{2,3},{3,2},{4,5},{5,4},{6,7},{7,6},{8,9},{9,8},{10,11... | collective-permute-start | bytes 2752520 | tf_op jit(solution)/shard_map/ppermute | solution.py:24
  47.8 8.1 %collective-permute-start.8 = (bf16[64,2048]{1,0:T(8,128)(2,1)S(1)}, bf16[64,2048]{1,0:T(8,128)(2,1)S(1)}, u32[]{:S(2)}, u32[]{:S(2)}) collective-permute-start(bf16[64,2048]{1,0:T(8,128)(2,1)S(1)} %slice.37), channel_id=1, source_target_pairs={{2,0},{4,2},{6,4},{8,6},{10,8},{12,10},{14,12},{16,14},{18,16},{20... | collective-permute-start | bytes 786440 | tf_op jit(solution)/shard_map/ppermute | solution.py:19
  53.2 31.8 %collective-permute-start.11 = (bf16[2,448,128]{2,1,0:T(8,128)(2,1)}, bf16[2,448,128]{2,1,0:T(8,128)(2,1)S(1)}, u32[]{:S(2)}, u32[]{:S(2)}) collective-permute-start(bf16[2,448,128]{2,1,0:T(8,128)(2,1)} %get-tuple-element.52), channel_id=1, source_target_pairs={{0,2},{2,0},{4,6},{6,4},{8,10},{10,8},{12,14},{14,12},{16,18},{18,... | collective-permute-start | bytes 688136 | tf_op jit(solution)/shard_map/ppermute | solution.py:24
  53.3 61.5 %collective-permute-start.15 = (bf16[8,448,128]{2,1,0:T(8,128)(2,1)}, bf16[8,448,128]{2,1,0:T(8,128)(2,1)}, u32[]{:S(2)}, u32[]{:S(2)}) collective-permute-start(bf16[8,448,128]{2,1,0:T(8,128)(2,1)} %collective-permute-done.10.refs_3_), channel_id=1, source_target_pairs={{8,0},{10,2},{12,4},{14,6},{16,24},{18,26},{20,28},{22,30},{9,1},{... | collective-permute-start | bytes 2752520 | tf_op jit(solution)/shard_map/ppermute | solution.py:454
  55.9 29.3 %collective-permute-start.12 = (bf16[2,448,128]{2,1,0:T(8,128)(2,1)}, bf16[2,448,128]{2,1,0:T(8,128)(2,1)}, u32[]{:S(2)}, u32[]{:S(2)}) collective-permute-start(bf16[2,448,128]{2,1,0:T(8,128)(2,1)} %get-tuple-element.53), channel_id=1, source_target_pairs={{0,4},{2,6},{4,0},{6,2},{8,12},{10,14},{12,8},{14,10},{16,20},{18,... | collective-permute-start | bytes 688136 | tf_op jit(solution)/shard_map/ppermute | solution.py:24
  85.0 6.8 %collective-permute-start.13 = (bf16[2,448,128]{2,1,0:T(8,128)(2,1)}, bf16[2,448,128]{2,1,0:T(8,128)(2,1)S(1)}, u32[]{:S(2)}, u32[]{:S(2)}) collective-permute-start(bf16[2,448,128]{2,1,0:T(8,128)(2,1)} %get-tuple-element.54), channel_id=1, source_target_pairs={{0,6},{2,4},{4,2},{6,0},{8,14},{10,12},{12,10},{14,8},{16,22},{18,... | collective-permute-start | bytes 688136 | tf_op jit(solution)/shard_map/ppermute | solution.py:24
  88.9 24.9 %collective-permute-start.20 = (bf16[2,448,128]{2,1,0:T(8,128)(2,1)}, bf16[2,448,128]{2,1,0:T(8,128)(2,1)S(1)}, u32[]{:S(2)}, u32[]{:S(2)}) collective-permute-start(bf16[2,448,128]{2,1,0:T(8,128)(2,1)} %get-tuple-element.60), channel_id=1, source_target_pairs={{0,2},{2,0},{4,6},{6,4},{8,10},{10,8},{12,14},{14,12},{16,18},{18,... | collective-permute-start | bytes 688136 | tf_op jit(solution)/shard_map/ppermute | solution.py:24
  91.9 40.8 %collective-permute-start.24 = (bf16[8,448,128]{2,1,0:T(8,128)(2,1)S(1)}, bf16[8,448,128]{2,1,0:T(8,128)(2,1)S(1)}, u32[]{:S(2)}, u32[]{:S(2)}) collective-permute-start(bf16[8,448,128]{2,1,0:T(8,128)(2,1)S(1)} %constant_dynamic-update-slice_fusion.4.refs_2_), channel_id=1, source_target_pairs={{0,1},{1,0},{2,3},{3,2},{4,5},{5,4},{6,7},{7,6},{8,9},{9,8},{10,11... | collective-permute-start | bytes 2752520 | tf_op jit(solution)/shard_map/ppermute | solution.py:24
  93.3 20.5 %collective-permute-start.21 = (bf16[2,448,128]{2,1,0:T(8,128)(2,1)}, bf16[2,448,128]{2,1,0:T(8,128)(2,1)}, u32[]{:S(2)}, u32[]{:S(2)}) collective-permute-start(bf16[2,448,128]{2,1,0:T(8,128)(2,1)} %get-tuple-element.61), channel_id=1, source_target_pairs={{0,4},{2,6},{4,0},{6,2},{8,12},{10,14},{12,8},{14,10},{16,20},{18,... | collective-permute-start | bytes 688136 | tf_op jit(solution)/shard_map/ppermute | solution.py:24
  94.1 24.1 %collective-permute-start.22 = (bf16[2,448,128]{2,1,0:T(8,128)(2,1)}, bf16[2,448,128]{2,1,0:T(8,128)(2,1)S(1)}, u32[]{:S(2)}, u32[]{:S(2)}) collective-permute-start(bf16[2,448,128]{2,1,0:T(8,128)(2,1)} %get-tuple-element.62), channel_id=1, source_target_pairs={{0,6},{2,4},{4,2},{6,0},{8,14},{10,12},{12,10},{14,8},{16,22},{18,... | collective-permute-start | bytes 688136 | tf_op jit(solution)/shard_map/ppermute | solution.py:24
  118.3 33.9 %collective-permute-start.23 = (bf16[8,448,128]{2,1,0:T(8,128)(2,1)S(1)}, bf16[8,448,128]{2,1,0:T(8,128)(2,1)S(1)}, u32[]{:S(2)}, u32[]{:S(2)}) collective-permute-start(bf16[8,448,128]{2,1,0:T(8,128)(2,1)S(1)} %constant_dynamic-update-slice_fusion.12.refs_2_), channel_id=1, source_target_pairs={{0,1},{1,0},{2,3},{3,2},{4,5},{5,4},{6,7},{7,6},{8,9},{9,8},{10,11... | collective-permute-start | bytes 2752520 | tf_op jit(solution)/shard_map/ppermute | solution.py:24
  118.5 7.1 %collective-permute-start.17 = (bf16[2,448,128]{2,1,0:T(8,128)(2,1)}, bf16[2,448,128]{2,1,0:T(8,128)(2,1)S(1)}, u32[]{:S(2)}, u32[]{:S(2)}) collective-permute-start(bf16[2,448,128]{2,1,0:T(8,128)(2,1)} %get-tuple-element.69), channel_id=1, source_target_pairs={{0,4},{2,6},{4,0},{6,2},{8,12},{10,14},{12,8},{14,10},{16,20},{18,... | collective-permute-start | bytes 688136 | tf_op jit(solution)/shard_map/ppermute | solution.py:24
  119.2 12.0 %collective-permute-start.18 = (bf16[2,448,128]{2,1,0:T(8,128)(2,1)}, bf16[2,448,128]{2,1,0:T(8,128)(2,1)S(1)}, u32[]{:S(2)}, u32[]{:S(2)}) collective-permute-start(bf16[2,448,128]{2,1,0:T(8,128)(2,1)} %get-tuple-element.70), channel_id=1, source_target_pairs={{0,6},{2,4},{4,2},{6,0},{8,14},{10,12},{12,10},{14,8},{16,22},{18,... | collective-permute-start | bytes 688136 | tf_op jit(solution)/shard_map/ppermute | solution.py:24
  131.3 40.4 %collective-permute-start.19 = (bf16[8,448,128]{2,1,0:T(8,128)(2,1)S(1)}, bf16[8,448,128]{2,1,0:T(8,128)(2,1)S(1)}, u32[]{:S(2)}, u32[]{:S(2)}) collective-permute-start(bf16[8,448,128]{2,1,0:T(8,128)(2,1)S(1)} %constant_dynamic-update-slice_fusion.8.refs_2_), channel_id=1, source_target_pairs={{0,1},{1,0},{2,3},{3,2},{4,5},{5,4},{6,7},{7,6},{8,9},{9,8},{10,11... | collective-permute-start | bytes 2752520 | tf_op jit(solution)/shard_map/ppermute | solution.py:24
  194.0 10.7 %collective-permute-start.25 = (bf16[64,2048]{1,0:T(8,128)(2,1)}, bf16[64,2048]{1,0:T(8,128)(2,1)S(1)}, u32[]{:S(2)}, u32[]{:S(2)}) collective-permute-start(bf16[64,2048]{1,0:T(8,128)(2,1)} %mix_last.1), channel_id=1, source_target_pairs={{0,2},{2,4},{4,6},{6,8},{8,10},{10,12},{12,14},{14,16},{16,18},{18... | collective-permute-start | bytes 786440 | tf_op jit(solution)/shard_map/ppermute | solution.py:19
  (17 other events, 333.7 us)

commit v5 on v4

--- a/solution.py
+++ b/solution.py
@@ -70,159 +70,152 @@
     )(queries, queries, incoming)
 
 
-def pick_kernel(count, which, table, *refs):
-    options = len(refs) - count - 3
-    sources, outs = refs[:options], refs[options : options + count]
+def pick_kernel(part, ranks, table, *refs):
+    count = INNER - 1
+    pieces = len(refs) - count - 3
+    sources, outs = refs[:pieces], refs[pieces : pieces + count]
     held, in_sems, out_sems = refs[-3:]
-    ranks = table.shape[1]
-    places = [(k, r) for k in range(count) for r in range(ranks)]
-
-    def fetch(source, n):
-        return pltpu.make_async_copy(source.at[table[places[n]]], held.at[n], in_sems.at[n])
-
-    for option, source in enumerate(sources):
-
-        @pl.when(which[0] == option)
-        def _(source=source):
-            for n in range(len(places)):
-                fetch(source, n).start()
-
-    stores = []
-    for n, (k, r) in enumerate(places):
-        fetch(sources[0], n).wait()
-        stores.append(pltpu.make_async_copy(held.at[n], outs[k].at[r], out_sems.at[n]))
-        stores[-1].start()
+    fetches, stores = [], []
+    for k in range(1, INNER):
+        for r in range(ranks):
+            block = table[(part * INNER + k) * ranks + r]
+            for piece in range(pieces):
+                n = len(fetches)
+                fetches.append(
+                    pltpu.make_async_copy(sources[piece].at[block], held.at[n], in_sems.at[n])
+                )
+                stores.append(
+                    pltpu.make_async_copy(held.at[n], outs[k - 1].at[r, piece], out_sems.at[n])
+                )
+    for fetch in fetches:
+        fetch.start()
+    for fetch, store in zip(fetches, stores):
+        fetch.wait()
+        store.start()
     for store in stores:
         store.wait()
 
 
-def pick_blocks(which, table, sources):
-    count, ranks = table.shape
+def pick_blocks(part, ranks, table, sources):
     shape = sources[0].shape[1:]
-    copies = count * ranks
+    pieces = len(sources)
+    copies = (INNER - 1) * ranks * pieces
 
     def body(*refs):
-        pick_kernel(count, *refs)
+        pick_kernel(part, ranks, *refs)
 
     return pl.pallas_call(
         body,
         grid_spec=pltpu.PrefetchScalarGridSpec(
-            num_scalar_prefetch=2,
+            num_scalar_prefetch=1,
             grid=(1,),
-            in_specs=[pl.BlockSpec(memory_space=pl.ANY)] * len(sources),
-            out_specs=[pl.BlockSpec(memory_space=pl.ANY)] * count,
+            in_specs=[pl.BlockSpec(memory_space=pl.ANY)] * pieces,
+            out_specs=[pl.BlockSpec(memory_space=pl.ANY)] * (INNER - 1),
             scratch_shapes=[
                 pltpu.VMEM((copies,) + shape, sources[0].dtype),
                 pltpu.SemaphoreType.DMA((copies,)),
                 pltpu.SemaphoreType.DMA((copies,)),
             ],
         ),
-        out_shape=[jax.ShapeDtypeStruct((ranks,) + shape, sources[0].dtype) for _ in range(count)],
+        out_shape=[
+            jax.ShapeDtypeStruct((ranks, pieces) + shape, sources[0].dtype)
+            for _ in range(INNER - 1)
+        ],
         compiler_params=pltpu.CompilerParams(vmem_limit_bytes=VMEM_LIMIT),
         name="pick_blocks",
-    )(which, table, *sources)
-
-
-def attend_kernel(cap, parts, steps, tp_index, spans, *refs):
-    x_refs = refs[:parts]
-    q_ref, wk_first, wk_next, wv_first, wv_next = refs[parts : parts + 5]
-    out_ref, lse_ref, x_all, weights_ref, k_even, v_even, k_odd, v_odd = refs[-8:]
-    nlen = x_refs[0].shape[-1]
-    width = x_refs[0].shape[1]
-    columns = q_ref.shape[-1]
-    pairs = columns // PAIR
+    )(table, *sources)
+
+
+def attend_kernel(part, cap, ranks, pieces, steps, tp_index, table, spans, *refs):
+    count = ranks * pieces + INNER - 1
+    own_refs, got_refs = refs[: ranks * pieces], refs[ranks * pieces : count]
+    q_ref, wk_first, wk_next, wv_first, wv_next = refs[count : count + 5]
+    out_ref, lse_ref, x_all, scores_ref, weights_ref, k_even, v_even, k_odd, v_odd = refs[-9:]
+    nlen = scores_ref.shape[-1]
+    pairs = scores_ref.shape[0] // cap
     step = pl.program_id(0)
     scale = HDIM ** (-0.5)
     lanes = lax.broadcasted_iota(jnp.int32, (SPAN, LANES), 1)
-    rows = 2 * SPAN
-
-    def two_slots(n):
-        return pl.ds(n * 2 * nlen, 2 * nlen)
-
-    def project(n, w_ref, out):
-        out[:, two_slots(n)] = jnp.dot(
-            w_ref[...], x_all[:, two_slots(n)], preferred_element_type=jnp.float32
-        ).astype(jnp.bfloat16)
-
-    def window(slot, pair):
-        q = q_ref[spans[slot], :, pair * PAIR : (pair + 1) * PAIR]
+
+    def project(w_ref, out):
+        out[...] = jnp.dot(w_ref[...], x_all[...], preferred_element_type=jnp.float32).astype(
+            jnp.bfloat16
+        )
+
+    def block(ref, pair, i):
+        return ref[pair * PAIR : (pair + 1) * PAIR, i * nlen : (i + 1) * nlen]
+
+    def score(k_ref):
         none = jnp.zeros((SPAN, HDIM), jnp.bfloat16)
-        upper = jnp.concatenate([q[:, :HDIM], none], axis=1)
-        lower = jnp.concatenate([none, q[:, HDIM:]], axis=1)
-        return [upper, lower]
-
-    def soften(n, pair, both):
-        for a in range(2):
-            scores = both[a * rows : (a + 1) * rows, a * nlen : (a + 1) * nlen]
-            highest = jnp.max(scores, axis=1, keepdims=True)
-            exponent = jnp.exp((scores - highest) * scale)
-            totals = jnp.sum(exponent, axis=1, keepdims=True)
-            weights_ref[pair, a * rows : (a + 1) * rows, a * nlen : (a + 1) * nlen] = (
-                exponent * (1.0 / totals)
-            ).astype(jnp.bfloat16)
-            lse = highest * scale + jnp.log(totals)
-            at = pairs * step + pair
-            held = jnp.where(lanes == at, lse[:SPAN], lse_ref[2 * n + a])
-            lse_ref[2 * n + a] = jnp.where(lanes == LANES // 8 + at, lse[SPAN:], held)
-
-    def attend(n, k_now, v_now, between):
-        scores = []
         for pair in range(pairs):
-            q = jnp.concatenate(window(2 * n, pair) + window(2 * n + 1, pair), axis=0)
-            keys = k_now[pair * PAIR : (pair + 1) * PAIR, two_slots(n)]
-            scores.append(jnp.dot(q, keys, preferred_element_type=jnp.float32))
-        between[0]()
-        for pair in range(pairs):
-            soften(n, pair, scores[pair])
-        between[1]()
+            for i in range(cap):
+                q = q_ref[spans[part * cap + i], :, pair * PAIR : (pair + 1) * PAIR]
+                upper = jnp.concatenate([q[:, :HDIM], none], axis=1)
+                lower = jnp.concatenate([none, q[:, HDIM:]], axis=1)
+                scores_ref[pair * cap + i] = jnp.dot(
+                    jnp.concatenate([upper, lower], axis=0),
+                    block(k_ref, pair, i),
+                    preferred_element_type=jnp.float32,
+                )
+
+    def soften():
+        for i in range(cap):
+            held = lse_ref[i]
+            for pair in range(pairs):
+                scores = scores_ref[pair * cap + i]
+                highest = jnp.max(scores, axis=1, keepdims=True)
+                exponent = jnp.exp((scores - highest) * scale)
+                totals = jnp.sum(exponent, axis=1, keepdims=True)
+                weights_ref[pair * cap + i] = (exponent * (1.0 / totals)).astype(jnp.bfloat16)
+                lse = highest * scale + jnp.log(totals)
+                at = pairs * step + pair
+                held = jnp.where(lanes == at, lse[:SPAN], held)
+                held = jnp.where(lanes == LANES // 8 + at, lse[SPAN:], held)
+            lse_ref[i] = held
+
+    def blend(v_ref):
         for pair in range(pairs):
             cols = slice(pair * PAIR, (pair + 1) * PAIR)
-            blended = lax.dot_general(
-                weights_ref[pair],
-                v_now[cols, two_slots(n)],
-                (((1,), (1,)), ((), ())),
-                preferred_element_type=jnp.float32,
-            )
-            for a in range(2):
-                top = a * rows
-                out_ref[2 * n + a, :, cols] = jnp.concatenate(
-                    [blended[top : top + SPAN, :HDIM], blended[top + SPAN : top + rows, HDIM:]],
-                    axis=1,
+            for i in range(cap):
+                blended = lax.dot_general(
+                    weights_ref[pair * cap + i],
+                    block(v_ref, pair, i),
+                    (((1,), (1,)), ((), ())),
+                    preferred_element_type=jnp.float32,
+                )
+                out_ref[i, :, cols] = jnp.concatenate(
+                    [blended[:SPAN, :HDIM], blended[SPAN:, HDIM:]], axis=1
                 ).astype(jnp.bfloat16)
-
-    def over_slots(body):
-        for n in range(cap // 2):
-            body(n)
 
     @pl.when(step == 0)
     def _():
         lse_ref[...] = jnp.zeros_like(lse_ref)
-        weights_ref[...] = jnp.zeros_like(weights_ref)
-        for part, x_ref in enumerate(x_refs):
-            top = 0
-            if parts == 2:
-                top = pl.multiple_of((tp_index[0] if part == 0 else 1 - tp_index[0]) * width, 16)
-            for i in range(cap):
-                x_all[pl.ds(top, width), i * nlen : (i + 1) * nlen] = x_ref[i]
-
-        def first(n):
-            project(n, wk_first, k_even)
-            project(n, wv_first, v_even)
-
-        over_slots(first)
+        for i in range(cap):
+            for piece in range(pieces):
+                if i < ranks:
+                    block = own_refs[i * pieces + piece][0]
+                else:
+                    block = got_refs[i // ranks - 1][i % ranks, piece]
+                width = block.shape[0]
+                top = 0
+                if pieces == 2:
+                    place = tp_index[0] if piece == 0 else 1 - tp_index[0]
+                    top = pl.multiple_of(place * width, 16)
+                x_all[pl.ds(top, width), i * nlen : (i + 1) * nlen] = block
+        project(wk_first, k_even)
+        project(wv_first, v_even)
 
     def work(k_now, v_now, k_later, v_later):
-        def body(n):
-            between = [
-                lambda: project(n, wk_next, k_later),
-                lambda: project(n, wv_next, v_later),
-            ]
-            attend(n, k_now, v_now, between)
-
-        over_slots(body)
+        score(k_now)
+        project(wk_next, k_later)
+        soften()
+        project(wv_next, v_later)
+        blend(v_now)
 
     def finish(k_now, v_now):
-        over_slots(lambda n: attend(n, k_now, v_now, [lambda: None] * 2))
+        score(k_now)
+        soften()
+        blend(v_now)
 
     if steps > 1:
         pl.when((step < steps - 1) & (step % 2 == 0))(lambda: work(k_even, v_even, k_odd, v_odd))
@@ -232,16 +225,23 @@
     pl.when(step == steps - 1)(lambda: finish(*ends))
 
 
-def attend_part(tp_index, spans, blocks, windows, weights, part_index, slots, held):
-    parts, cap = len(blocks), spans.shape[0]
-    width, nlen = blocks[0].shape[1:]
-    features = width * parts
+def attend_part(part, cap, scalars, own, got, windows, weights, slots, held):
+    pieces = len(own)
+    ranks = got[0].shape[0]
+    width, nlen = own[0].shape[1:]
+    features = width * pieces
     columns = 2 * PAIR
     steps = windows.shape[-1] // columns
 
-    in_specs = [pl.BlockSpec(x.shape, lambda t, *_: (0, 0, 0)) for x in blocks]
+    def own_at(r):
+        return lambda t, tp_index, table, spans: (table[part * cap + r], 0, 0)
+
+    in_specs = [pl.BlockSpec((1, width, nlen), own_at(r)) for r in range(ranks) for _ in own]
+    operands = list(own) * ranks
+    in_specs += [pl.BlockSpec(g.shape, lambda t, *_: (0, 0, 0, 0)) for g in got]
+    operands += list(got)
     in_specs += [pl.BlockSpec((windows.shape[0], SPAN, columns), lambda t, *_: (0, 0, t))]
-    operands = list(blocks) + [windows]
+    operands += [windows]
     for weight in weights:
         in_specs += [
             pl.BlockSpec((columns, features), lambda t, *_: (0, 0)),
@@ -251,26 +251,27 @@
     aliases = {}
     if held is not None:
         in_specs += [pl.BlockSpec(memory_space=pl.ANY)] * 2
-        aliases = {2 + len(operands): 0, 3 + len(operands): 1}
+        aliases = {3 + len(operands): 0, 4 + len(operands): 1}
         operands += list(held)
     kv = pltpu.VMEM((columns, cap * nlen), jnp.bfloat16)
 
     def body(*refs):
-        attend_kernel(cap, parts, steps, *refs)
+        attend_kernel(part, cap, ranks, pieces, steps, *refs)
 
     return pl.pallas_call(
         body,
         grid_spec=pltpu.PrefetchScalarGridSpec(
-            num_scalar_prefetch=2,
+            num_scalar_prefetch=3,
             grid=(steps,),
             in_specs=in_specs,
             out_specs=[
-                pl.BlockSpec((cap, SPAN, columns), lambda t, *_: (part_index, 0, t)),
-                pl.BlockSpec((cap, SPAN, LANES), lambda t, *_: (part_index, 0, 0)),
+                pl.BlockSpec((cap, SPAN, columns), lambda t, *_: (part, 0, t)),
+                pl.BlockSpec((cap, SPAN, LANES), lambda t, *_: (part, 0, 0)),
             ],
             scratch_shapes=[
                 pltpu.VMEM((features, cap * nlen), jnp.bfloat16),
-                pltpu.VMEM((2, 4 * SPAN, 2 * nlen), jnp.bfloat16),
+                pltpu.VMEM((2 * cap, 2 * SPAN, nlen), jnp.float32),
+                pltpu.VMEM((2 * cap, 2 * SPAN, nlen), jnp.bfloat16),
                 kv, kv, kv, kv,
             ],
         ),
@@ -281,7 +282,7 @@
         input_output_aliases=aliases,
         compiler_params=pltpu.CompilerParams(vmem_limit_bytes=VMEM_LIMIT),
         name="attend_part",
-    )(tp_index, spans, *operands)
+    )(*scalars, *operands)
 
 
 def spread_matrix(columns):
@@ -421,16 +422,27 @@
     ranks = (wants + seq_count - 1) // seq_count
     outer = seq_count // INNER
     slots = seq_count * ranks
+    cap = INNER * ranks
     own_index = lax.axis_index("seq")
     tp_index = lax.axis_index("tp").astype(jnp.int32).reshape(1)
-
-    own_ids = neighbour_ids.reshape(wants)
-    group_ids = jnp.stack([own_ids] + [swapped(own_ids, "seq", k) for k in range(1, INNER)])
 
     def all_features(part):
         if tp_count == 2:
             return [part, swapped(part, "tp", 1)]
         return [lax.all_gather(part, "tp", axis=1, tiled=True)]
+
+    def along(x, offset, senders):
+        pairs = [(i, i ^ offset) for i in range(seq_count) if i // INNER in senders]
+        return lax.ppermute(x, "seq", pairs)
+
+    near = swapped(neighbours, "seq", INNER)
+    across = along(neighbours, 3 * INNER, (1, 2)) if outer == 4 else near
+    own = all_features(neighbours)
+    own_ids = neighbour_ids.reshape(wants)
+    group_ids = jnp.stack([own_ids] + [swapped(own_ids, "seq", k) for k in range(1, INNER)])
+    incoming = passed_along(queries[:SPAN], "seq", -1)
+    weights = (key_weight.T, value_weight.T)
+    near, across = after((near, across), weights)
 
     group_sources = group_ids // block_count
     group_ranks = slot_ranks(group_sources)
@@ -439,7 +451,7 @@
         group_ranks[None, :, None, :] == jnp.arange(ranks)[None, None, :, None]
     )
     table = jnp.sum(jnp.where(hit, (group_ids % block_count)[None, :, None, :], 0), axis=-1)
-    table = table.astype(jnp.int32)
+    table = table.astype(jnp.int32).reshape(outer * cap)
 
     own_sources = own_ids // block_count
     places = ((own_sources ^ own_index) * ranks + slot_ranks(own_sources)).astype(jnp.int32)
@@ -447,61 +459,49 @@
     spans = jnp.sum(
         jnp.where(places[None, :] == jnp.arange(slots)[:, None], order[None, :] // 2, 0), axis=1
     ).astype(jnp.int32)
-    spans = spans.reshape(outer, INNER * ranks)
-
-    def along(x, offset, senders):
-        pairs = [(i, i ^ offset) for i in range(seq_count) if i // INNER in senders]
-        return lax.ppermute(x, "seq", pairs)
-
-    first = jnp.zeros((1,), jnp.int32)
-    held_parts = [([neighbours], first)]
-
-    def fetch(j, *others):
-        sources, which = held_parts[j]
-        picked = pick_blocks(which, after(table[j], *others), sources)
-        wanted = [picked[0]] + [swapped(picked[k], "seq", k) for k in range(1, INNER)]
-        return picked, jnp.concatenate(wanted, axis=0)
-
-    picked, wanted = fetch(0)
-    own_blocks, edge = after((neighbours, queries[:SPAN]), picked)
-    near = swapped(own_blocks, "seq", INNER)
+
+    def send(j, own, *others):
+        picked = pick_blocks(j, ranks, after(table, *others), own)
+        return picked, [swapped(picked[k - 1], "seq", k) for k in range(1, INNER)]
+
+    def attend(j, own, got, held, *others):
+        scalars = (tp_index, table, after(spans, *others))
+        return attend_part(j, cap, scalars, own, got, windows, weights, slots, held)
+
+    inside = (own_index // INNER == 1) | (own_index // INNER == 2)
     if outer == 4:
-        across = along(own_blocks, 3 * INNER, (1, 2))
-    incoming = passed_along(edge, "seq", -1)
-    weights = tuple(after(w, picked).T for w in (key_weight, value_weight))
-
-    if outer == 4:
-        near, across = after((near, across), weights)
-        outer_index = own_index // INNER
-        inside = ((outer_index == 1) | (outer_index == 2)).astype(jnp.int32).reshape(1)
         second = along(near, 3 * INNER, (1, 2))
         outward = along(across, INNER, (1, 2))
+    owns = [own, all_features(near)]
+    picked, got = send(0, own)
+    gots = [got]
+    windows = span_windows(after(queries, picked), incoming, span_count)
+    if outer == 4:
+        second, outward = after((second, outward), windows)
+        far = jnp.where(inside, second, outward)
         third = along(second, INNER, (1, 2))
-        held_parts += [([near], first), ([outward, second], inside), ([third, across], inside)]
     else:
-        held_parts.append(([near], first))
-        for j in range(2, outer):
+        far = swapped(near, "seq", 3 * INNER)
+    owns.append(all_features(far))
+    picked, got = send(1, owns[1], far)
+    gots.append(got)
+    held = attend(0, owns[0], gots[0], None, picked)
+    parts = [neighbours, near, far]
+    for j in range(3, outer):
+        if outer == 4:
+            part = jnp.where(inside, *after((across, third), held))
+        else:
             low = j & -j
-            part = swapped(held_parts[j ^ low][0][0], "seq", INNER * low)
-            held_parts.append(([part], first))
-
-    def attend(j, blocks, held, *others):
-        return attend_part(
-            tp_index, after(spans[j], *others), blocks, windows, weights, j, slots, held
-        )
-
-    held = None
-    blocks = [all_features(wanted)]
-    picked, wanted = fetch(1, wanted)
-    windows = span_windows(after(queries, picked), incoming, span_count)
-    for j in range(2, outer):
-        blocks.append(all_features(wanted))
-        picked, wanted_next = fetch(j, windows if held is None else held)
-        held = attend(j - 2, blocks[j - 2], held, picked, wanted)
-        wanted = wanted_next
-    blocks.append(all_features(wanted))
-    held = attend(outer - 2, blocks[outer - 2], held, wanted)
-    held = attend(outer - 1, blocks[outer - 1], held)
+            part = swapped(after(parts[j ^ low], held), "seq", INNER * low)
+        parts.append(part)
+        owns.append(all_features(part))
+        picked, got = send(j - 1, owns[j - 1], part)
+        gots.append(got)
+        held = attend(j - 2, owns[j - 2], gots[j - 2], held, picked)
+    picked, got = send(outer - 1, owns[outer - 1], held)
+    gots.append(got)
+    held = attend(outer - 2, owns[outer - 2], gots[outer - 2], held, picked)
+    held = attend(outer - 1, owns[outer - 1], gots[outer - 1], held)
 
     partials, log_totals = held
     last = mix_last(places, partials, log_totals, span_count)

time: 211 us -> 211 us (level)
  waiting for transfers between devices: 28.1 us -> 36.6 us
  starting transfers between devices: 50.7 us -> 44.3 us
  other arithmetic: 0.88 us -> 3.96 us
    optimization_barrier x6 -> x0, local copies, waits for them, and re-layouts: 14.9 us -> none  [after(): return lax.optimization_barrier((values, others))[0]]
    unnamed x43 -> x49, local copies, waits for them, and re-layouts: 7.4 us -> 20.3 us
    ppermute x20, starting transfers between devices: 40.9 us -> 33.6 us  [swapped(): return lax.ppermute(x, axis, [(i, i ^ offset) for i in range(peers)])]
    ppermute x4, waiting for transfers between devices: 0.01 us -> 6.75 us  [along(): return lax.ppermute(x, 'seq', pairs)]
    select_n x0 -> x2, other arithmetic: none -> 2.57 us  [the longest x1 1.29 us: shards(): part = jnp.where(inside, *after((across, third), held))]
  transfers between devices with their start and end apart: 26 -> 26, of which waited for: 7 -> 7; matrix products, arithmetic and copies ran while one was open for 9% -> 9% of each run, Pallas kernels for 37% -> 38%
where the time goes in v5:
time: 211 us; the launch traced here: 209 us
  Pallas kernels  102 us (48%)
  starting transfers between devices  44.3 us (21%)
  waiting for transfers between devices  36.6 us (17%)
  local copies, waits for them, and re-layouts  22.1 us (10%)
  other arithmetic  3.96 us (2%)
    pallas_call x4, Pallas kernels, attend_part(): pl.pallas_call(body, grid_spec=pltpu.PrefetchScalarGridSpec(num_scalar_pr...  72.1 us
    ppermute x20, starting transfers between devices, swapped(): return lax.ppermute(x, axis, [(i, i ^ offset) for i in range(peers)])  33.6 us
    ppermute x20, waiting for transfers between devices, swapped(): return lax.ppermute(x, axis, [(i, i ^ offset) for i in range(peers)])  29.8 us
    unnamed x49, local copies, waits for them, and re-layouts  20.3 us
    pallas_call x4, Pallas kernels, pick_blocks(): pl.pallas_call(body, grid_spec=pltpu.PrefetchScalarGridSpec(num_scalar_pr...  12.1 us
    pallas_call x1, Pallas kernels, mix(): pl.pallas_call(mix_kernel, grid_spec=pltpu.PrefetchScalarGridSpec(num_sca...  8.24 us
    ppermute x4, waiting for transfers between devices, along(): return lax.ppermute(x, 'seq', pairs)  6.75 us
    ppermute x4, starting transfers between devices, along(): return lax.ppermute(x, 'seq', pairs)  5.73 us
  transfers between devices with their start and end apart: 26, of which 7 were waited for; matrix products, arithmetic and copies ran while one was open for 9% of the time, Pallas kernels for 38%

profile of v5, /device:TPU:1, one launch (start us, length us, event | category | flops | bytes accessed | tf_op | source)
XLA Modules:
  0.0 209.3 jit_solution(3419893824187933227)
XLA Ops:
  8.0 6.1 %copy.24 = bf16[896,2048]{0,1:T(8,128)(2,1)} copy(bf16[896,2048]{1,0:T(8,128)(2,1)} %param.7) | data formatting | bytes 7340032 | tf_op args[2]
  14.1 6.1 %copy.25 = bf16[896,2048]{0,1:T(8,128)(2,1)} copy(bf16[896,2048]{1,0:T(8,128)(2,1)} %param.8) | data formatting | bytes 7340032 | tf_op args[3]
  20.2 2.2 %collective-permute-done.3.refs_1_.refs_3_.refs_5_ = bf16[8,448,128]{2,1,0:T(8,128)(2,1)S(1)} collective-permute-done((bf16[8,448,128]{2,1,0:T(8,128)(2,1)}, bf16[8,448,128]{2,1,0:T(8,128)(2,1)S(1)}, u32[]{:S(2)}, u32[]{:S(2)}) %collective-permute-start.3) | collective-permute-done | bytes 917536 | tf_op jit(solution)/shard_map/ppermute | solution.py:24
  26.4 2.6 %collective-permute-start.2 = (s32[32]{0:T(128)S(1)}, s32[32]{0:T(128)S(1)}, u32[]{:S(2)}, u32[]{:S(2)}) collective-permute-start(s32[32]{0:T(128)S(1)} %reshape.595), channel_id=1, source_target_pairs={{0,6},{2,4},{4,2},{6,0},{8,14},{10,12},{12,10},{14,8},{16,22},{18,... | collective-permute-start | bytes 392 | tf_op jit(solution)/shard_map/ppermute | solution.py:24
  34.4 3.0 %pick_blocks.4 = (bf16[2,2,448,128]{3,2,1,0:T(8,128)(2,1)}, bf16[2,2,448,128]{3,2,1,0:T(8,128)(2,1)}, bf16[2,2,448,128]{3,2,1,0:T(8,128)(2,1)}) custom-call(s32[32]{0:T(128)} %reshape.597.refs_0_.refs_1_, bf16[8,448,128]{2,1,0:T(8,128)(2,1)} %refs_5_.1, bf16[8,448,128]{2,1,0:T(8,128)(2,1)} %copy-done.6), custom_call_target="tpu_custom_call" | custom-call | tf_op jit(solution)/shard_map/pick_blocks/pallas_call | solution.py:107
  38.1 5.0 %windows.1.refs_10_ = bf16[16,64,2048]{2,1,0:T(8,128)(2,1)} custom-call(bf16[1024,2048]{1,0:T(8,128)(2,1)} %next_ref, bf16[1024,2048]{1,0:T(8,128)(2,1)} %next_ref, bf16[64,2048]{1,0:T(8,128)(2,1)} %copy-done.17), custom_call_target="tpu_custom_call" | custom-call | tf_op jit(solution)/shard_map/windows/pallas_call | solution.py:56
  43.1 6.7 %collective-permute-done.6 = bf16[8,448,128]{2,1,0:T(8,128)(2,1)} collective-permute-done((bf16[8,448,128]{2,1,0:T(8,128)(2,1)}, bf16[8,448,128]{2,1,0:T(8,128)(2,1)}, u32[]{:S(2)}, u32[]{:S(2)}) %collective-permute-start.6) | collective-permute-done | bytes 917536 | tf_op jit(solution)/shard_map/ppermute | solution.py:436
  51.4 2.9 %collective-permute-start.11 = (bf16[2,2,448,128]{3,2,1,0:T(8,128)(2,1)}, bf16[2,2,448,128]{3,2,1,0:T(8,128)(2,1)S(1)}, u32[]{:S(2)}, u32[]{:S(2)}) collective-permute-start(bf16[2,2,448,128]{3,2,1,0:T(8,128)(2,1)} %get-tuple-element.40), channel_id=1, source_target_pairs={{0,2},{2,0},{4,6},{6,4},{8,10},{10,8},{12,14},{14,12},{16,18},{18,... | collective-permute-start | bytes 1376264 | tf_op jit(solution)/shard_map/ppermute | solution.py:24
  54.2 9.2 %collective-permute-start.12 = (bf16[2,2,448,128]{3,2,1,0:T(8,128)(2,1)}, bf16[2,2,448,128]{3,2,1,0:T(8,128)(2,1)}, u32[]{:S(2)}, u32[]{:S(2)}) collective-permute-start(bf16[2,2,448,128]{3,2,1,0:T(8,128)(2,1)} %get-tuple-element.41), channel_id=1, source_target_pairs={{0,4},{2,6},{4,0},{6,2},{8,12},{10,14},{12,8},{14,10},{16,20},{18,... | collective-permute-start | bytes 1376264 | tf_op jit(solution)/shard_map/ppermute | solution.py:24
  67.0 3.0 %pick_blocks.5 = (bf16[2,2,448,128]{3,2,1,0:T(8,128)(2,1)}, bf16[2,2,448,128]{3,2,1,0:T(8,128)(2,1)}, bf16[2,2,448,128]{3,2,1,0:T(8,128)(2,1)}) custom-call(s32[32]{0:T(128)} %reshape.597.refs_0_.refs_1_, bf16[8,448,128]{2,1,0:T(8,128)(2,1)} %copy-done.2, bf16[8,448,128]{2,1,0:T(8,128)(2,1)} %copy-done.3), custom_call_target="tpu_custom_call" | custom-call | tf_op jit(solution)/shard_map/pick_blocks/pallas_call | solution.py:107
  70.1 4.2 %collective-permute-done.12.refs_8_ = bf16[2,2,448,128]{3,2,1,0:T(8,128)(2,1)} collective-permute-done((bf16[2,2,448,128]{3,2,1,0:T(8,128)(2,1)}, bf16[2,2,448,128]{3,2,1,0:T(8,128)(2,1)}, u32[]{:S(2)}, u32[]{:S(2)}) %collective-permute-start.12) | collective-permute-done | bytes 458784 | tf_op jit(solution)/shard_map/ppermute | solution.py:24
  74.3 10.3 %collective-permute-done.13.refs_9_ = bf16[2,2,448,128]{3,2,1,0:T(8,128)(2,1)} collective-permute-done((bf16[2,2,448,128]{3,2,1,0:T(8,128)(2,1)}, bf16[2,2,448,128]{3,2,1,0:T(8,128)(2,1)}, u32[]{:S(2)}, u32[]{:S(2)}) %collective-permute-start.13) | collective-permute-done | bytes 458784 | tf_op jit(solution)/shard_map/ppermute | solution.py:24
  84.6 18.0 %attend_part.4 = (bf16[32,64,2048]{2,1,0:T(8,128)(2,1)}, f32[32,64,128]{2,1,0:T(8,128)}) custom-call(s32[1]{0:T(128)} %bitcast.refs_0_, s32[32]{0:T(128)} %reshape.597.refs_0_.refs_1_, s32[32]{0:T(128)} %select_reduce_fusion.1.refs_2_, bf16[8,448,128]{2,1,0:T(8,128)(2,1)} %refs_5_.1, bf16[8,448,128]{2,1,0:T(8,128)(2,1)} %copy-done.6, ...), custom_call_target="tpu_custom_call" | custom-call | tf_op jit(solution)/shard_map/attend_part/pallas_call | solution.py:261
  108.2 3.2 %pick_blocks.6 = (bf16[2,2,448,128]{3,2,1,0:T(8,128)(2,1)}, bf16[2,2,448,128]{3,2,1,0:T(8,128)(2,1)}, bf16[2,2,448,128]{3,2,1,0:T(8,128)(2,1)}) custom-call(s32[32]{0:T(128)} %reshape.597.refs_0_.refs_1_, bf16[8,448,128]{2,1,0:T(8,128)(2,1)} %copy-done, bf16[8,448,128]{2,1,0:T(8,128)(2,1)} %copy-done.4), custom_call_target="tpu_custom_call" | custom-call | tf_op jit(solution)/shard_map/pick_blocks/pallas_call | solution.py:107
  112.8 4.5 %collective-permute-done.17.refs_8_ = bf16[2,2,448,128]{3,2,1,0:T(8,128)(2,1)S(1)} collective-permute-done((bf16[2,2,448,128]{3,2,1,0:T(8,128)(2,1)S(1)}, bf16[2,2,448,128]{3,2,1,0:T(8,128)(2,1)S(1)}, u32[]{:S(2)}, u32[]{:S(2)}) %collective-permute-start.17) | collective-permute-done | bytes 458784 | tf_op jit(solution)/shard_map/ppermute | solution.py:24
  117.3 3.1 %collective-permute-start.24 = (bf16[2,2,448,128]{3,2,1,0:T(8,128)(2,1)}, bf16[2,2,448,128]{3,2,1,0:T(8,128)(2,1)S(1)}, u32[]{:S(2)}, u32[]{:S(2)}) collective-permute-start(bf16[2,2,448,128]{3,2,1,0:T(8,128)(2,1)} %get-tuple-element.58), channel_id=1, source_target_pairs={{0,6},{2,4},{4,2},{6,0},{8,14},{10,12},{12,10},{14,8},{16,22},{18,... | collective-permute-start | bytes 1376264 | tf_op jit(solution)/shard_map/ppermute | solution.py:24
  120.4 7.8 %collective-permute-done.18.refs_9_ = bf16[2,2,448,128]{3,2,1,0:T(8,128)(2,1)S(1)} collective-permute-done((bf16[2,2,448,128]{3,2,1,0:T(8,128)(2,1)S(1)}, bf16[2,2,448,128]{3,2,1,0:T(8,128)(2,1)S(1)}, u32[]{:S(2)}, u32[]{:S(2)}) %collective-permute-start.18) | collective-permute-done | bytes 458784 | tf_op jit(solution)/shard_map/ppermute | solution.py:24
  129.0 18.0 %attend_part.5 = (bf16[32,64,2048]{2,1,0:T(8,128)(2,1)}, f32[32,64,128]{2,1,0:T(8,128)}) custom-call(s32[1]{0:T(128)} %bitcast.refs_0_, s32[32]{0:T(128)} %reshape.597.refs_0_.refs_1_, s32[32]{0:T(128)} %select_reduce_fusion.1.refs_2_, bf16[8,448,128]{2,1,0:T(8,128)(2,1)} %copy-done.2, ...), custom_call_target="tpu_custom_call", output_to_operand_aliasing={{0}: (15, {}), {1}: (16, {})} | custom-call | tf_op jit(solution)/shard_map/attend_part/pallas_call | solution.py:261
  147.9 3.0 %pick_blocks.7 = (bf16[2,2,448,128]{3,2,1,0:T(8,128)(2,1)}, bf16[2,2,448,128]{3,2,1,0:T(8,128)(2,1)}, bf16[2,2,448,128]{3,2,1,0:T(8,128)(2,1)}) custom-call(s32[32]{0:T(128)} %reshape.597.refs_0_.refs_1_, bf16[8,448,128]{2,1,0:T(8,128)(2,1)} %copy-done.1, bf16[8,448,128]{2,1,0:T(8,128)(2,1)} %copy-done.5), custom_call_target="tpu_custom_call" | custom-call | tf_op jit(solution)/shard_map/pick_blocks/pallas_call | solution.py:107
  155.0 18.0 %attend_part.6 = (bf16[32,64,2048]{2,1,0:T(8,128)(2,1)}, f32[32,64,128]{2,1,0:T(8,128)}) custom-call(s32[1]{0:T(128)} %bitcast.refs_0_, s32[32]{0:T(128)} %reshape.597.refs_0_.refs_1_, s32[32]{0:T(128)} %select_reduce_fusion.1.refs_2_, bf16[8,448,128]{2,1,0:T(8,128)(2,1)} %copy-done, ...), custom_call_target="tpu_custom_call", output_to_operand_aliasing={{0}: (15, {}), {1}: (16, {})} | custom-call | tf_op jit(solution)/shard_map/attend_part/pallas_call | solution.py:261
  174.6 18.1 %attend_part.7 = (bf16[32,64,2048]{2,1,0:T(8,128)(2,1)}, f32[32,64,128]{2,1,0:T(8,128)}) custom-call(s32[1]{0:T(128)} %bitcast.refs_0_, s32[32]{0:T(128)} %reshape.597.refs_0_.refs_1_, s32[32]{0:T(128)} %select_reduce_fusion.1.refs_2_, bf16[8,448,128]{2,1,0:T(8,128)(2,1)} %copy-done.1, ...), custom_call_target="tpu_custom_call", output_to_operand_aliasing={{0}: (15, {}), {1}: (16, {})} | custom-call | tf_op jit(solution)/shard_map/attend_part/pallas_call | solution.py:261
  192.8 2.8 %mix_last.1 = bf16[64,2048]{1,0:T(8,128)(2,1)} custom-call(s32[32]{0:T(128)} %copy-done.19, bf16[32,64,2048]{2,1,0:T(8,128)(2,1)} %get-tuple-element.69.p0.p1.refs_0_.refs_1_.refs_4_.refs_5_.refs_8_.refs_9_.refs_12_.refs_13_, bf16[32,64,2048]{2,1,0:T(8,128)(2,1)} %get-tuple-element.69.p0.p1.refs_0_.refs_1_.refs_4_.refs_5_.refs_8_.refs_9_.refs_12_.refs_13_, ...), custom_call_target="tpu_custom_call" | custom-call | tf_op jit(solution)/shard_map/mix_last/pallas_call | solution.py:355
  195.5 3.1 %collective-permute-start.25 = (bf16[64,2048]{1,0:T(8,128)(2,1)}, bf16[64,2048]{1,0:T(8,128)(2,1)S(1)}, u32[]{:S(2)}, u32[]{:S(2)}) collective-permute-start(bf16[64,2048]{1,0:T(8,128)(2,1)} %mix_last.1), channel_id=1, source_target_pairs={{0,2},{2,4},{4,6},{6,8},{8,10},{10,12},{12,14},{14,16},{16,18},{18... | collective-permute-start | bytes 786440 | tf_op jit(solution)/shard_map/ppermute | solution.py:19
  198.6 8.2 %mix.1.rows = bf16[1024,2048]{1,0:T(8,128)(2,1)} custom-call(s32[32]{0:T(128)} %copy-done.19, bf16[32,64,2048]{2,1,0:T(8,128)(2,1)} %get-tuple-element.69.p0.p1.refs_0_.refs_1_.refs_4_.refs_5_.refs_8_.refs_9_.refs_12_.refs_13_, bf16[32,64,2048]{2,1,0:T(8,128)(2,1)} %get-tuple-element.69.p0.p1.refs_0_.refs_1_.refs_4_.refs_5_.refs_8_.refs_9_.refs_12_.refs_13_, ...), custom_call_target="tpu_custom_call" | custom-call | tf_op jit(solution)/shard_map/mix/pallas_call | solution.py:375
  (108 shorter events, 40.0 us)
Async XLA Ops:
  0.0 22.4 %collective-permute-start.3 = (bf16[8,448,128]{2,1,0:T(8,128)(2,1)}, bf16[8,448,128]{2,1,0:T(8,128)(2,1)S(1)}, u32[]{:S(2)}, u32[]{:S(2)}) collective-permute-start(bf16[8,448,128]{2,1,0:T(8,128)(2,1)} %refs_5_.1), channel_id=1, source_target_pairs={{0,8},{2,10},{4,12},{6,14},{8,0},{10,2},{12,4},{14,6},{16,24},{18,... | collective-permute-start | bytes 2752520 | tf_op jit(solution)/shard_map/ppermute | solution.py:24
  2.1 20.3 %collective-permute-start.4 = (bf16[8,448,128]{2,1,0:T(8,128)(2,1)}, bf16[8,448,128]{2,1,0:T(8,128)(2,1)}, u32[]{:S(2)}, u32[]{:S(2)}) collective-permute-start(bf16[8,448,128]{2,1,0:T(8,128)(2,1)} %refs_5_.1), channel_id=1, source_target_pairs={{8,16},{10,18},{12,20},{14,22},{16,8},{18,10},{20,12},{22,14},{9,1... | collective-permute-start | bytes 2752520 | tf_op jit(solution)/shard_map/ppermute | solution.py:436
  4.6 21.8 %collective-permute-start = (s32[32]{0:T(128)S(1)}, s32[32]{0:T(128)S(1)}, u32[]{:S(2)}, u32[]{:S(2)}) collective-permute-start(s32[32]{0:T(128)S(1)} %reshape.595), channel_id=1, source_target_pairs={{0,2},{2,0},{4,6},{6,4},{8,10},{10,8},{12,14},{14,12},{16,18},{18,... | collective-permute-start | bytes 392 | tf_op jit(solution)/shard_map/ppermute | solution.py:24
  5.6 23.4 %collective-permute-start.1 = (s32[32]{0:T(128)S(1)}, s32[32]{0:T(128)S(1)}, u32[]{:S(2)}, u32[]{:S(2)}) collective-permute-start(s32[32]{0:T(128)S(1)} %reshape.595), channel_id=1, source_target_pairs={{0,4},{2,6},{4,0},{6,2},{8,12},{10,14},{12,8},{14,10},{16,20},{18,... | collective-permute-start | bytes 392 | tf_op jit(solution)/shard_map/ppermute | solution.py:24
  6.8 26.6 %collective-permute-start.7 = (bf16[8,448,128]{2,1,0:T(8,128)(2,1)}, bf16[8,448,128]{2,1,0:T(8,128)(2,1)S(1)}, u32[]{:S(2)}, u32[]{:S(2)}) collective-permute-start(bf16[8,448,128]{2,1,0:T(8,128)(2,1)} %refs_5_.1), channel_id=1, source_target_pairs={{0,1},{1,0},{2,3},{3,2},{4,5},{5,4},{6,7},{7,6},{8,9},{9,8},{10,11... | collective-permute-start | bytes 2752520 | tf_op jit(solution)/shard_map/ppermute | solution.py:24
  22.4 20.7 %collective-permute-start.5 = (bf16[8,448,128]{2,1,0:T(8,128)(2,1)S(1)}, bf16[8,448,128]{2,1,0:T(8,128)(2,1)}, u32[]{:S(2)}, u32[]{:S(2)}) collective-permute-start(bf16[8,448,128]{2,1,0:T(8,128)(2,1)S(1)} %collective-permute-done.3.refs_1_.refs_3_.refs_5_), channel_id=1, source_target_pairs={{8,16},{10,18},{12,20},{14,22},{16,8},{18,10},{20,12},{22,14},{9,1... | collective-permute-start | bytes 2752520 | tf_op jit(solution)/shard_map/ppermute | solution.py:436
  24.0 25.8 %collective-permute-start.6 = (bf16[8,448,128]{2,1,0:T(8,128)(2,1)}, bf16[8,448,128]{2,1,0:T(8,128)(2,1)}, u32[]{:S(2)}, u32[]{:S(2)}) collective-permute-start(bf16[8,448,128]{2,1,0:T(8,128)(2,1)} %collective-permute-done.4), channel_id=1, source_target_pairs={{8,0},{10,2},{12,4},{14,6},{16,24},{18,26},{20,28},{22,30},{9,1},{... | collective-permute-start | bytes 2752520 | tf_op jit(solution)/shard_map/ppermute | solution.py:436
  29.0 8.4 %collective-permute-start.8 = (bf16[64,2048]{1,0:T(8,128)(2,1)S(1)}, bf16[64,2048]{1,0:T(8,128)(2,1)S(1)}, u32[]{:S(2)}, u32[]{:S(2)}) collective-permute-start(bf16[64,2048]{1,0:T(8,128)(2,1)S(1)} %slice.3), channel_id=1, source_target_pairs={{2,0},{4,2},{6,4},{8,6},{10,8},{12,10},{14,12},{16,14},{18,16},{20... | collective-permute-start | bytes 786440 | tf_op jit(solution)/shard_map/ppermute | solution.py:19
  31.2 33.9 %collective-permute-start.10 = (bf16[8,448,128]{2,1,0:T(8,128)(2,1)S(1)}, bf16[8,448,128]{2,1,0:T(8,128)(2,1)S(1)}, u32[]{:S(2)}, u32[]{:S(2)}) collective-permute-start(bf16[8,448,128]{2,1,0:T(8,128)(2,1)S(1)} %collective-permute-done.3.refs_1_.refs_3_.refs_5_), channel_id=1, source_target_pairs={{0,1},{1,0},{2,3},{3,2},{4,5},{5,4},{6,7},{7,6},{8,9},{9,8},{10,11... | collective-permute-start | bytes 2752520 | tf_op jit(solution)/shard_map/ppermute | solution.py:24
  49.8 52.8 %collective-permute-start.9 = (bf16[8,448,128]{2,1,0:T(8,128)(2,1)}, bf16[8,448,128]{2,1,0:T(8,128)(2,1)}, u32[]{:S(2)}, u32[]{:S(2)}) collective-permute-start(bf16[8,448,128]{2,1,0:T(8,128)(2,1)} %collective-permute-done.5), channel_id=1, source_target_pairs={{8,0},{10,2},{12,4},{14,6},{16,24},{18,26},{20,28},{22,30},{9,1},{... | collective-permute-start | bytes 2752520 | tf_op jit(solution)/shard_map/ppermute | solution.py:436
  51.4 18.7 %collective-permute-start.11 = (bf16[2,2,448,128]{3,2,1,0:T(8,128)(2,1)}, bf16[2,2,448,128]{3,2,1,0:T(8,128)(2,1)S(1)}, u32[]{:S(2)}, u32[]{:S(2)}) collective-permute-start(bf16[2,2,448,128]{3,2,1,0:T(8,128)(2,1)} %get-tuple-element.40), channel_id=1, source_target_pairs={{0,2},{2,0},{4,6},{6,4},{8,10},{10,8},{12,14},{14,12},{16,18},{18,... | collective-permute-start | bytes 1376264 | tf_op jit(solution)/shard_map/ppermute | solution.py:24
  54.2 20.1 %collective-permute-start.12 = (bf16[2,2,448,128]{3,2,1,0:T(8,128)(2,1)}, bf16[2,2,448,128]{3,2,1,0:T(8,128)(2,1)}, u32[]{:S(2)}, u32[]{:S(2)}) collective-permute-start(bf16[2,2,448,128]{3,2,1,0:T(8,128)(2,1)} %get-tuple-element.41), channel_id=1, source_target_pairs={{0,4},{2,6},{4,0},{6,2},{8,12},{10,14},{12,8},{14,10},{16,20},{18,... | collective-permute-start | bytes 1376264 | tf_op jit(solution)/shard_map/ppermute | solution.py:24
  63.4 21.1 %collective-permute-start.13 = (bf16[2,2,448,128]{3,2,1,0:T(8,128)(2,1)}, bf16[2,2,448,128]{3,2,1,0:T(8,128)(2,1)}, u32[]{:S(2)}, u32[]{:S(2)}) collective-permute-start(bf16[2,2,448,128]{3,2,1,0:T(8,128)(2,1)} %get-tuple-element.42), channel_id=1, source_target_pairs={{0,6},{2,4},{4,2},{6,0},{8,14},{10,12},{12,10},{14,8},{16,22},{18,... | collective-permute-start | bytes 1376264 | tf_op jit(solution)/shard_map/ppermute | solution.py:24
  65.1 42.2 %collective-permute-start.15 = (bf16[8,448,128]{2,1,0:T(8,128)(2,1)S(1)}, bf16[8,448,128]{2,1,0:T(8,128)(2,1)S(1)}, u32[]{:S(2)}, u32[]{:S(2)}) collective-permute-start(bf16[8,448,128]{2,1,0:T(8,128)(2,1)S(1)} %broadcast_select_fusion.1.refs_1_.refs_3_.refs_5_), channel_id=1, source_target_pairs={{0,1},{1,0},{2,3},{3,2},{4,5},{5,4},{6,7},{7,6},{8,9},{9,8},{10,11... | collective-permute-start | bytes 2752520 | tf_op jit(solution)/shard_map/ppermute | solution.py:24
  103.9 43.0 %collective-permute-start.14 = (bf16[8,448,128]{2,1,0:T(8,128)(2,1)S(1)}, bf16[8,448,128]{2,1,0:T(8,128)(2,1)S(1)}, u32[]{:S(2)}, u32[]{:S(2)}) collective-permute-start(bf16[8,448,128]{2,1,0:T(8,128)(2,1)S(1)} %broadcast_select_fusion.refs_1_.refs_3_.refs_5_), channel_id=1, source_target_pairs={{0,1},{1,0},{2,3},{3,2},{4,5},{5,4},{6,7},{7,6},{8,9},{9,8},{10,11... | collective-permute-start | bytes 2752520 | tf_op jit(solution)/shard_map/ppermute | solution.py:24
  105.4 11.9 %collective-permute-start.17 = (bf16[2,2,448,128]{3,2,1,0:T(8,128)(2,1)S(1)}, bf16[2,2,448,128]{3,2,1,0:T(8,128)(2,1)S(1)}, u32[]{:S(2)}, u32[]{:S(2)}) collective-permute-start(bf16[2,2,448,128]{3,2,1,0:T(8,128)(2,1)S(1)} %copy-done.21), channel_id=1, source_target_pairs={{0,4},{2,6},{4,0},{6,2},{8,12},{10,14},{12,8},{14,10},{16,20},{18,... | collective-permute-start | bytes 1376264 | tf_op jit(solution)/shard_map/ppermute | solution.py:24
  106.7 21.5 %collective-permute-start.18 = (bf16[2,2,448,128]{3,2,1,0:T(8,128)(2,1)S(1)}, bf16[2,2,448,128]{3,2,1,0:T(8,128)(2,1)S(1)}, u32[]{:S(2)}, u32[]{:S(2)}) collective-permute-start(bf16[2,2,448,128]{3,2,1,0:T(8,128)(2,1)S(1)} %copy-done.20), channel_id=1, source_target_pairs={{0,6},{2,4},{4,2},{6,0},{8,14},{10,12},{12,10},{14,8},{16,22},{18,... | collective-permute-start | bytes 1376264 | tf_op jit(solution)/shard_map/ppermute | solution.py:24
  111.5 41.6 %collective-permute-start.22 = (bf16[2,2,448,128]{3,2,1,0:T(8,128)(2,1)}, bf16[2,2,448,128]{3,2,1,0:T(8,128)(2,1)S(1)}, u32[]{:S(2)}, u32[]{:S(2)}) collective-permute-start(bf16[2,2,448,128]{3,2,1,0:T(8,128)(2,1)} %get-tuple-element.56), channel_id=1, source_target_pairs={{0,2},{2,0},{4,6},{6,4},{8,10},{10,8},{12,14},{14,12},{16,18},{18,... | collective-permute-start | bytes 1376264 | tf_op jit(solution)/shard_map/ppermute | solution.py:24
  111.6 41.9 %collective-permute-start.23 = (bf16[2,2,448,128]{3,2,1,0:T(8,128)(2,1)}, bf16[2,2,448,128]{3,2,1,0:T(8,128)(2,1)S(1)}, u32[]{:S(2)}, u32[]{:S(2)}) collective-permute-start(bf16[2,2,448,128]{3,2,1,0:T(8,128)(2,1)} %get-tuple-element.57), channel_id=1, source_target_pairs={{0,4},{2,6},{4,0},{6,2},{8,12},{10,14},{12,8},{14,10},{16,20},{18,... | collective-permute-start | bytes 1376264 | tf_op jit(solution)/shard_map/ppermute | solution.py:24
  117.3 36.2 %collective-permute-start.24 = (bf16[2,2,448,128]{3,2,1,0:T(8,128)(2,1)}, bf16[2,2,448,128]{3,2,1,0:T(8,128)(2,1)S(1)}, u32[]{:S(2)}, u32[]{:S(2)}) collective-permute-start(bf16[2,2,448,128]{3,2,1,0:T(8,128)(2,1)} %get-tuple-element.58), channel_id=1, source_target_pairs={{0,6},{2,4},{4,2},{6,0},{8,14},{10,12},{12,10},{14,8},{16,22},{18,... | collective-permute-start | bytes 1376264 | tf_op jit(solution)/shard_map/ppermute | solution.py:24
  150.9 22.2 %collective-permute-start.19 = (bf16[2,2,448,128]{3,2,1,0:T(8,128)(2,1)}, bf16[2,2,448,128]{3,2,1,0:T(8,128)(2,1)S(1)}, u32[]{:S(2)}, u32[]{:S(2)}) collective-permute-start(bf16[2,2,448,128]{3,2,1,0:T(8,128)(2,1)} %get-tuple-element.63), channel_id=1, source_target_pairs={{0,2},{2,0},{4,6},{6,4},{8,10},{10,8},{12,14},{14,12},{16,18},{18,... | collective-permute-start | bytes 1376264 | tf_op jit(solution)/shard_map/ppermute | solution.py:24
  151.2 21.9 %collective-permute-start.20 = (bf16[2,2,448,128]{3,2,1,0:T(8,128)(2,1)}, bf16[2,2,448,128]{3,2,1,0:T(8,128)(2,1)S(1)}, u32[]{:S(2)}, u32[]{:S(2)}) collective-permute-start(bf16[2,2,448,128]{3,2,1,0:T(8,128)(2,1)} %get-tuple-element.64), channel_id=1, source_target_pairs={{0,4},{2,6},{4,0},{6,2},{8,12},{10,14},{12,8},{14,10},{16,20},{18,... | collective-permute-start | bytes 1376264 | tf_op jit(solution)/shard_map/ppermute | solution.py:24
  153.1 20.8 %collective-permute-start.21 = (bf16[2,2,448,128]{3,2,1,0:T(8,128)(2,1)}, bf16[2,2,448,128]{3,2,1,0:T(8,128)(2,1)S(1)}, u32[]{:S(2)}, u32[]{:S(2)}) collective-permute-start(bf16[2,2,448,128]{3,2,1,0:T(8,128)(2,1)} %get-tuple-element.65), channel_id=1, source_target_pairs={{0,6},{2,4},{4,2},{6,0},{8,14},{10,12},{12,10},{14,8},{16,22},{18,... | collective-permute-start | bytes 1376264 | tf_op jit(solution)/shard_map/ppermute | solution.py:24
  195.5 11.3 %collective-permute-start.25 = (bf16[64,2048]{1,0:T(8,128)(2,1)}, bf16[64,2048]{1,0:T(8,128)(2,1)S(1)}, u32[]{:S(2)}, u32[]{:S(2)}) collective-permute-start(bf16[64,2048]{1,0:T(8,128)(2,1)} %mix_last.1), channel_id=1, source_target_pairs={{0,2},{2,4},{4,6},{6,8},{8,10},{10,12},{12,14},{14,16},{16,18},{18... | collective-permute-start | bytes 786440 | tf_op jit(solution)/shard_map/ppermute | solution.py:19
  (25 other events, 280.7 us)

commit v6 on v5

--- a/solution.py
+++ b/solution.py
@@ -11,6 +11,10 @@
 INNER = 4
 LANES = 128
 VMEM_LIMIT = 56 * 1024 * 1024
+
+
+LIGHT = pl.CostEstimate(flops=1000, bytes_accessed=1000, transcendentals=0)
+HEAVY = pl.CostEstimate(flops=20 * 10**9, bytes_accessed=10**7, transcendentals=0)
 
 
 def passed_along(x, axis, by):
@@ -66,26 +70,25 @@
         out_specs=pl.BlockSpec((per, SPAN, columns), lambda u: (u, 0, 0)),
         out_shape=jax.ShapeDtypeStruct((span_count, SPAN, columns), jnp.bfloat16),
         compiler_params=pltpu.CompilerParams(vmem_limit_bytes=VMEM_LIMIT),
+        cost_estimate=LIGHT,
         name="windows",
     )(queries, queries, incoming)
 
 
 def pick_kernel(part, ranks, table, *refs):
-    count = INNER - 1
-    pieces = len(refs) - count - 3
-    sources, outs = refs[:pieces], refs[pieces : pieces + count]
+    sources, outs = refs[:2], refs[2:4]
     held, in_sems, out_sems = refs[-3:]
     fetches, stores = [], []
-    for k in range(1, INNER):
-        for r in range(ranks):
-            block = table[(part * INNER + k) * ranks + r]
-            for piece in range(pieces):
+    for e in range(2):
+        for a in range(2):
+            for r in range(ranks):
                 n = len(fetches)
+                block = table[((part * 2 + e) * 2 + a) * ranks + r]
                 fetches.append(
-                    pltpu.make_async_copy(sources[piece].at[block], held.at[n], in_sems.at[n])
+                    pltpu.make_async_copy(sources[a].at[block], held.at[n], in_sems.at[n])
                 )
                 stores.append(
-                    pltpu.make_async_copy(held.at[n], outs[k - 1].at[r, piece], out_sems.at[n])
+                    pltpu.make_async_copy(held.at[n], outs[e].at[a * ranks + r], out_sems.at[n])
                 )
     for fetch in fetches:
         fetch.start()
@@ -98,8 +101,7 @@
 
 def pick_blocks(part, ranks, table, sources):
     shape = sources[0].shape[1:]
-    pieces = len(sources)
-    copies = (INNER - 1) * ranks * pieces
+    copies = 4 * ranks
 
     def body(*refs):
         pick_kernel(part, ranks, *refs)
@@ -109,27 +111,24 @@
         grid_spec=pltpu.PrefetchScalarGridSpec(
             num_scalar_prefetch=1,
             grid=(1,),
-            in_specs=[pl.BlockSpec(memory_space=pl.ANY)] * pieces,
-            out_specs=[pl.BlockSpec(memory_space=pl.ANY)] * (INNER - 1),
+            in_specs=[pl.BlockSpec(memory_space=pltpu.HBM)] * 2,
+            out_specs=[pl.BlockSpec(memory_space=pltpu.HBM)] * 2,
             scratch_shapes=[
                 pltpu.VMEM((copies,) + shape, sources[0].dtype),
                 pltpu.SemaphoreType.DMA((copies,)),
                 pltpu.SemaphoreType.DMA((copies,)),
             ],
         ),
-        out_shape=[
-            jax.ShapeDtypeStruct((ranks, pieces) + shape, sources[0].dtype)
-            for _ in range(INNER - 1)
-        ],
+        out_shape=[jax.ShapeDtypeStruct((2 * ranks,) + shape, sources[0].dtype)] * 2,
         compiler_params=pltpu.CompilerParams(vmem_limit_bytes=VMEM_LIMIT),
+        cost_estimate=LIGHT,
         name="pick_blocks",
     )(table, *sources)
 
 
-def attend_kernel(part, cap, ranks, pieces, steps, tp_index, table, spans, *refs):
-    count = ranks * pieces + INNER - 1
-    own_refs, got_refs = refs[: ranks * pieces], refs[ranks * pieces : count]
-    q_ref, wk_first, wk_next, wv_first, wv_next = refs[count : count + 5]
+def attend_kernel(part, cap, pieces, steps, tp_index, spans, *refs):
+    x_refs = refs[:pieces]
+    q_ref, wk_first, wk_next, wv_first, wv_next = refs[pieces : pieces + 5]
     out_ref, lse_ref, x_all, scores_ref, weights_ref, k_even, v_even, k_odd, v_odd = refs[-9:]
     nlen = scores_ref.shape[-1]
     pairs = scores_ref.shape[0] // cap
@@ -190,18 +189,14 @@
     @pl.when(step == 0)
     def _():
         lse_ref[...] = jnp.zeros_like(lse_ref)
-        for i in range(cap):
-            for piece in range(pieces):
-                if i < ranks:
-                    block = own_refs[i * pieces + piece][0]
-                else:
-                    block = got_refs[i // ranks - 1][i % ranks, piece]
-                width = block.shape[0]
-                top = 0
-                if pieces == 2:
-                    place = tp_index[0] if piece == 0 else 1 - tp_index[0]
-                    top = pl.multiple_of(place * width, 16)
-                x_all[pl.ds(top, width), i * nlen : (i + 1) * nlen] = block
+        for piece, x_ref in enumerate(x_refs):
+            width = x_ref.shape[1]
+            top = 0
+            if pieces == 2:
+                place = tp_index[0] if piece == 0 else 1 - tp_index[0]
+                top = pl.multiple_of(place * width, 16)
+            for i in range(cap):
+                x_all[pl.ds(top, width), i * nlen : (i + 1) * nlen] = x_ref[i]
         project(wk_first, k_even)
         project(wv_first, v_even)
 
@@ -225,21 +220,15 @@
     pl.when(step == steps - 1)(lambda: finish(*ends))
 
 
-def attend_part(part, cap, scalars, own, got, windows, weights, slots, held):
-    pieces = len(own)
-    ranks = got[0].shape[0]
-    width, nlen = own[0].shape[1:]
+def attend_part(part, cap, scalars, blocks, windows, weights, slots, held):
+    pieces = len(blocks)
+    width, nlen = blocks[0].shape[1:]
     features = width * pieces
     columns = 2 * PAIR
     steps = windows.shape[-1] // columns
 
-    def own_at(r):
-        return lambda t, tp_index, table, spans: (table[part * cap + r], 0, 0)
-
-    in_specs = [pl.BlockSpec((1, width, nlen), own_at(r)) for r in range(ranks) for _ in own]
-    operands = list(own) * ranks
-    in_specs += [pl.BlockSpec(g.shape, lambda t, *_: (0, 0, 0, 0)) for g in got]
-    operands += list(got)
+    in_specs = [pl.BlockSpec(x.shape, lambda t, *_: (0, 0, 0)) for x in blocks]
+    operands = list(blocks)
     in_specs += [pl.BlockSpec((windows.shape[0], SPAN, columns), lambda t, *_: (0, 0, t))]
     operands += [windows]
     for weight in weights:
@@ -251,17 +240,17 @@
     aliases = {}
     if held is not None:
         in_specs += [pl.BlockSpec(memory_space=pl.ANY)] * 2
-        aliases = {3 + len(operands): 0, 4 + len(operands): 1}
+        aliases = {2 + len(operands): 0, 3 + len(operands): 1}
         operands += list(held)
     kv = pltpu.VMEM((columns, cap * nlen), jnp.bfloat16)
 
     def body(*refs):
-        attend_kernel(part, cap, ranks, pieces, steps, *refs)
+        attend_kernel(part, cap, pieces, steps, *refs)
 
     return pl.pallas_call(
         body,
         grid_spec=pltpu.PrefetchScalarGridSpec(
-            num_scalar_prefetch=3,
+            num_scalar_prefetch=2,
             grid=(steps,),
             in_specs=in_specs,
             out_specs=[
@@ -281,6 +270,7 @@
         ],
         input_output_aliases=aliases,
         compiler_params=pltpu.CompilerParams(vmem_limit_bytes=VMEM_LIMIT),
+        cost_estimate=HEAVY,
         name="attend_part",
     )(*scalars, *operands)
 
@@ -362,6 +352,7 @@
             scratch_shapes=[pltpu.VMEM((LANES // 2, columns), jnp.bfloat16)],
         ),
         out_shape=jax.ShapeDtypeStruct((SPAN, columns), jnp.bfloat16),
+        cost_estimate=LIGHT,
         name="mix_last",
     )(places, partials, partials, log_totals, log_totals)
 
@@ -386,6 +377,7 @@
         ),
         out_shape=jax.ShapeDtypeStruct((span_count * SPAN, columns), jnp.bfloat16),
         compiler_params=pltpu.CompilerParams(vmem_limit_bytes=VMEM_LIMIT),
+        cost_estimate=LIGHT,
         name="mix",
     )(places, *([partials, partials, log_totals, log_totals] * per))
 
@@ -406,6 +398,7 @@
         out_specs=spec,
         out_shape=jax.ShapeDtypeStruct(mixed_rows.shape, mixed_rows.dtype),
         input_output_aliases={1: 0},
+        cost_estimate=LIGHT,
         name="with_head",
     )(carried, mixed_rows)
 
@@ -435,23 +428,23 @@
         pairs = [(i, i ^ offset) for i in range(seq_count) if i // INNER in senders]
         return lax.ppermute(x, "seq", pairs)
 
+    own_ids = neighbour_ids.reshape(wants)
+    group_ids = jnp.stack([own_ids, swapped(own_ids, "seq", 2)])
+    mate = swapped(neighbours, "seq", 1)
+    incoming = passed_along(queries[:SPAN], "seq", -1)
     near = swapped(neighbours, "seq", INNER)
     across = along(neighbours, 3 * INNER, (1, 2)) if outer == 4 else near
-    own = all_features(neighbours)
-    own_ids = neighbour_ids.reshape(wants)
-    group_ids = jnp.stack([own_ids] + [swapped(own_ids, "seq", k) for k in range(1, INNER)])
-    incoming = passed_along(queries[:SPAN], "seq", -1)
-    weights = (key_weight.T, value_weight.T)
-    near, across = after((near, across), weights)
 
     group_sources = group_ids // block_count
     group_ranks = slot_ranks(group_sources)
-    part_sources = own_index ^ (INNER * jnp.arange(outer))
-    hit = (group_sources[None, :, None, :] == part_sources[:, None, None, None]) & (
-        group_ranks[None, :, None, :] == jnp.arange(ranks)[None, None, :, None]
+    sources = own_index ^ (INNER * jnp.arange(outer)[:, None] + jnp.arange(2))
+    hit = (group_sources[None, :, None, None, :] == sources[:, None, :, None, None]) & (
+        group_ranks[None, :, None, None, :] == jnp.arange(ranks)[None, None, None, :, None]
     )
-    table = jnp.sum(jnp.where(hit, (group_ids % block_count)[None, :, None, :], 0), axis=-1)
-    table = table.astype(jnp.int32).reshape(outer * cap)
+    table = jnp.sum(
+        jnp.where(hit, (group_ids % block_count)[None, :, None, None, :], 0), axis=-1
+    )
+    table = table.astype(jnp.int32).reshape(-1)
 
     own_sources = own_ids // block_count
     places = ((own_sources ^ own_index) * ranks + slot_ranks(own_sources)).astype(jnp.int32)
@@ -460,48 +453,55 @@
         jnp.where(places[None, :] == jnp.arange(slots)[:, None], order[None, :] // 2, 0), axis=1
     ).astype(jnp.int32)
 
-    def send(j, own, *others):
-        picked = pick_blocks(j, ranks, after(table, *others), own)
-        return picked, [swapped(picked[k - 1], "seq", k) for k in range(1, INNER)]
-
-    def attend(j, own, got, held, *others):
-        scalars = (tp_index, table, after(spans, *others))
-        return attend_part(j, cap, scalars, own, got, windows, weights, slots, held)
-
-    inside = (own_index // INNER == 1) | (own_index // INNER == 2)
+    def pick(j, part, mate, *others):
+        mine, outgoing = pick_blocks(j, ranks, after(table, *others), [part, mate])
+        return mine, swapped(outgoing, "seq", 2)
+
+    def join(picked, *others):
+        return jnp.concatenate([picked[0], after(picked[1], *others)], axis=0)
+
+    def attend(j, blocks, held, *others):
+        scalars = (tp_index, after(spans, *others))
+        return attend_part(j, cap, scalars, blocks, windows, weights, slots, held)
+
+    weights = (key_weight.T, value_weight.T)
+    picked = pick(0, neighbours, mate, weights, incoming)
+    near, across = after((near, across), picked[0])
+    parts = [neighbours, near]
     if outer == 4:
+        inside = (own_index // INNER == 1) | (own_index // INNER == 2)
         second = along(near, 3 * INNER, (1, 2))
         outward = along(across, INNER, (1, 2))
-    owns = [own, all_features(near)]
-    picked, got = send(0, own)
-    gots = [got]
-    windows = span_windows(after(queries, picked), incoming, span_count)
+
+    def part_of(j, *others):
+        if outer != 4:
+            low = j & -j
+            return swapped(after(parts[j ^ low], *others), "seq", INNER * low)
+        if j == 2:
+            return jnp.where(inside, *after((second, outward), *others))
+        return jnp.where(inside, *after((across, third), *others))
+
+    wanted = join(picked)
+    blocks = [all_features(wanted)]
+    picked = pick(1, near, swapped(near, "seq", 1), wanted)
+    windows = span_windows(after(queries, picked[0]), incoming, span_count)
+    wanted = join(picked, windows)
+    blocks.append(all_features(wanted))
+    parts.append(part_of(2, wanted, blocks[0]))
     if outer == 4:
-        second, outward = after((second, outward), windows)
-        far = jnp.where(inside, second, outward)
         third = along(second, INNER, (1, 2))
-    else:
-        far = swapped(near, "seq", 3 * INNER)
-    owns.append(all_features(far))
-    picked, got = send(1, owns[1], far)
-    gots.append(got)
-    held = attend(0, owns[0], gots[0], None, picked)
-    parts = [neighbours, near, far]
+    picked = pick(2, parts[2], swapped(parts[2], "seq", 1))
+    held = attend(0, blocks[0], None, picked[0])
     for j in range(3, outer):
-        if outer == 4:
-            part = jnp.where(inside, *after((across, third), held))
-        else:
-            low = j & -j
-            part = swapped(after(parts[j ^ low], held), "seq", INNER * low)
-        parts.append(part)
-        owns.append(all_features(part))
-        picked, got = send(j - 1, owns[j - 1], part)
-        gots.append(got)
-        held = attend(j - 2, owns[j - 2], gots[j - 2], held, picked)
-    picked, got = send(outer - 1, owns[outer - 1], held)
-    gots.append(got)
-    held = attend(outer - 2, owns[outer - 2], gots[outer - 2], held, picked)
-    held = attend(outer - 1, owns[outer - 1], gots[outer - 1], held)
+        wanted = join(picked, held)
+        blocks.append(all_features(wanted))
+        parts.append(part_of(j, wanted, blocks[j - 2]))
+        picked = pick(j, parts[j], swapped(parts[j], "seq", 1))
+        held = attend(j - 2, blocks[j - 2], held, picked[0])
+    wanted = join(picked, held)
+    blocks.append(all_features(wanted))
+    held = attend(outer - 2, blocks[outer - 2], held, wanted)
+    held = attend(outer - 1, blocks[outer - 1], held)
 
     partials, log_totals = held
     last = mix_last(places, partials, log_totals, span_count)

time: 211 us -> 178 us (0.84)
  waiting for transfers between devices: 36.6 us -> 17.9 us
  starting transfers between devices: 44.3 us -> 33.6 us
    ppermute x20 -> x14, waiting for transfers between devices: 29.8 us -> 15.6 us  [swapped(): return lax.ppermute(x, axis, [(i, i ^ offset) for i in range(peers)])]
    ppermute x20 -> x14, starting transfers between devices: 33.6 us -> 22.3 us  [swapped(): return lax.ppermute(x, axis, [(i, i ^ offset) for i in range(peers)])]
    ppermute x4, waiting for transfers between devices: 6.75 us -> 2.26 us  [along(): return lax.ppermute(x, 'seq', pairs)]
    unnamed x49 -> x44, local copies, waits for them, and re-layouts: 20.3 us -> 18.4 us
  transfers between devices with their start and end apart: 26 -> 20, of which waited for: 7 -> 6; matrix products, arithmetic and copies ran while one was open for 9% -> 10% of each run, Pallas kernels for 38% -> 44%
where the time goes in v6:
time: 178 us; the launch traced here: 176 us
  Pallas kernels  100 us (56%)
  starting transfers between devices  33.6 us (19%)
  local copies, waits for them, and re-layouts  20.4 us (11%)
  waiting for transfers between devices  17.9 us (10%)
  other arithmetic  3.91 us (2%)
    pallas_call x4, Pallas kernels, attend_part(): pl.pallas_call(body, grid_spec=pltpu.PrefetchScalarGridSpec(num_scalar_pr...  71.5 us
    ppermute x14, starting transfers between devices, swapped(): return lax.ppermute(x, axis, [(i, i ^ offset) for i in range(peers)])  22.3 us
    unnamed x44, local copies, waits for them, and re-layouts  18.4 us
    ppermute x14, waiting for transfers between devices, swapped(): return lax.ppermute(x, axis, [(i, i ^ offset) for i in range(peers)])  15.6 us
    pallas_call x4, Pallas kernels, pick_blocks(): pl.pallas_call(body, grid_spec=pltpu.PrefetchScalarGridSpec(num_scalar_pr...  10.9 us
    pallas_call x1, Pallas kernels, mix(): pl.pallas_call(mix_kernel, grid_spec=pltpu.PrefetchScalarGridSpec(num_sca...  8.22 us
    ppermute x2, starting transfers between devices, passed_along(): return lax.ppermute(x, axis, pairs)  6.46 us
    pallas_call x1, Pallas kernels, span_windows(): pl.pallas_call(windows_kernel, grid=(steps,), in_specs=[pl.BlockSpec((per...  5.01 us
  transfers between devices with their start and end apart: 20, of which 6 were waited for; matrix products, arithmetic and copies ran while one was open for 10% of the time, Pallas kernels for 44%

profile of v6, /device:TPU:1, one launch (start us, length us, event | category | flops | bytes accessed | tf_op | source)
XLA Modules:
  0.0 176.4 jit_solution(4991051813879439190)
XLA Ops:
  0.7 4.7 %collective-permute-start.1 = (bf16[8,448,128]{2,1,0:T(8,128)(2,1)}, bf16[8,448,128]{2,1,0:T(8,128)(2,1)S(1)}, u32[]{:S(2)}, u32[]{:S(2)}) collective-permute-start(bf16[8,448,128]{2,1,0:T(8,128)(2,1)} %refs_1_.1), channel_id=1, source_target_pairs={{0,8},{2,10},{4,12},{6,14},{8,0},{10,2},{12,4},{14,6},{16,24},{18,... | collective-permute-start | bytes 2752520 | tf_op jit(solution)/shard_map/ppermute | solution.py:28
  9.7 2.2 %collective-permute-start.3 = (bf16[64,2048]{1,0:T(8,128)(2,1)S(1)}, bf16[64,2048]{1,0:T(8,128)(2,1)S(1)}, u32[]{:S(2)}, u32[]{:S(2)}) collective-permute-start(bf16[64,2048]{1,0:T(8,128)(2,1)S(1)} %slice.3), channel_id=1, source_target_pairs={{2,0},{4,2},{6,4},{8,6},{10,8},{12,10},{14,12},{16,14},{18,16},{20... | collective-permute-start | bytes 786440 | tf_op jit(solution)/shard_map/ppermute | solution.py:23
  12.1 6.1 %copy.24 = bf16[896,2048]{0,1:T(8,128)(2,1)} copy(bf16[896,2048]{1,0:T(8,128)(2,1)} %param.7) | data formatting | bytes 7340032 | tf_op args[2]
  18.2 6.0 %copy.25 = bf16[896,2048]{0,1:T(8,128)(2,1)} copy(bf16[896,2048]{1,0:T(8,128)(2,1)} %param.8) | data formatting | bytes 7340032 | tf_op args[3]
  26.4 2.7 %pick_blocks.4 = (bf16[4,448,128]{2,1,0:T(8,128)(2,1)}, bf16[4,448,128]{2,1,0:T(8,128)(2,1)}) custom-call(s32[32]{0:T(128)} %reshape.422.refs_0_, bf16[8,448,128]{2,1,0:T(8,128)(2,1)} %refs_1_.1, bf16[8,448,128]{2,1,0:T(8,128)(2,1)} %copy-done.4), custom_call_target="tpu_custom_call" | custom-call | flops 1000 | bytes 1000 | tf_op jit(solution)/shard_map/pick_blocks/pallas_call | solution.py:109
  29.2 4.8 %collective-permute-start.8 = (bf16[4,448,128]{2,1,0:T(8,128)(2,1)}, bf16[4,448,128]{2,1,0:T(8,128)(2,1)S(1)}, u32[]{:S(2)}, u32[]{:S(2)}) collective-permute-start(bf16[4,448,128]{2,1,0:T(8,128)(2,1)} %get-tuple-element.40), channel_id=1, source_target_pairs={{0,4},{2,6},{4,0},{6,2},{8,12},{10,14},{12,8},{14,10},{16,20},{18,... | collective-permute-start | bytes 1376264 | tf_op jit(solution)/shard_map/ppermute | solution.py:28
  37.0 5.4 %collective-permute-done.8 = bf16[4,448,128]{2,1,0:T(8,128)(2,1)S(1)} collective-permute-done((bf16[4,448,128]{2,1,0:T(8,128)(2,1)}, bf16[4,448,128]{2,1,0:T(8,128)(2,1)S(1)}, u32[]{:S(2)}, u32[]{:S(2)}) %collective-permute-start.8) | collective-permute-done | bytes 458784 | tf_op jit(solution)/shard_map/ppermute | solution.py:28
  45.7 2.7 %pick_blocks.5 = (bf16[4,448,128]{2,1,0:T(8,128)(2,1)}, bf16[4,448,128]{2,1,0:T(8,128)(2,1)}) custom-call(s32[32]{0:T(128)} %reshape.422.refs_0_, bf16[8,448,128]{2,1,0:T(8,128)(2,1)} %copy-done.3, bf16[8,448,128]{2,1,0:T(8,128)(2,1)} %copy-done.5), custom_call_target="tpu_custom_call" | custom-call | flops 1000 | bytes 1000 | tf_op jit(solution)/shard_map/pick_blocks/pallas_call | solution.py:109
  48.5 1.8 %collective-permute-start.10 = (bf16[4,448,128]{2,1,0:T(8,128)(2,1)}, bf16[4,448,128]{2,1,0:T(8,128)(2,1)S(1)}, u32[]{:S(2)}, u32[]{:S(2)}) collective-permute-start(bf16[4,448,128]{2,1,0:T(8,128)(2,1)} %get-tuple-element.43), channel_id=1, source_target_pairs={{0,4},{2,6},{4,0},{6,2},{8,12},{10,14},{12,8},{14,10},{16,20},{18,... | collective-permute-start | bytes 1376264 | tf_op jit(solution)/shard_map/ppermute | solution.py:28
  50.3 5.0 %windows.1.refs_4_ = bf16[16,64,2048]{2,1,0:T(8,128)(2,1)} custom-call(bf16[1024,2048]{1,0:T(8,128)(2,1)} %next_ref, bf16[1024,2048]{1,0:T(8,128)(2,1)} %next_ref, bf16[64,2048]{1,0:T(8,128)(2,1)} %copy-done.10), custom_call_target="tpu_custom_call" | custom-call | flops 1000 | bytes 1000 | tf_op jit(solution)/shard_map/windows/pallas_call | solution.py:60
  55.4 4.4 %collective-permute-done.10 = bf16[4,448,128]{2,1,0:T(8,128)(2,1)S(1)} collective-permute-done((bf16[4,448,128]{2,1,0:T(8,128)(2,1)}, bf16[4,448,128]{2,1,0:T(8,128)(2,1)S(1)}, u32[]{:S(2)}, u32[]{:S(2)}) %collective-permute-start.10) | collective-permute-done | bytes 458784 | tf_op jit(solution)/shard_map/ppermute | solution.py:28
  59.9 3.6 %collective-permute-done.11.refs_3_ = bf16[8,448,128]{2,1,0:T(8,128)(2,1)} collective-permute-done((bf16[8,448,128]{2,1,0:T(8,128)(2,1)S(1)}, bf16[8,448,128]{2,1,0:T(8,128)(2,1)}, u32[]{:S(2)}, u32[]{:S(2)}) %collective-permute-start.11) | collective-permute-done | bytes 917536 | tf_op jit(solution)/shard_map/ppermute | solution.py:28
  68.4 2.7 %pick_blocks.6 = (bf16[4,448,128]{2,1,0:T(8,128)(2,1)}, bf16[4,448,128]{2,1,0:T(8,128)(2,1)}) custom-call(s32[32]{0:T(128)} %reshape.422.refs_0_, bf16[8,448,128]{2,1,0:T(8,128)(2,1)} %copy-done, bf16[8,448,128]{2,1,0:T(8,128)(2,1)} %collective-permute-done.12.refs_2_), custom_call_target="tpu_custom_call" | custom-call | flops 1000 | bytes 1000 | tf_op jit(solution)/shard_map/pick_blocks/pallas_call | solution.py:109
  71.1 2.1 %collective-permute-start.13 = (bf16[4,448,128]{2,1,0:T(8,128)(2,1)}, bf16[4,448,128]{2,1,0:T(8,128)(2,1)S(1)}, u32[]{:S(2)}, u32[]{:S(2)}) collective-permute-start(bf16[4,448,128]{2,1,0:T(8,128)(2,1)} %get-tuple-element.49), channel_id=1, source_target_pairs={{0,4},{2,6},{4,0},{6,2},{8,12},{10,14},{12,8},{14,10},{16,20},{18,... | collective-permute-start | bytes 1376264 | tf_op jit(solution)/shard_map/ppermute | solution.py:28
  73.2 17.8 %attend_part.4 = (bf16[32,64,2048]{2,1,0:T(8,128)(2,1)}, f32[32,64,128]{2,1,0:T(8,128)}) custom-call(s32[1]{0:T(128)} %bitcast.refs_0_, s32[32]{0:T(128)} %select_reduce_fusion.2.refs_1_, bf16[8,448,128]{2,1,0:T(8,128)(2,1)} %copy-done.2, bf16[8,448,128]{2,1,0:T(8,128)(2,1)} %collective-permute-done.11.refs_3_, bf16[16,64,2048]{2,1,0:T(8,128)(2,1)} %windows.1.refs_4_, ...), custom_call_target="tpu_custom_call" | custom-call | flops 20000000000 | bytes 10000000 | tf_op jit(solution)/shard_map/attend_part/pallas_call | solution.py:250
  91.1 2.3 %collective-permute-done.6 = bf16[8,448,128]{2,1,0:T(8,128)(2,1)S(1)} collective-permute-done((bf16[8,448,128]{2,1,0:T(8,128)(2,1)}, bf16[8,448,128]{2,1,0:T(8,128)(2,1)S(1)}, u32[]{:S(2)}, u32[]{:S(2)}) %collective-permute-start.6) | collective-permute-done | bytes 917536 | tf_op jit(solution)/shard_map/ppermute | solution.py:429
  97.2 2.7 %pick_blocks.7 = (bf16[4,448,128]{2,1,0:T(8,128)(2,1)}, bf16[4,448,128]{2,1,0:T(8,128)(2,1)}) custom-call(s32[32]{0:T(128)} %reshape.422.refs_0_, bf16[8,448,128]{2,1,0:T(8,128)(2,1)} %copy-done.1, bf16[8,448,128]{2,1,0:T(8,128)(2,1)} %copy-done.6), custom_call_target="tpu_custom_call" | custom-call | flops 1000 | bytes 1000 | tf_op jit(solution)/shard_map/pick_blocks/pallas_call | solution.py:109
  100.5 17.8 %attend_part.5 = (bf16[32,64,2048]{2,1,0:T(8,128)(2,1)}, f32[32,64,128]{2,1,0:T(8,128)}) custom-call(s32[1]{0:T(128)} %bitcast.refs_0_, s32[32]{0:T(128)} %select_reduce_fusion.2.refs_1_, bf16[8,448,128]{2,1,0:T(8,128)(2,1)} %copy-done.14, bf16[8,448,128]{2,1,0:T(8,128)(2,1)} %copy-done.16, ...), custom_call_target="tpu_custom_call", output_to_operand_aliasing={{0}: (9, {}), {1}: (10, {})} | custom-call | flops 20000000000 | bytes 10000000 | tf_op jit(solution)/shard_map/attend_part/pallas_call | solution.py:250
  120.7 17.9 %attend_part.6 = (bf16[32,64,2048]{2,1,0:T(8,128)(2,1)}, f32[32,64,128]{2,1,0:T(8,128)}) custom-call(s32[1]{0:T(128)} %bitcast.refs_0_, s32[32]{0:T(128)} %select_reduce_fusion.2.refs_1_, bf16[8,448,128]{2,1,0:T(8,128)(2,1)} %copy-done.12, bf16[8,448,128]{2,1,0:T(8,128)(2,1)} %copy-done.17, ...), custom_call_target="tpu_custom_call", output_to_operand_aliasing={{0}: (9, {}), {1}: (10, {})} | custom-call | flops 20000000000 | bytes 10000000 | tf_op jit(solution)/shard_map/attend_part/pallas_call | solution.py:250
  140.7 18.0 %attend_part.7 = (bf16[32,64,2048]{2,1,0:T(8,128)(2,1)}, f32[32,64,128]{2,1,0:T(8,128)}) custom-call(s32[1]{0:T(128)} %bitcast.refs_0_, s32[32]{0:T(128)} %select_reduce_fusion.2.refs_1_, bf16[8,448,128]{2,1,0:T(8,128)(2,1)} %copy-done.13, bf16[8,448,128]{2,1,0:T(8,128)(2,1)} %copy-done.18, ...), custom_call_target="tpu_custom_call", output_to_operand_aliasing={{0}: (9, {}), {1}: (10, {})} | custom-call | flops 20000000000 | bytes 10000000 | tf_op jit(solution)/shard_map/attend_part/pallas_call | solution.py:250
  158.7 2.8 %mix_last.1 = bf16[64,2048]{1,0:T(8,128)(2,1)} custom-call(s32[32]{0:T(128)} %copy-done.15, bf16[32,64,2048]{2,1,0:T(8,128)(2,1)} %get-tuple-element.65.p0.p1.refs_0_.refs_1_.refs_4_.refs_5_.refs_8_.refs_9_.refs_12_.refs_13_, bf16[32,64,2048]{2,1,0:T(8,128)(2,1)} %get-tuple-element.65.p0.p1.refs_0_.refs_1_.refs_4_.refs_5_.refs_8_.refs_9_.refs_12_.refs_13_, ...), custom_call_target="tpu_custom_call" | custom-call | flops 1000 | bytes 1000 | tf_op jit(solution)/shard_map/mix_last/pallas_call | solution.py:345
  161.4 4.3 %collective-permute-start.19 = (bf16[64,2048]{1,0:T(8,128)(2,1)}, bf16[64,2048]{1,0:T(8,128)(2,1)S(1)}, u32[]{:S(2)}, u32[]{:S(2)}) collective-permute-start(bf16[64,2048]{1,0:T(8,128)(2,1)} %mix_last.1), channel_id=1, source_target_pairs={{0,2},{2,4},{4,6},{6,8},{8,10},{10,12},{12,14},{14,16},{16,18},{18... | collective-permute-start | bytes 786440 | tf_op jit(solution)/shard_map/ppermute | solution.py:23
  165.7 8.2 %mix.1.rows = bf16[1024,2048]{1,0:T(8,128)(2,1)} custom-call(s32[32]{0:T(128)} %copy-done.15, bf16[32,64,2048]{2,1,0:T(8,128)(2,1)} %get-tuple-element.65.p0.p1.refs_0_.refs_1_.refs_4_.refs_5_.refs_8_.refs_9_.refs_12_.refs_13_, bf16[32,64,2048]{2,1,0:T(8,128)(2,1)} %get-tuple-element.65.p0.p1.refs_0_.refs_1_.refs_4_.refs_5_.refs_8_.refs_9_.refs_12_.refs_13_, ...), custom_call_target="tpu_custom_call" | custom-call | flops 1000 | bytes 1000 | tf_op jit(solution)/shard_map/mix/pallas_call | solution.py:366
  174.6 1.8 with_head.1
  (96 shorter events, 28.2 us)
Async XLA Ops:
  0.0 34.0 %collective-permute-start.2 = (bf16[8,448,128]{2,1,0:T(8,128)(2,1)}, bf16[8,448,128]{2,1,0:T(8,128)(2,1)S(1)}, u32[]{:S(2)}, u32[]{:S(2)}) collective-permute-start(bf16[8,448,128]{2,1,0:T(8,128)(2,1)} %refs_1_.1), channel_id=1, source_target_pairs={{8,16},{10,18},{12,20},{14,22},{16,8},{18,10},{20,12},{22,14},{9,1... | collective-permute-start | bytes 2752520 | tf_op jit(solution)/shard_map/ppermute | solution.py:429
  0.7 33.3 %collective-permute-start.1 = (bf16[8,448,128]{2,1,0:T(8,128)(2,1)}, bf16[8,448,128]{2,1,0:T(8,128)(2,1)S(1)}, u32[]{:S(2)}, u32[]{:S(2)}) collective-permute-start(bf16[8,448,128]{2,1,0:T(8,128)(2,1)} %refs_1_.1), channel_id=1, source_target_pairs={{0,8},{2,10},{4,12},{6,14},{8,0},{10,2},{12,4},{14,6},{16,24},{18,... | collective-permute-start | bytes 2752520 | tf_op jit(solution)/shard_map/ppermute | solution.py:28
  5.4 20.1 %collective-permute-start.4 = (bf16[8,448,128]{2,1,0:T(8,128)(2,1)}, bf16[8,448,128]{2,1,0:T(8,128)(2,1)S(1)}, u32[]{:S(2)}, u32[]{:S(2)}) collective-permute-start(bf16[8,448,128]{2,1,0:T(8,128)(2,1)} %refs_1_.1), channel_id=1, source_target_pairs={{0,2},{2,0},{4,6},{6,4},{8,10},{10,8},{12,14},{14,12},{16,18},{18,... | collective-permute-start | bytes 2752520 | tf_op jit(solution)/shard_map/ppermute | solution.py:28
  7.5 16.7 %collective-permute-start = (s32[32]{0:T(128)S(1)}, s32[32]{0:T(128)S(1)}, u32[]{:S(2)}, u32[]{:S(2)}) collective-permute-start(s32[32]{0:T(128)S(1)} %reshape.420), channel_id=1, source_target_pairs={{0,4},{2,6},{4,0},{6,2},{8,12},{10,14},{12,8},{14,10},{16,20},{18,... | collective-permute-start | bytes 392 | tf_op jit(solution)/shard_map/ppermute | solution.py:28
  9.7 15.7 %collective-permute-start.3 = (bf16[64,2048]{1,0:T(8,128)(2,1)S(1)}, bf16[64,2048]{1,0:T(8,128)(2,1)S(1)}, u32[]{:S(2)}, u32[]{:S(2)}) collective-permute-start(bf16[64,2048]{1,0:T(8,128)(2,1)S(1)} %slice.3), channel_id=1, source_target_pairs={{2,0},{4,2},{6,4},{8,6},{10,8},{12,10},{14,12},{16,14},{18,16},{20... | collective-permute-start | bytes 786440 | tf_op jit(solution)/shard_map/ppermute | solution.py:23
  25.5 24.8 %copy-start.10 = (bf16[64,2048]{1,0:T(8,128)(2,1)}, bf16[64,2048]{1,0:T(8,128)(2,1)S(1)}, u32[]{:S(2)}) copy-start(bf16[64,2048]{1,0:T(8,128)(2,1)S(1)} %collective-permute-done.3.incoming_ref) | copy-start | bytes 786436
  29.2 13.2 %collective-permute-start.8 = (bf16[4,448,128]{2,1,0:T(8,128)(2,1)}, bf16[4,448,128]{2,1,0:T(8,128)(2,1)S(1)}, u32[]{:S(2)}, u32[]{:S(2)}) collective-permute-start(bf16[4,448,128]{2,1,0:T(8,128)(2,1)} %get-tuple-element.40), channel_id=1, source_target_pairs={{0,4},{2,6},{4,0},{6,2},{8,12},{10,14},{12,8},{14,10},{16,20},{18,... | collective-permute-start | bytes 1376264 | tf_op jit(solution)/shard_map/ppermute | solution.py:28
  34.0 10.8 %collective-permute-start.9 = (bf16[8,448,128]{2,1,0:T(8,128)(2,1)S(1)}, bf16[8,448,128]{2,1,0:T(8,128)(2,1)S(1)}, u32[]{:S(2)}, u32[]{:S(2)}) collective-permute-start(bf16[8,448,128]{2,1,0:T(8,128)(2,1)S(1)} %collective-permute-done.1.refs_1_), channel_id=1, source_target_pairs={{0,2},{2,0},{4,6},{6,4},{8,10},{10,8},{12,14},{14,12},{16,18},{18,... | collective-permute-start | bytes 2752520 | tf_op jit(solution)/shard_map/ppermute | solution.py:28
  34.1 25.8 %collective-permute-start.5 = (bf16[8,448,128]{2,1,0:T(8,128)(2,1)S(1)}, bf16[8,448,128]{2,1,0:T(8,128)(2,1)}, u32[]{:S(2)}, u32[]{:S(2)}) collective-permute-start(bf16[8,448,128]{2,1,0:T(8,128)(2,1)S(1)} %collective-permute-done.1.refs_1_), channel_id=1, source_target_pairs={{8,16},{10,18},{12,20},{14,22},{16,8},{18,10},{20,12},{22,14},{9,1... | collective-permute-start | bytes 2752520 | tf_op jit(solution)/shard_map/ppermute | solution.py:429
  35.7 24.2 %collective-permute-start.7 = (bf16[8,448,128]{2,1,0:T(8,128)(2,1)S(1)}, bf16[8,448,128]{2,1,0:T(8,128)(2,1)}, u32[]{:S(2)}, u32[]{:S(2)}) collective-permute-start(bf16[8,448,128]{2,1,0:T(8,128)(2,1)S(1)} %collective-permute-done.2), channel_id=1, source_target_pairs={{8,0},{10,2},{12,4},{14,6},{16,24},{18,26},{20,28},{22,30},{9,1},{... | collective-permute-start | bytes 2752520 | tf_op jit(solution)/shard_map/ppermute | solution.py:429
  43.5 20.0 %collective-permute-start.11 = (bf16[8,448,128]{2,1,0:T(8,128)(2,1)S(1)}, bf16[8,448,128]{2,1,0:T(8,128)(2,1)}, u32[]{:S(2)}, u32[]{:S(2)}) collective-permute-start(bf16[8,448,128]{2,1,0:T(8,128)(2,1)S(1)} %pad_maximum_fusion.refs_2_), channel_id=1, source_target_pairs={{0,1},{1,0},{2,3},{3,2},{4,5},{5,4},{6,7},{7,6},{8,9},{9,8},{10,11... | collective-permute-start | bytes 2752520 | tf_op jit(solution)/shard_map/ppermute | solution.py:28
  48.5 11.3 %collective-permute-start.10 = (bf16[4,448,128]{2,1,0:T(8,128)(2,1)}, bf16[4,448,128]{2,1,0:T(8,128)(2,1)S(1)}, u32[]{:S(2)}, u32[]{:S(2)}) collective-permute-start(bf16[4,448,128]{2,1,0:T(8,128)(2,1)} %get-tuple-element.43), channel_id=1, source_target_pairs={{0,4},{2,6},{4,0},{6,2},{8,12},{10,14},{12,8},{14,10},{16,20},{18,... | collective-permute-start | bytes 1376264 | tf_op jit(solution)/shard_map/ppermute | solution.py:28
  64.8 3.6 %collective-permute-start.12 = (bf16[8,448,128]{2,1,0:T(8,128)(2,1)S(1)}, bf16[8,448,128]{2,1,0:T(8,128)(2,1)}, u32[]{:S(2)}, u32[]{:S(2)}) collective-permute-start(bf16[8,448,128]{2,1,0:T(8,128)(2,1)S(1)} %broadcast_select_fusion.1.refs_1_), channel_id=1, source_target_pairs={{0,2},{2,0},{4,6},{6,4},{8,10},{10,8},{12,14},{14,12},{16,18},{18,... | collective-permute-start | bytes 2752520 | tf_op jit(solution)/shard_map/ppermute | solution.py:28
  65.1 25.9 %copy-start.15 = (s32[32]{0:T(128)}, s32[32]{0:T(128)S(1)}, u32[]{:S(2)}) copy-start(s32[32]{0:T(128)S(1)} %multiply_add_fusion.places) | copy-start | bytes 388
  65.8 27.6 %collective-permute-start.6 = (bf16[8,448,128]{2,1,0:T(8,128)(2,1)}, bf16[8,448,128]{2,1,0:T(8,128)(2,1)S(1)}, u32[]{:S(2)}, u32[]{:S(2)}) collective-permute-start(bf16[8,448,128]{2,1,0:T(8,128)(2,1)} %collective-permute-done.5), channel_id=1, source_target_pairs={{8,0},{10,2},{12,4},{14,6},{16,24},{18,26},{20,28},{22,30},{9,1},{... | collective-permute-start | bytes 2752520 | tf_op jit(solution)/shard_map/ppermute | solution.py:429
  67.1 26.3 %collective-permute-start.14 = (bf16[8,448,128]{2,1,0:T(8,128)(2,1)}, bf16[8,448,128]{2,1,0:T(8,128)(2,1)S(1)}, u32[]{:S(2)}, u32[]{:S(2)}) collective-permute-start(bf16[8,448,128]{2,1,0:T(8,128)(2,1)} %copy-done.14), channel_id=1, source_target_pairs={{0,1},{1,0},{2,3},{3,2},{4,5},{5,4},{6,7},{7,6},{8,9},{9,8},{10,11... | collective-permute-start | bytes 2752520 | tf_op jit(solution)/shard_map/ppermute | solution.py:28
  71.1 19.9 %collective-permute-start.13 = (bf16[4,448,128]{2,1,0:T(8,128)(2,1)}, bf16[4,448,128]{2,1,0:T(8,128)(2,1)S(1)}, u32[]{:S(2)}, u32[]{:S(2)}) collective-permute-start(bf16[4,448,128]{2,1,0:T(8,128)(2,1)} %get-tuple-element.49), channel_id=1, source_target_pairs={{0,4},{2,6},{4,0},{6,2},{8,12},{10,14},{12,8},{14,10},{16,20},{18,... | collective-permute-start | bytes 1376264 | tf_op jit(solution)/shard_map/ppermute | solution.py:28
  91.1 27.2 %copy-start.12 = (bf16[8,448,128]{2,1,0:T(8,128)(2,1)}, bf16[8,448,128]{2,1,0:T(8,128)(2,1)S(1)}, u32[]{:S(2)}) copy-start(bf16[8,448,128]{2,1,0:T(8,128)(2,1)S(1)} %constant_dynamic-update-slice_fusion.2.refs_2_) | copy-start | bytes 2752516
  93.5 2.8 %collective-permute-start.15 = (bf16[8,448,128]{2,1,0:T(8,128)(2,1)S(1)}, bf16[8,448,128]{2,1,0:T(8,128)(2,1)S(1)}, u32[]{:S(2)}, u32[]{:S(2)}) collective-permute-start(bf16[8,448,128]{2,1,0:T(8,128)(2,1)S(1)} %broadcast_select_fusion.refs_1_), channel_id=1, source_target_pairs={{0,2},{2,0},{4,6},{6,4},{8,10},{10,8},{12,14},{14,12},{16,18},{18,... | collective-permute-start | bytes 2752520 | tf_op jit(solution)/shard_map/ppermute | solution.py:28
  94.2 25.6 %collective-permute-start.18 = (bf16[8,448,128]{2,1,0:T(8,128)(2,1)S(1)}, bf16[8,448,128]{2,1,0:T(8,128)(2,1)S(1)}, u32[]{:S(2)}, u32[]{:S(2)}) collective-permute-start(bf16[8,448,128]{2,1,0:T(8,128)(2,1)S(1)} %constant_dynamic-update-slice_fusion.2.refs_2_), channel_id=1, source_target_pairs={{0,1},{1,0},{2,3},{3,2},{4,5},{5,4},{6,7},{7,6},{8,9},{9,8},{10,11... | collective-permute-start | bytes 2752520 | tf_op jit(solution)/shard_map/ppermute | solution.py:28
  100.0 18.4 %collective-permute-start.16 = (bf16[4,448,128]{2,1,0:T(8,128)(2,1)}, bf16[4,448,128]{2,1,0:T(8,128)(2,1)S(1)}, u32[]{:S(2)}, u32[]{:S(2)}) collective-permute-start(bf16[4,448,128]{2,1,0:T(8,128)(2,1)} %get-tuple-element.57), channel_id=1, source_target_pairs={{0,4},{2,6},{4,0},{6,2},{8,12},{10,14},{12,8},{14,10},{16,20},{18,... | collective-permute-start | bytes 1376264 | tf_op jit(solution)/shard_map/ppermute | solution.py:28
  118.5 20.1 %copy-start.13 = (bf16[8,448,128]{2,1,0:T(8,128)(2,1)}, bf16[8,448,128]{2,1,0:T(8,128)(2,1)S(1)}, u32[]{:S(2)}) copy-start(bf16[8,448,128]{2,1,0:T(8,128)(2,1)S(1)} %constant_dynamic-update-slice_fusion.4.refs_2_) | copy-start | bytes 2752516
  118.5 21.3 %collective-permute-start.17 = (bf16[8,448,128]{2,1,0:T(8,128)(2,1)S(1)}, bf16[8,448,128]{2,1,0:T(8,128)(2,1)S(1)}, u32[]{:S(2)}, u32[]{:S(2)}) collective-permute-start(bf16[8,448,128]{2,1,0:T(8,128)(2,1)S(1)} %constant_dynamic-update-slice_fusion.4.refs_2_), channel_id=1, source_target_pairs={{0,1},{1,0},{2,3},{3,2},{4,5},{5,4},{6,7},{7,6},{8,9},{9,8},{10,11... | collective-permute-start | bytes 2752520 | tf_op jit(solution)/shard_map/ppermute | solution.py:28
  161.4 12.5 %collective-permute-start.19 = (bf16[64,2048]{1,0:T(8,128)(2,1)}, bf16[64,2048]{1,0:T(8,128)(2,1)S(1)}, u32[]{:S(2)}, u32[]{:S(2)}) collective-permute-start(bf16[64,2048]{1,0:T(8,128)(2,1)} %mix_last.1), channel_id=1, source_target_pairs={{0,2},{2,4},{4,6},{6,8},{8,10},{10,12},{12,14},{14,16},{16,18},{18... | collective-permute-start | bytes 786440 | tf_op jit(solution)/shard_map/ppermute | solution.py:23
  (15 other events, 86.3 us)
